TPU v7x, 32 devices: a whole 2x2x4 slice. The times are simulated.
32 devices in a mesh: rep: 2 (over y), ctx: 4 (over z), ep: 4 (over x, core), tp: 1.
Axes of the slice: x: 2, y: 2, z: 4, core: 2. Of those that a mesh axis runs over, the one named last changes fastest.
Arguments:
- queries: bfloat16 [512, 2, 16, 128], P(('rep', 'ctx'), 'tp', 'ep'), parts along dimension 0, may hold values from -120 to 120
- key_rows: bfloat16 [1024, 2, 128], P(('rep', 'ctx'), 'tp'), parts along dimension 0, may hold values from -6.5 to 6.5
- values: bfloat16 [1024, 2, 128], P(('rep', 'ctx'), 'tp'), parts along dimension 0, may hold values from -48 to 48
- offset: int32 [2], P('rep'), parts along dimension 0, may hold values from 0 to 256
- tokens: bfloat16 [4096, 2048], P(('rep', 'ctx', 'ep')), parts along dimension 0, may hold values from -6 to 6
- routes: int32 [4096, 8], P(('rep', 'ctx', 'ep')), parts along dimension 0, may hold values from 0 to 15, all different within a row; in each aligned block of 128 rows (0 to 127, 128 to 255, ...) at most 80 rows name the same one
- gate_share: float32 [4096, 8], P(('rep', 'ctx', 'ep')), parts along dimension 0, may hold values from 0.1 to 1
- expert_gate: bfloat16 [16, 2048, 768], P(('ctx', 'ep'), None, 'tp'), may hold values from -0.125 to 0.125
- expert_down: bfloat16 [16, 768, 2048], P(('ctx', 'ep'), 'tp'), may hold values from -0.21875 to 0.21875
Outputs:
- attended: bfloat16 [512, 2, 16, 128], P(('rep', 'ctx'), 'tp', 'ep'), parts along dimension 0
- mixture: bfloat16 [4096, 2048], P(('rep', 'ctx', 'ep'), 'tp'), parts along dimension 0
There are 2 independent parts, one for each index of `rep`. A program takes and returns all parts, laid end to end along the dimension named above; an argument that names none is the same for every part. Nothing has to cross between parts.
Inputs may be any that keep to these rules, and one draw needn't show every extreme that they name: `routes`: within each aligned block of 128 rows (the rows of one device) no expert is named by more than 80 of them, a bound that some block reaches.
All inputs are finite; a program needn't handle non-finite values. Where the computation divides by a largest or mean magnitude, that divisor is 1e-20 or more.
Results may differ from a plain program's by a relative error of at most 0.008.
Values may be sent and summed in bfloat16 or wider, within the bound.
No kernel may reach another device: no remote copies, remote signals or barrier semaphores. Data moves between devices by JAX's collectives and lax.ppermute only.
A program may use at most 128 MiB of HBM per device.

v0:
```python
import math

import jax
import jax.numpy as jnp
from jax import lax
from jax.sharding import PartitionSpec as P


def attention_shard(queries, key_rows, values, offset):
    query_rows, head_count, group_count, head_size = queries.shape
    inv_root = 1.0 / math.sqrt(head_size)
    query_pos = (
        offset[0] + lax.axis_index("ctx") * query_rows + jnp.arange(query_rows, dtype=jnp.int32)
    )
    row_pos = jnp.tile(query_pos, group_count)
    head_rows = jnp.transpose(queries, (1, 2, 0, 3)).reshape(
        head_count, group_count * query_rows, head_size
    )
    state_shape = (head_count, group_count * query_rows)
    highest = jnp.full(state_shape, -1e30, jnp.float32)
    key_piece = lax.all_gather(key_rows, "ctx", axis=0, tiled=True)
    value_piece = lax.all_gather(values, "ctx", axis=0, tiled=True)
    scores = (
        jnp.einsum("hrd,khd->hrk", head_rows, key_piece, preferred_element_type=jnp.float32)
        * inv_root
    )
    key_pos = jnp.arange(key_piece.shape[0], dtype=jnp.int32)
    visible = (key_pos[None, :] <= row_pos[:, None])[None]
    masked = jnp.where(visible, scores, -1e30)
    newest = jnp.maximum(highest, jnp.max(masked, axis=-1))
    weights = jnp.where(visible, jnp.exp(masked - newest[..., None]), 0.0)
    running = jnp.sum(weights, axis=-1)
    summed = jnp.einsum(
        "hrk,khd->hrd",
        weights.astype(jnp.bfloat16),
        value_piece,
        preferred_element_type=jnp.float32,
    )
    highest, running, summed = (newest, running, summed)
    result = (summed / running[..., None]).astype(jnp.bfloat16)
    return jnp.transpose(
        result.reshape(head_count, group_count, query_rows, head_size), (2, 0, 1, 3)
    )


def expert_pass(arrived_rows, expert_gate, expert_down):
    coded_in, scale_in = arrived_rows
    senders, capacity, features = coded_in.shape
    resident = expert_gate.shape[0]
    restored = (
        coded_in.astype(jnp.float32).reshape(senders, capacity, scale_in.shape[2], -1)
        * scale_in.astype(jnp.float32)[..., None]
    ).astype(jnp.bfloat16)
    restored = restored.reshape(senders // resident, resident, capacity, features)
    hidden = jax.nn.silu(
        jnp.einsum("sfcd,fdh->sfch", restored, expert_gate, preferred_element_type=jnp.float32)
    ).astype(jnp.bfloat16)
    result = jnp.einsum(
        "sfch,fhd->sfcd", hidden, expert_down, preferred_element_type=jnp.float32
    ).astype(jnp.bfloat16)
    result = result.reshape(senders, capacity, features)
    return result


def body(queries, key_rows, values, offset, tokens, routes, gate_share, expert_gate, expert_down):
    attended = attention_shard(queries, key_rows, values, offset)
    rows_here, features = tokens.shape
    topk_count = routes.shape[1]
    resident = expert_gate.shape[0]
    ctx_devices = lax.axis_size("ctx")
    ep_devices = lax.axis_size("ep")
    expert_total = ctx_devices * ep_devices * resident
    capacity = min(rows_here, max(2, 5 * rows_here * topk_count // (4 * expert_total)))
    scale_blocks = features // 128
    grouped = tokens.astype(jnp.float32).reshape(rows_here, scale_blocks, 128)
    block_scale = (jnp.max(jnp.abs(grouped), axis=-1) + 1e-06).astype(jnp.bfloat16)
    coded_rows = (
        (grouped / block_scale.astype(jnp.float32)[..., None])
        .astype(jnp.bfloat16)
        .reshape(rows_here, features)
    )
    pair_count = rows_here * topk_count
    chosen = routes.reshape(pair_count)
    onehot = (chosen[:, None] == jnp.arange(expert_total, dtype=jnp.int32)[None, :]).astype(
        jnp.bfloat16
    )
    before_mask = (jnp.arange(pair_count)[:, None] > jnp.arange(pair_count)[None, :]).astype(
        jnp.bfloat16
    )
    earlier = jnp.dot(before_mask, onehot, preferred_element_type=jnp.float32)
    slot_index = jnp.sum(earlier * onehot.astype(jnp.float32), axis=1).astype(jnp.int32)
    target = chosen * capacity + slot_index
    matches = (
        jnp.arange(expert_total * capacity, dtype=jnp.int32)[:, None, None]
        == target.reshape(rows_here, topk_count)[None]
    )
    placing = jnp.sum(matches.astype(jnp.int32), axis=2).astype(jnp.bfloat16)
    outgoing = (
        jnp.dot(placing, coded_rows, preferred_element_type=jnp.float32)
        .astype(jnp.bfloat16)
        .reshape(expert_total, capacity, -1)
    )
    outgoing_scale = (
        jnp.dot(placing, block_scale, preferred_element_type=jnp.float32)
        .astype(jnp.bfloat16)
        .reshape(expert_total, capacity, -1)
    )
    computed = expert_pass(
        (
            lax.all_to_all(outgoing, ("ctx", "ep"), split_axis=0, concat_axis=0, tiled=True),
            lax.all_to_all(outgoing_scale, ("ctx", "ep"), split_axis=0, concat_axis=0, tiled=True),
        ),
        expert_gate,
        expert_down,
    )
    returned = lax.all_to_all(computed, ("ctx", "ep"), split_axis=0, concat_axis=0, tiled=True)
    back_width = returned.shape[-1]
    flat_back = returned.reshape(expert_total * capacity, back_width)
    picked = jnp.take(flat_back, target, axis=0)
    parts_in = lax.all_to_all(
        picked.reshape(pair_count, 1, back_width), "tp", split_axis=2, concat_axis=1, tiled=True
    )
    picked = jnp.sum(parts_in.astype(jnp.float32), axis=1).astype(jnp.bfloat16)
    picked = picked.reshape(rows_here, topk_count, -1)
    shares = gate_share / jnp.sum(gate_share, axis=1, keepdims=True)
    mixture = jnp.sum(shares[..., None] * picked.astype(jnp.float32), axis=1).astype(jnp.bfloat16)
    return (attended, mixture)


def solution(mesh):
    return jax.shard_map(
        body,
        mesh=mesh,
        in_specs=(
            P(("rep", "ctx"), "tp", "ep", None),
            P(("rep", "ctx"), "tp", None),
            P(("rep", "ctx"), "tp", None),
            P("rep"),
            P(("rep", "ctx", "ep"), None),
            P(("rep", "ctx", "ep"), None),
            P(("rep", "ctx", "ep"), None),
            P(("ctx", "ep"), None, "tp"),
            P(("ctx", "ep"), "tp", None),
        ),
        out_specs=(P(("rep", "ctx"), "tp", "ep", None), P(("rep", "ctx", "ep"), "tp")),
        check_vma=False,
    )
```

profile of v0, /device:TPU:0, one launch (start us, length us, event | category | flops | bytes accessed | tf_op | source)
XLA Modules:
  0.0 330.5 jit_solution(4105306458870256702)
XLA Ops:
  0.6 0.9 copy.50
  1.7 0.5 fusion.17
  2.3 0.7 compare_and_fusion
  3.0 7.5 %convert_reduce_fusion = s32[1280,128]{1,0:T(8,128)} fusion(s32[128,8]{0,1:T(8,128)S(1)} %get-tuple-element.3), kind=kLoop, calls=%fused_computation.5 | loop fusion | flops 3768320 | bytes 659456 | tf_op jit(solution)/shard_map/reduce_sum | solution.py:97
  10.6 1.1 fusion.18
  11.7 1.2 copy.56
  12.9 1.6 reduce_max.19
  14.5 1.3 convolution_convert_fusion.2
  15.9 0.6 copy.53
  16.6 7.4 %all-to-all-start.1 = ((bf16[16,80,16]{1,2,0:T(8,128)(2,1)}), bf16[16,80,16]{1,2,0:T(8,128)(2,1)S(1)}, u32[]{:S(2)}, u32[]{:S(2)}) async-start(bf16[16,80,16]{1,2,0:T(8,128)(2,1)} %copy.53), calls=%async_computation.1 | async-start | bytes 131072 | tf_op jit(solution)/shard_map/all_to_all | solution.py:111
  24.3 5.2 %convolution_convert_fusion = bf16[1280,2048]{1,0:T(8,128)(2,1)} fusion(bf16[128,2048]{1,0:T(8,128)(2,1)} %param.13, f32[16,8,16,128]{3,2,1,0:T(8,128)S(1)} %bitcast.68, s32[1280,128]{1,0:T(8,128)} %convert_reduce_fusion), kind=kOutput, calls=%fused_computation.3 | convolution fusion | flops 674660352 | bytes 7471104 | tf_op jit(solution)/shard_map/dot_general | solution.py:99
  29.5 1.3 all-to-all-done.1
  30.8 4.7 %all-to-all-start = ((bf16[16,80,2048]{2,1,0:T(8,128)(2,1)}), bf16[16,80,2048]{2,1,0:T(8,128)(2,1)}, u32[]{:S(2)}, u32[]{:S(2)}) async-start(bf16[16,80,2048]{2,1,0:T(8,128)(2,1)} %bitcast.66), calls=%async_computation | async-start | bytes 10485760 | tf_op jit(solution)/shard_map/all_to_all | solution.py:110
  35.6 1.0 copy.54
  36.6 6.7 %mul.65 = f32[16,80,16,128]{3,2,1,0:T(8,128)} broadcast(f32[16,80,16]{2,1,0:T(8,128)} %copy.54), dimensions={0,1,2} | broadcast | bytes 10567680 | tf_op jit(solution)/shard_map/mul | solution.py:51
  43.3 11.5 %mul.66 = f32[16,80,2048]{2,1,0:T(8,128)} reshape(f32[16,80,16,128]{3,2,1,0:T(8,128)} %mul.65) | data formatting | bytes 20971520 | tf_op jit(solution)/shard_map/mul | solution.py:51
  54.8 76.7 %all-to-all-done = bf16[16,80,2048]{2,1,0:T(8,128)(2,1)} async-done(((bf16[16,80,2048]{2,1,0:T(8,128)(2,1)}), bf16[16,80,2048]{2,1,0:T(8,128)(2,1)}, u32[]{:S(2)}, u32[]{:S(2)}) %all-to-all-start) | async-done | bytes 5242912 | tf_op jit(solution)/shard_map/all_to_all | solution.py:110
  131.5 15.5 %convolution_convert_fusion.1 = bf16[16,80,2048]{2,1,0:T(8,128)(2,1)} fusion(bf16[1,768,2048]{2,1,0:T(8,128)(2,1)S(1)} %copy-done, f32[16,80,2048]{2,1,0:T(8,128)} %mul.66, bf16[16,80,2048]{2,1,0:T(8,128)(2,1)} %all-to-all-done, bf16[1,2048,768]{2,1,0:T(8,128)(2,1)} %param.16), kind=kOutput, calls=%fused_computation.10 | convolution fusion | flops 8068464640 | bytes 27262976 | tf_op jit(solution)/shard_map/sfch,fhd->sfcd/dot_general | solution.py:58
  147.0 24.0 %all-to-all-start.2 = ((bf16[16,80,2048]{2,1,0:T(8,128)(2,1)}), bf16[16,80,2048]{2,1,0:T(8,128)(2,1)}, u32[]{:S(2)}, u32[]{:S(2)}) async-start(bf16[16,80,2048]{2,1,0:T(8,128)(2,1)} %convolution_convert_fusion.1), calls=%async_computation.2 | async-start | bytes 10485760 | tf_op jit(solution)/shard_map/all_to_all | solution.py:116
  172.0 123.2 %all_gather.6 = bf16[512,2,128]{2,0,1:T(8,128)(2,1)S(1)} all-gather(bf16[128,2,128]{2,0,1:T(8,128)(2,1)S(1)} %copy.46), channel_id=1, replica_groups=mesh['rep'=2,'ctx'=4,'ep'=4,'tp'=1] {'ctx'}, dimensions={0}, use_global_device_ids=true | all-gather | bytes 327680 | tf_op jit(solution)/shard_map/all_gather | solution.py:21
  295.2 14.4 %all_gather.7 = bf16[512,2,128]{2,0,1:T(8,128)(2,1)S(1)} all-gather(bf16[128,2,128]{2,0,1:T(8,128)(2,1)S(1)} %copy.47), channel_id=1, replica_groups=mesh['rep'=2,'ctx'=4,'ep'=4,'tp'=1] {'ctx'}, dimensions={0}, use_global_device_ids=true | all-gather | bytes 327680 | tf_op jit(solution)/shard_map/all_gather | solution.py:22
  310.9 0.8 copy.61
  312.2 12.1 %gather_fusion = bf16[1024,2048]{1,0:T(8,128)(2,1)} fusion(bf16[1280,2048]{1,0:T(8,128)(2,1)} %bitcast.16, s32[1024]{0:T(1024)S(1)} %broadcast_clamp_fusion), kind=kCustom, calls=%fused_computation | custom fusion | bytes 8392704 | tf_op jit(solution)/shard_map/jit(_take)/gather | solution.py:119
  324.3 6.3 %multiply_reduce_fusion = bf16[128,2048]{1,0:T(8,128)(2,1)} fusion(bf16[1024,2048]{1,0:T(8,128)(2,1)} %gather_fusion, f32[128,8]{1,0:T(8,128)S(1)} %copy.49, pred[128,8]{1,0:T(8,128)(4,1)S(1)} %copy.52), kind=kLoop, calls=%fused_computation.2 | loop fusion | flops 8126464 | bytes 4723712 | tf_op jit(solution)/shard_map/reduce_sum | solution.py:126
  (40 shorter events, 2.7 us)
Async XLA Ops:
  0.6 130.9 %copy-start = (bf16[1,768,2048]{2,1,0:T(8,128)(2,1)S(1)}, bf16[1,768,2048]{2,1,0:T(8,128)(2,1)}, u32[]{:S(2)}) copy-start(bf16[1,768,2048]{2,1,0:T(8,128)(2,1)} %param.17) | copy-start | bytes 9437188
  16.6 14.3 %all-to-all-start.1 = ((bf16[16,80,16]{1,2,0:T(8,128)(2,1)}), bf16[16,80,16]{1,2,0:T(8,128)(2,1)S(1)}, u32[]{:S(2)}, u32[]{:S(2)}) async-start(bf16[16,80,16]{1,2,0:T(8,128)(2,1)} %copy.53), calls=%async_computation.1 | async-start | bytes 131072 | tf_op jit(solution)/shard_map/all_to_all | solution.py:111
  30.8 100.7 %all-to-all-start = ((bf16[16,80,2048]{2,1,0:T(8,128)(2,1)}), bf16[16,80,2048]{2,1,0:T(8,128)(2,1)}, u32[]{:S(2)}, u32[]{:S(2)}) async-start(bf16[16,80,2048]{2,1,0:T(8,128)(2,1)} %bitcast.66), calls=%async_computation | async-start | bytes 10485760 | tf_op jit(solution)/shard_map/all_to_all | solution.py:110
  147.0 24.9 %copy-start.2 = (bf16[128,2,128]{2,1,0:T(2,128)(2,1)S(1)}, bf16[128,2,128]{2,1,0:T(2,128)(2,1)}, u32[]{:S(2)}) copy-start(bf16[128,2,128]{2,1,0:T(2,128)(2,1)} %param.10) | copy-start | bytes 196612
  147.0 24.9 %copy-start.1 = (bf16[64,2,4,128]{3,2,1,0:T(4,128)(2,1)S(1)}, bf16[64,2,4,128]{3,2,1,0:T(4,128)(2,1)}, u32[]{:S(2)}) copy-start(bf16[64,2,4,128]{3,2,1,0:T(4,128)(2,1)} %param.9) | copy-start | bytes 393220
  147.0 24.9 %copy-start.3 = (bf16[128,2,128]{2,1,0:T(2,128)(2,1)S(1)}, bf16[128,2,128]{2,1,0:T(2,128)(2,1)}, u32[]{:S(2)}) copy-start(bf16[128,2,128]{2,1,0:T(2,128)(2,1)} %param.11) | copy-start | bytes 196612
  147.0 165.2 %all-to-all-start.2 = ((bf16[16,80,2048]{2,1,0:T(8,128)(2,1)}), bf16[16,80,2048]{2,1,0:T(8,128)(2,1)}, u32[]{:S(2)}, u32[]{:S(2)}) async-start(bf16[16,80,2048]{2,1,0:T(8,128)(2,1)} %convolution_convert_fusion.1), calls=%async_computation.2 | async-start | bytes 10485760 | tf_op jit(solution)/shard_map/all_to_all | solution.py:116
  171.1 140.6 %copy-start.4 = (s32[128,8]{0,1:T(8,128)S(1)}, s32[128,8]{0,1:T(8,128)}, u32[]{:S(2)}) copy-start(s32[128,8]{0,1:T(8,128)} %param.14) | copy-start | bytes 12292
  171.1 140.9 %copy-start.5 = (f32[128,8]{0,1:T(8,128)S(1)}, f32[128,8]{0,1:T(8,128)}, u32[]{:S(2)}) copy-start(f32[128,8]{0,1:T(8,128)} %param.15) | copy-start | bytes 12292
where the time goes:
time: 331 us
  blocking collectives  138 us (42%)
  waiting for transfers between devices  78 us (24%)
  local copies, waits for them, and re-layouts  36.1 us (11%)
  starting transfers between devices  36.1 us (11%)
  matrix products  23.3 us (7%)
  other arithmetic  17.8 us (5%)
    all_gather x1, blocking collectives, attention_shard(): key_piece = lax.all_gather(key_rows, 'ctx', axis=0, tiled=True)  123 us
    all_to_all x1, waiting for transfers between devices, body(): lax.all_to_all(outgoing, ('ctx', 'ep'), split_axis=0, concat_axis=0, tile...  76.7 us
    all_to_all x1, starting transfers between devices, body(): lax.all_to_all(computed, ('ctx', 'ep'), split_axis=0, concat_axis=0, tile...  24 us
    mul x2, local copies, waits for them, and re-layouts, expert_pass(): coded_in.astype(jnp.float32)  18.2 us
    dot_general x1, matrix products, expert_pass(): jnp.einsum('sfch,fhd->sfcd', hidden, expert_down, preferred_element_type=...  15.5 us
    all_gather x1, blocking collectives, attention_shard(): value_piece = lax.all_gather(values, 'ctx', axis=0, tiled=True)  14.4 us
    gather x1, local copies, waits for them, and re-layouts, body(): picked = jnp.take(flat_back, target, axis=0)  12.1 us
    reduce_sum x1, other arithmetic, body(): placing = jnp.sum(matches.astype(jnp.int32), axis=2).astype(jnp.bfloat16)  7.51 us
  transfers between devices with their start and end apart: 3, of which 2 were waited for; matrix products, arithmetic and copies ran while one was open for 8% of the time, Pallas kernels for 0%

commit v1 on v0

--- a/solution.py
+++ b/solution.py
@@ -1,9 +1,14 @@
+import functools
 import math
 
 import jax
 import jax.numpy as jnp
 from jax import lax
+from jax.experimental import pallas as pl
+from jax.experimental.pallas import tpu as pltpu
 from jax.sharding import PartitionSpec as P
+
+TAG = 128
 
 
 def attention_shard(queries, key_rows, values, offset):
@@ -127,9 +132,235 @@
     return (attended, mixture)
 
 
+def prepare_kernel(tokens_ref, routes_ref, gate_ref, out_ref, *, expert_total):
+    rows, features = tokens_ref.shape
+    for block in range(features // 128):
+        cols = slice(block * 128, (block + 1) * 128)
+        part = tokens_ref[:, cols].astype(jnp.float32)
+        scale = jnp.max(jnp.abs(part), axis=1, keepdims=True) + 1e-06
+        scale = scale.astype(jnp.bfloat16).astype(jnp.float32)
+        coded = (part / scale).astype(jnp.bfloat16).astype(jnp.float32)
+        out_ref[:, cols] = (coded * scale).astype(jnp.bfloat16)
+    gate = gate_ref[...]
+    shares = gate / jnp.sum(gate, axis=1, keepdims=True)
+    lane = lax.broadcasted_iota(jnp.int32, (rows, TAG), 1)
+    expert = lax.rem(lane, expert_total)
+    dense = jnp.zeros((rows, TAG), jnp.float32)
+    for k in range(gate.shape[1]):
+        dense += jnp.where(routes_ref[:, k : k + 1] == expert, shares[:, k : k + 1], 0.0)
+    high = dense.astype(jnp.bfloat16).astype(jnp.float32)
+    tag = jnp.where(lane < expert_total, high, jnp.where(lane < 2 * expert_total, dense - high, 0.0))
+    out_ref[:, features:] = tag.astype(jnp.bfloat16)
+
+
+def prepare(tokens, routes, gate_share, expert_total):
+    rows, features = tokens.shape
+    return pl.pallas_call(
+        functools.partial(prepare_kernel, expert_total=expert_total),
+        out_shape=jax.ShapeDtypeStruct((rows, features + TAG), jnp.bfloat16),
+    )(tokens, routes, gate_share)
+
+
+def experts_kernel(ids_ref, *refs, count, expert_total, up_steps, up_tile):
+    blocks = refs[:count]
+    gate_a, gate_b, down_a, down_b = refs[count : count + 4]
+    outs = refs[count + 4 : 2 * count + 4]
+    rows_in, shares_in, hidden = refs[2 * count + 4 :]
+    step = pl.program_id(0)
+    rows, width = blocks[0].shape
+    features = width - TAG
+    half = up_steps // 2
+
+    @pl.when(step == 0)
+    def _():
+        lane = lax.broadcasted_iota(jnp.int32, (rows, TAG), 1)
+        for i, block in enumerate(blocks):
+            here = slice(i * rows, (i + 1) * rows)
+            rows_in[here, :] = block[:, :features]
+            tag = block[:, features:].astype(jnp.float32)
+            for j in range(2):
+                expert = ids_ref[j]
+                mine = (lane == expert) | (lane == expert + expert_total)
+                share = jnp.sum(jnp.where(mine, tag, 0.0), axis=1, keepdims=True)
+                shares_in[j, here, :] = jnp.broadcast_to(share, (rows, TAG))
+
+    def up(weights_ref, j, tile):
+        value = jnp.dot(rows_in[...], weights_ref[...], preferred_element_type=jnp.float32)
+        value = value / (1.0 + jnp.exp(-value)) * shares_in[j, :, :1]
+        start = pl.multiple_of((j * half + tile) * up_tile, up_tile)
+        hidden[:, pl.ds(start, up_tile)] = value.astype(jnp.bfloat16)
+
+    @pl.when(step < half)
+    def _():
+        up(gate_a, 0, step)
+
+    @pl.when((step >= half) & (step < up_steps))
+    def _():
+        up(gate_b, 1, step - half)
+
+    @pl.when(step >= up_steps)
+    def _():
+        units = half * up_tile
+        total = jnp.dot(hidden[:, :units], down_a[...], preferred_element_type=jnp.float32)
+        total += jnp.dot(hidden[:, units:], down_b[...], preferred_element_type=jnp.float32)
+        for i, out in enumerate(outs):
+            out[...] = total[i * rows : (i + 1) * rows].astype(jnp.bfloat16)
+
+
+def experts(ids, blocks, gate_a, gate_b, down_a, down_b, expert_total):
+    count = len(blocks)
+    rows, width = blocks[0].shape
+    features, units = gate_a.shape
+    up_tile, down_tile = 256, 512
+    half = units // up_tile
+    up_steps = 2 * half
+    down_steps = features // down_tile
+    whole = pl.BlockSpec((rows, width), lambda i: (0, 0))
+    down_spec = pl.BlockSpec((units, down_tile), lambda i: (0, jnp.maximum(i - up_steps, 0)))
+    out_spec = pl.BlockSpec((rows, down_tile), lambda i: (0, jnp.maximum(i - up_steps, 0)))
+    flops = 2 * 2 * 2 * count * rows * features * units
+    return pl.pallas_call(
+        functools.partial(
+            experts_kernel,
+            count=count,
+            expert_total=expert_total,
+            up_steps=up_steps,
+            up_tile=up_tile,
+        ),
+        grid=(up_steps + down_steps,),
+        in_specs=[pl.BlockSpec(memory_space=pltpu.SMEM)]
+        + [whole] * count
+        + [
+            pl.BlockSpec((features, up_tile), lambda i: (0, jnp.minimum(i, half - 1))),
+            pl.BlockSpec((features, up_tile), lambda i: (0, jnp.clip(i - half, 0, half - 1))),
+            down_spec,
+            down_spec,
+        ],
+        out_specs=[out_spec] * count,
+        out_shape=[jax.ShapeDtypeStruct((rows, features), jnp.bfloat16)] * count,
+        scratch_shapes=[
+            pltpu.VMEM((count * rows, features), jnp.bfloat16),
+            pltpu.VMEM((2, count * rows, TAG), jnp.float32),
+            pltpu.VMEM((count * rows, 2 * units), jnp.bfloat16),
+        ],
+        compiler_params=pltpu.CompilerParams(
+            dimension_semantics=("arbitrary",), vmem_limit_bytes=48 * 1024 * 1024
+        ),
+        cost_estimate=pl.CostEstimate(
+            flops=flops, bytes_accessed=8 * features * units, transcendentals=0
+        ),
+    )(ids, *blocks, gate_a, gate_b, down_a, down_b)
+
+
+NEAR = [(0, 1), (1, 0), (2, 3), (3, 2)]
+MIDDLE = [(1, 2), (2, 1)]
+OUTWARD = [(1, 0), (2, 3)]
+INWARD = [(0, 1), (3, 2)]
+ACROSS = [(i, i ^ 2) for i in range(4)]
+SIBLING = [(i, i ^ 1) for i in range(4)]
+
+
+def along_z(array, pairs):
+    return lax.ppermute(array, "ctx", pairs)
+
+
+def across(array):
+    return lax.ppermute(array, "ep", ACROSS)
+
+
+def added(*terms):
+    return sum(term.astype(jnp.float32) for term in terms).astype(jnp.bfloat16)
+
+
+def attention_pieces(queries, key_rows, values, offset):
+    query_rows, head_count, group_count, head_size = queries.shape
+    here = lax.axis_index("ctx")
+    span = key_rows.shape[0]
+    both = jnp.concatenate(
+        [key_rows.reshape(span, -1), values.reshape(span, -1)], axis=1
+    )
+    pieces = [both] + [
+        lax.ppermute(both, "ctx", [(i, i ^ j) for i in range(4)]) for j in (1, 2, 3)
+    ]
+    pieces = jnp.concatenate(pieces, axis=0)
+    total = pieces.shape[0]
+    key_piece = pieces[:, : head_count * head_size].reshape(total, head_count, head_size)
+    value_piece = pieces[:, head_count * head_size :].reshape(total, head_count, head_size)
+    key_pos = jnp.arange(total, dtype=jnp.int32)
+    key_pos = jnp.bitwise_xor(key_pos // span, here) * span + key_pos % span
+    query_pos = offset[0] + here * query_rows + jnp.arange(query_rows, dtype=jnp.int32)
+    row_pos = jnp.tile(query_pos, group_count)
+    head_rows = jnp.transpose(queries, (1, 2, 0, 3)).reshape(
+        head_count, group_count * query_rows, head_size
+    )
+    scores = jnp.einsum(
+        "hrd,khd->hrk", head_rows, key_piece, preferred_element_type=jnp.float32
+    ) * (1.0 / math.sqrt(head_size))
+    visible = (key_pos[None, :] <= row_pos[:, None])[None]
+    masked = jnp.where(visible, scores, -1e30)
+    newest = jnp.max(masked, axis=-1, keepdims=True)
+    weights = jnp.where(visible, jnp.exp(masked - newest), 0.0)
+    running = jnp.sum(weights, axis=-1, keepdims=True)
+    summed = jnp.einsum(
+        "hrk,khd->hrd",
+        weights.astype(jnp.bfloat16),
+        value_piece,
+        preferred_element_type=jnp.float32,
+    )
+    result = (summed / running).astype(jnp.bfloat16)
+    return jnp.transpose(
+        result.reshape(head_count, group_count, query_rows, head_size), (2, 0, 1, 3)
+    )
+
+
+def plane_body(queries, key_rows, values, offset, tokens, routes, gate_share, expert_gate, expert_down):
+    expert_total = lax.axis_size("ctx") * lax.axis_size("ep")
+    z = lax.axis_index("ctx")
+    middle = (z == 1) | (z == 2)
+    own_expert = z * lax.axis_size("ep") + lax.axis_index("ep")
+    ids = jnp.stack([own_expert, own_expert ^ 1]).astype(jnp.int32)
+    gate_a, down_a = expert_gate[0], expert_down[0]
+    own = prepare(tokens, routes, gate_share, expert_total)
+    near = along_z(own, NEAR)
+    mid_one = along_z(own, MIDDLE)
+    own_x = across(own)
+    gate_b = lax.ppermute(gate_a, "ep", SIBLING)
+    down_b = lax.ppermute(down_a, "ep", SIBLING)
+
+    def run(*blocks):
+        return experts(ids, blocks, gate_a, gate_b, down_a, down_b, expert_total)
+
+    mid_two = along_z(near, MIDDLE)
+    end_one = along_z(mid_one, OUTWARD)
+    near_x = across(near)
+    attended = attention_pieces(queries, key_rows, values, offset)
+    part_own, part_own_x, part_near = run(own, own_x, near)
+    end_two = along_z(mid_two, OUTWARD)
+    second = jnp.where(middle, mid_one, end_one)
+    second_x = across(second)
+    part_near_x, part_second = run(near_x, second)
+    third = jnp.where(middle, mid_two, end_two)
+    third_x = across(third)
+    part_second_x, part_third = run(second_x, third)
+    (part_third_x,) = run(third_x)
+
+    sum_third = added(part_third, across(part_third_x))
+    back_two = along_z(sum_third, INWARD)
+    sum_second = added(part_second, across(part_second_x))
+    back_mid_two = along_z(added(sum_third, back_two), MIDDLE)
+    back_one = along_z(sum_second, INWARD)
+    sum_near = added(part_near, across(part_near_x), back_mid_two)
+    back_mid_one = along_z(added(sum_second, back_one), MIDDLE)
+    back_near = along_z(sum_near, NEAR)
+    mixture = added(part_own, across(part_own_x), back_mid_one, back_near)
+    return (attended, mixture)
+
+
 def solution(mesh):
+    plane = dict(mesh.shape)
+    plane = plane["ctx"] == 4 and plane["ep"] == 4 and plane["tp"] == 1
     return jax.shard_map(
-        body,
+        plane_body if plane else body,
         mesh=mesh,
         in_specs=(
             P(("rep", "ctx"), "tp", "ep", None),

time: 331 us -> 179 us (0.54)
  blocking collectives: 138 us -> 0 us
  Pallas kernels: 0 us -> 44.1 us
  local copies, waits for them, and re-layouts: 36.1 us -> 7.07 us
  matrix products: 23.3 us -> 1.56 us
  starting transfers between devices: 36.1 us -> 53 us
  waiting for transfers between devices: 78 us -> 63.3 us
  other arithmetic: 17.8 us -> 7.76 us
    all_gather x2 -> x0, blocking collectives: 138 us -> none  [the longest x1 123 us: attention_shard(): key_piece = lax.all_gather(key_rows, 'ctx', axis=0, tiled=True)]
    all_to_all x3 -> x0, waiting for transfers between devices: 78 us -> none  [the longest x1 76.7 us: body(): lax.all_to_all(outgoing, ('ctx', 'ep'), split_axis=0, concat_axis=0, tile...]
    ppermute x0 -> x23, waiting for transfers between devices: none -> 63.3 us  [the longest x8 32 us: across(): return lax.ppermute(array, 'ep', ACROSS)]
    ppermute x0 -> x23, starting transfers between devices: none -> 53 us  [the longest x3 26.1 us: attention_pieces(): lax.ppermute(both, 'ctx', [(i, i ^ j) for i in range(4)])]
    pallas_call x0 -> x5, Pallas kernels: none -> 44.1 us  [the longest x4 41.3 us: experts(): pl.pallas_call(functools.partial(experts_kernel, count=count, expert_tota...]
    all_to_all x3 -> x0, starting transfers between devices: 36.1 us -> none  [the longest x1 24 us: body(): lax.all_to_all(computed, ('ctx', 'ep'), split_axis=0, concat_axis=0, tile...]
    dot_general x6 -> x2, matrix products: 23.3 us -> 0.88 us  [the longest x1 0.52 us: attention_pieces(): jnp.einsum('hrk,khd->hrd', weights.astype(jnp.bfloat16), value_piece, pre...]
    mul x4 -> x0, local copies, waits for them, and re-layouts: 18.4 us -> none  [the longest x2 18.2 us: expert_pass(): coded_in.astype(jnp.float32)]
  transfers between devices with their start and end apart: 3 -> 23, of which waited for: 2 -> 9; matrix products, arithmetic and copies ran while one was open for 8% -> 6% of each run, Pallas kernels for 0% -> 23%
where the time goes in v1:
time: 179 us; the launch traced here: 178 us
  waiting for transfers between devices  63.3 us (35%)
  starting transfers between devices  53 us (30%)
  Pallas kernels  44.1 us (25%)
  other arithmetic  7.76 us (4%)
  local copies, waits for them, and re-layouts  7.07 us (4%)
    pallas_call x4, Pallas kernels, experts(): pl.pallas_call(functools.partial(experts_kernel, count=count, expert_tota...  41.3 us
    ppermute x8, waiting for transfers between devices, across(): return lax.ppermute(array, 'ep', ACROSS)  32 us
    ppermute x10, waiting for transfers between devices, along_z(): return lax.ppermute(array, 'ctx', pairs)  29.3 us
    ppermute x3, starting transfers between devices, attention_pieces(): lax.ppermute(both, 'ctx', [(i, i ^ j) for i in range(4)])  26.1 us
    ppermute x10, starting transfers between devices, along_z(): return lax.ppermute(array, 'ctx', pairs)  17 us
    ppermute x8, starting transfers between devices, across(): return lax.ppermute(array, 'ep', ACROSS)  9.39 us
    unnamed x15, local copies, waits for them, and re-layouts  5.47 us
    convert_element_type x6, other arithmetic, added(): sum((term.astype(jnp.float32) for term in terms)).astype(jnp.bfloat16)  4.67 us
  transfers between devices with their start and end apart: 23, of which 9 were waited for; matrix products, arithmetic and copies ran while one was open for 6% of the time, Pallas kernels for 23%

profile of v1, /device:TPU:0, one launch (start us, length us, event | category | flops | bytes accessed | tf_op | source)
XLA Modules:
  0.0 178.3 jit_solution(8615942266378023063)
XLA Ops:
  3.5 2.8 %shard_map.104.refs_0_ = bf16[128,2176]{1,0:T(8,128)(2,1)} custom-call(bf16[128,2048]{1,0:T(8,128)(2,1)} %tokens_ref.1, s32[128,8]{1,0:T(8,128)} %copy.22.routes_ref, f32[128,8]{1,0:T(8,128)} %copy.23.gate_ref), custom_call_target="tpu_custom_call" | custom-call | tf_op jit(solution)/shard_map/pallas_call | solution.py:158
  6.3 3.0 %collective-permute-start.4 = (bf16[128,2176]{1,0:T(8,128)(2,1)}, bf16[128,2176]{1,0:T(8,128)(2,1)}, u32[]{:S(2)}, u32[]{:S(2)}) collective-permute-start(bf16[128,2176]{1,0:T(8,128)(2,1)} %shard_map.104.refs_0_), channel_id=1, source_target_pairs={{0,4},{4,0},{8,12},{12,8},{1,5},{5,1},{9,13},{13,9},{2,6},{6,2},{1... | collective-permute-start | bytes 1671176 | tf_op jit(solution)/shard_map/ppermute | solution.py:264
  9.8 12.4 %collective-permute-done.4.refs_2_ = bf16[128,2176]{1,0:T(8,128)(2,1)} collective-permute-done((bf16[128,2176]{1,0:T(8,128)(2,1)}, bf16[128,2176]{1,0:T(8,128)(2,1)}, u32[]{:S(2)}, u32[]{:S(2)}) %collective-permute-start.4) | collective-permute-done | bytes 557088 | tf_op jit(solution)/shard_map/ppermute | solution.py:264
  29.2 15.4 %collective-permute-start = (bf16[128,512]{0,1:T(8,128)(2,1)}, bf16[128,512]{0,1:T(8,128)(2,1)}, u32[]{:S(2)}, u32[]{:S(2)}) collective-permute-start(bf16[128,512]{0,1:T(8,128)(2,1)} %pad_maximum_fusion.1), channel_id=1, source_target_pairs={{0,4},{4,0},{8,12},{12,8},{1,5},{5,1},{9,13},{13,9},{2,6},{6,2},{1... | collective-permute-start | bytes 393224 | tf_op jit(solution)/shard_map/ppermute | solution.py:283
  45.5 7.4 %collective-permute-start.1 = (bf16[128,512]{0,1:T(8,128)(2,1)}, bf16[128,512]{0,1:T(8,128)(2,1)S(1)}, u32[]{:S(2)}, u32[]{:S(2)}) collective-permute-start(bf16[128,512]{0,1:T(8,128)(2,1)} %pad_maximum_fusion.1), channel_id=1, source_target_pairs={{0,8},{4,12},{8,0},{12,4},{1,9},{5,13},{9,1},{13,5},{2,10},{6,14},... | collective-permute-start | bytes 393224 | tf_op jit(solution)/shard_map/ppermute | solution.py:283
  52.9 3.2 %collective-permute-done.13 = bf16[128,2176]{1,0:T(8,128)(2,1)} collective-permute-done((bf16[128,2176]{1,0:T(8,128)(2,1)}, bf16[128,2176]{1,0:T(8,128)(2,1)}, u32[]{:S(2)}, u32[]{:S(2)}) %collective-permute-start.13) | collective-permute-done | bytes 557088 | tf_op jit(solution)/shard_map/ppermute | solution.py:264
  58.5 2.0 %collective-permute-done = bf16[128,512]{0,1:T(8,128)(2,1)} collective-permute-done((bf16[128,512]{0,1:T(8,128)(2,1)}, bf16[128,512]{0,1:T(8,128)(2,1)}, u32[]{:S(2)}, u32[]{:S(2)}) %collective-permute-start) | collective-permute-done | bytes 131104 | tf_op jit(solution)/shard_map/ppermute | solution.py:283
  60.6 3.3 %collective-permute-start.2 = (bf16[128,512]{0,1:T(8,128)(2,1)}, bf16[128,512]{0,1:T(8,128)(2,1)S(1)}, u32[]{:S(2)}, u32[]{:S(2)}) collective-permute-start(bf16[128,512]{0,1:T(8,128)(2,1)} %pad_maximum_fusion.1), channel_id=1, source_target_pairs={{0,12},{4,8},{8,4},{12,0},{1,13},{5,9},{9,5},{13,1},{2,14},{6,10},... | collective-permute-start | bytes 393224 | tf_op jit(solution)/shard_map/ppermute | solution.py:283
  63.9 8.5 %collective-permute-done.10 = bf16[128,2176]{1,0:T(8,128)(2,1)S(1)} collective-permute-done((bf16[128,2176]{1,0:T(8,128)(2,1)}, bf16[128,2176]{1,0:T(8,128)(2,1)S(1)}, u32[]{:S(2)}, u32[]{:S(2)}) %collective-permute-start.10) | collective-permute-done | bytes 557088 | tf_op jit(solution)/shard_map/ppermute | solution.py:264
  77.8 10.1 %collective-permute-done.18.refs_0_ = bf16[128,2176]{1,0:T(8,128)(2,1)S(1)} collective-permute-done((bf16[128,2176]{1,0:T(8,128)(2,1)S(1)}, bf16[128,2176]{1,0:T(8,128)(2,1)S(1)}, u32[]{:S(2)}, u32[]{:S(2)}) %collective-permute-start.18) | collective-permute-done | bytes 557088 | tf_op jit(solution)/shard_map/ppermute | solution.py:268
  88.0 9.0 %shard_map.108 = bf16[128,2048]{1,0:T(8,128)(2,1)S(1)} custom-call(s32[2]{0:T(128)S(1)} %pad_add_fusion.ids_ref, bf16[128,2176]{1,0:T(8,128)(2,1)S(1)} %collective-permute-done.18.refs_0_, bf16[2048,768]{1,0:T(8,128)(2,1)S(1)} %bitcast.33, bf16[2048,768]{1,0:T(8,128)(2,1)} %collective-permute-done.5.refs_4_.refs_3_.refs_2_, bf16[768,2048]{1,0:T(8,128)(2,1)} %bitcast.37, ...), custom_call_target="tpu_custom_call" | custom-call | flops 1610612736 | bytes 12582912 | tf_op jit(solution)/shard_map/pallas_call | solution.py:222
  96.9 1.6 collective-permute-start.19
  99.9 10.1 %shard_map.107 = (bf16[128,2048]{1,0:T(8,128)(2,1)S(1)}, bf16[128,2048]{1,0:T(8,128)(2,1)S(1)}) custom-call(s32[2]{0:T(128)S(1)} %pad_add_fusion.ids_ref, bf16[128,2176]{1,0:T(8,128)(2,1)S(1)} %collective-permute-done.11.refs_0_, bf16[128,2176]{1,0:T(8,128)(2,1)S(1)} %broadcast_select_fusion.refs_1_, bf16[2048,768]{1,0:T(8,128)(2,1)S(1)} %bitcast.34, ...), custom_call_target="tpu_custom_call" | custom-call | flops 3221225472 | bytes 12582912 | tf_op jit(solution)/shard_map/pallas_call | solution.py:222
  110.0 1.6 collective-permute-start.14
  111.5 11.5 %collective-permute-done.19 = bf16[128,2048]{1,0:T(8,128)(2,1)S(1)} collective-permute-done((bf16[128,2048]{1,0:T(8,128)(2,1)S(1)}, bf16[128,2048]{1,0:T(8,128)(2,1)S(1)}, u32[]{:S(2)}, u32[]{:S(2)}) %collective-permute-start.19) | collective-permute-done | bytes 524320 | tf_op jit(solution)/shard_map/ppermute | solution.py:268
  123.2 1.6 collective-permute-start.20
  124.8 10.2 %collective-permute-done.8.refs_0_ = bf16[128,2176]{1,0:T(8,128)(2,1)S(1)} collective-permute-done((bf16[128,2176]{1,0:T(8,128)(2,1)}, bf16[128,2176]{1,0:T(8,128)(2,1)S(1)}, u32[]{:S(2)}, u32[]{:S(2)}) %collective-permute-start.8) | collective-permute-done | bytes 557088 | tf_op jit(solution)/shard_map/ppermute | solution.py:268
  135.0 10.1 %shard_map.106 = (bf16[128,2048]{1,0:T(8,128)(2,1)S(1)}, bf16[128,2048]{1,0:T(8,128)(2,1)S(1)}) custom-call(s32[2]{0:T(128)S(1)} %pad_add_fusion.ids_ref, bf16[128,2176]{1,0:T(8,128)(2,1)S(1)} %collective-permute-done.8.refs_0_, bf16[128,2176]{1,0:T(8,128)(2,1)S(1)} %broadcast_select_fusion.1.refs_1_, bf16[2048,768]{1,0:T(8,128)(2,1)S(1)} %bitcast.35, ...), custom_call_target="tpu_custom_call" | custom-call | flops 3221225472 | bytes 12582912 | tf_op jit(solution)/shard_map/pallas_call | solution.py:222
  145.1 1.6 collective-permute-start.17
  146.8 1.6 collective-permute-start.15
  149.2 12.2 %shard_map.105 = (bf16[128,2048]{1,0:T(8,128)(2,1)S(1)}, bf16[128,2048]{1,0:T(8,128)(2,1)S(1)}, bf16[128,2048]{1,0:T(8,128)(2,1)S(1)}) custom-call(s32[2]{0:T(128)S(1)} %pad_add_fusion.ids_ref, bf16[128,2176]{1,0:T(8,128)(2,1)S(1)} %copy-done.1, bf16[128,2176]{1,0:T(8,128)(2,1)S(1)} %collective-permute-done.3.refs_1_, ...), custom_call_target="tpu_custom_call" | custom-call | flops 4831838208 | bytes 12582912 | tf_op jit(solution)/shard_map/pallas_call | solution.py:222
  165.4 3.1 %collective-permute-start.22 = (bf16[128,2048]{1,0:T(8,128)(2,1)}, bf16[128,2048]{1,0:T(8,128)(2,1)}, u32[]{:S(2)}, u32[]{:S(2)}) collective-permute-start(bf16[128,2048]{1,0:T(8,128)(2,1)} %add_convert_fusion.1), channel_id=1, source_target_pairs={{0,4},{4,0},{8,12},{12,8},{1,5},{5,1},{9,13},{13,9},{2,6},{6,2},{1... | collective-permute-start | bytes 1572872 | tf_op jit(solution)/shard_map/ppermute | solution.py:264
  170.9 5.1 %collective-permute-done.22 = bf16[128,2048]{1,0:T(8,128)(2,1)} collective-permute-done((bf16[128,2048]{1,0:T(8,128)(2,1)}, bf16[128,2048]{1,0:T(8,128)(2,1)}, u32[]{:S(2)}, u32[]{:S(2)}) %collective-permute-start.22) | collective-permute-done | bytes 524320 | tf_op jit(solution)/shard_map/ppermute | solution.py:264
  176.0 2.3 %add_convert_fusion = bf16[128,2048]{1,0:T(8,128)(2,1)} fusion(bf16[128,2048]{1,0:T(8,128)(2,1)} %collective-permute-done.22, bf16[128,2048]{1,0:T(8,128)(2,1)} %collective-permute-done.16, bf16[128,2048]{1,0:T(8,128)(2,1)S(1)} %collective-permute-done.7, bf16[128,2048]{1,0:T(8,128)(2,1)S(1)} %get-tuple-element.9), kind=kLoop, calls=%fused_computation.9 | loop fusion | flops 2097152 | bytes 2621440 | tf_op jit(solution)/shard_map/convert_element_type | solution.py:272
  (63 shorter events, 27.1 us)
Async XLA Ops:
  3.5 84.4 %copy-start = (bf16[1,2048,768]{2,1,0:T(8,128)(2,1)S(1)}, bf16[1,2048,768]{2,1,0:T(8,128)(2,1)}, u32[]{:S(2)}) copy-start(bf16[1,2048,768]{2,1,0:T(8,128)(2,1)} %param.16) | copy-start | bytes 9437188
  6.3 16.0 %collective-permute-start.4 = (bf16[128,2176]{1,0:T(8,128)(2,1)}, bf16[128,2176]{1,0:T(8,128)(2,1)}, u32[]{:S(2)}, u32[]{:S(2)}) collective-permute-start(bf16[128,2176]{1,0:T(8,128)(2,1)} %shard_map.104.refs_0_), channel_id=1, source_target_pairs={{0,4},{4,0},{8,12},{12,8},{1,5},{5,1},{9,13},{13,9},{2,6},{6,2},{1... | collective-permute-start | bytes 1671176 | tf_op jit(solution)/shard_map/ppermute | solution.py:264
  9.3 78.6 %collective-permute-start.5 = (bf16[2048,768]{1,0:T(8,128)(2,1)}, bf16[2048,768]{1,0:T(8,128)(2,1)}, u32[]{:S(2)}, u32[]{:S(2)}) collective-permute-start(bf16[2048,768]{1,0:T(8,128)(2,1)} %bitcast.31), channel_id=1, source_target_pairs={{0,1},{1,0},{2,3},{3,2},{4,5},{5,4},{6,7},{7,6},{8,9},{9,8},{10,11... | collective-permute-start | bytes 9437192 | tf_op jit(solution)/shard_map/ppermute | solution.py:327
  9.3 78.6 %collective-permute-start.6 = (bf16[768,2048]{1,0:T(8,128)(2,1)}, bf16[768,2048]{1,0:T(8,128)(2,1)}, u32[]{:S(2)}, u32[]{:S(2)}) collective-permute-start(bf16[768,2048]{1,0:T(8,128)(2,1)} %bitcast.36), channel_id=1, source_target_pairs={{0,1},{1,0},{2,3},{3,2},{4,5},{5,4},{6,7},{7,6},{8,9},{9,8},{10,11... | collective-permute-start | bytes 9437192 | tf_op jit(solution)/shard_map/ppermute | solution.py:328
  22.3 4.9 %collective-permute-start.12 = (bf16[128,2176]{1,0:T(8,128)(2,1)}, bf16[128,2176]{1,0:T(8,128)(2,1)}, u32[]{:S(2)}, u32[]{:S(2)}) collective-permute-start(bf16[128,2176]{1,0:T(8,128)(2,1)} %collective-permute-done.4.refs_2_), channel_id=1, source_target_pairs={{4,8},{8,4},{5,9},{9,5},{6,10},{10,6},{7,11},{11,7},{20,24},{24,20... | collective-permute-start | bytes 1671176 | tf_op jit(solution)/shard_map/ppermute | solution.py:264
  23.8 21.7 %collective-permute-start.9 = (bf16[128,2176]{1,0:T(8,128)(2,1)}, bf16[128,2176]{1,0:T(8,128)(2,1)}, u32[]{:S(2)}, u32[]{:S(2)}) collective-permute-start(bf16[128,2176]{1,0:T(8,128)(2,1)} %shard_map.104.refs_0_), channel_id=1, source_target_pairs={{4,8},{8,4},{5,9},{9,5},{6,10},{10,6},{7,11},{11,7},{20,24},{24,20... | collective-permute-start | bytes 1671176 | tf_op jit(solution)/shard_map/ppermute | solution.py:264
  27.2 28.9 %collective-permute-start.13 = (bf16[128,2176]{1,0:T(8,128)(2,1)}, bf16[128,2176]{1,0:T(8,128)(2,1)}, u32[]{:S(2)}, u32[]{:S(2)}) collective-permute-start(bf16[128,2176]{1,0:T(8,128)(2,1)} %collective-permute-done.12), channel_id=1, source_target_pairs={{4,0},{8,12},{5,1},{9,13},{6,2},{10,14},{7,3},{11,15},{20,16},{24,... | collective-permute-start | bytes 1671176 | tf_op jit(solution)/shard_map/ppermute | solution.py:264
  29.2 31.4 %collective-permute-start = (bf16[128,512]{0,1:T(8,128)(2,1)}, bf16[128,512]{0,1:T(8,128)(2,1)}, u32[]{:S(2)}, u32[]{:S(2)}) collective-permute-start(bf16[128,512]{0,1:T(8,128)(2,1)} %pad_maximum_fusion.1), channel_id=1, source_target_pairs={{0,4},{4,0},{8,12},{12,8},{1,5},{5,1},{9,13},{13,9},{2,6},{6,2},{1... | collective-permute-start | bytes 393224 | tf_op jit(solution)/shard_map/ppermute | solution.py:283
  45.5 28.4 %collective-permute-start.1 = (bf16[128,512]{0,1:T(8,128)(2,1)}, bf16[128,512]{0,1:T(8,128)(2,1)S(1)}, u32[]{:S(2)}, u32[]{:S(2)}) collective-permute-start(bf16[128,512]{0,1:T(8,128)(2,1)} %pad_maximum_fusion.1), channel_id=1, source_target_pairs={{0,8},{4,12},{8,0},{12,4},{1,9},{5,13},{9,1},{13,5},{2,10},{6,14},... | collective-permute-start | bytes 393224 | tf_op jit(solution)/shard_map/ppermute | solution.py:283
  56.1 16.3 %collective-permute-start.10 = (bf16[128,2176]{1,0:T(8,128)(2,1)}, bf16[128,2176]{1,0:T(8,128)(2,1)S(1)}, u32[]{:S(2)}, u32[]{:S(2)}) collective-permute-start(bf16[128,2176]{1,0:T(8,128)(2,1)} %collective-permute-done.9), channel_id=1, source_target_pairs={{4,0},{8,12},{5,1},{9,13},{6,2},{10,14},{7,3},{11,15},{20,16},{24,... | collective-permute-start | bytes 1671176 | tf_op jit(solution)/shard_map/ppermute | solution.py:264
  60.6 14.7 %collective-permute-start.2 = (bf16[128,512]{0,1:T(8,128)(2,1)}, bf16[128,512]{0,1:T(8,128)(2,1)S(1)}, u32[]{:S(2)}, u32[]{:S(2)}) collective-permute-start(bf16[128,512]{0,1:T(8,128)(2,1)} %pad_maximum_fusion.1), channel_id=1, source_target_pairs={{0,12},{4,8},{8,4},{12,0},{1,13},{5,9},{9,5},{13,1},{2,14},{6,10},... | collective-permute-start | bytes 393224 | tf_op jit(solution)/shard_map/ppermute | solution.py:283
  72.4 15.6 %collective-permute-start.18 = (bf16[128,2176]{1,0:T(8,128)(2,1)S(1)}, bf16[128,2176]{1,0:T(8,128)(2,1)S(1)}, u32[]{:S(2)}, u32[]{:S(2)}) collective-permute-start(bf16[128,2176]{1,0:T(8,128)(2,1)S(1)} %broadcast_select_fusion.refs_1_), channel_id=1, source_target_pairs={{0,2},{1,3},{2,0},{3,1},{4,6},{5,7},{6,4},{7,5},{8,10},{9,11},{10,... | collective-permute-start | bytes 1671176 | tf_op jit(solution)/shard_map/ppermute | solution.py:268
  74.0 25.9 %collective-permute-start.11 = (bf16[128,2176]{1,0:T(8,128)(2,1)S(1)}, bf16[128,2176]{1,0:T(8,128)(2,1)S(1)}, u32[]{:S(2)}, u32[]{:S(2)}) collective-permute-start(bf16[128,2176]{1,0:T(8,128)(2,1)S(1)} %broadcast_select_fusion.1.refs_1_), channel_id=1, source_target_pairs={{0,2},{1,3},{2,0},{3,1},{4,6},{5,7},{6,4},{7,5},{8,10},{9,11},{10,... | collective-permute-start | bytes 1671176 | tf_op jit(solution)/shard_map/ppermute | solution.py:268
  75.3 73.9 %collective-permute-start.3 = (bf16[128,2176]{1,0:T(8,128)(2,1)S(1)}, bf16[128,2176]{1,0:T(8,128)(2,1)S(1)}, u32[]{:S(2)}, u32[]{:S(2)}) collective-permute-start(bf16[128,2176]{1,0:T(8,128)(2,1)S(1)} %copy-done.1), channel_id=1, source_target_pairs={{0,2},{1,3},{2,0},{3,1},{4,6},{5,7},{6,4},{7,5},{8,10},{9,11},{10,... | collective-permute-start | bytes 1671176 | tf_op jit(solution)/shard_map/ppermute | solution.py:268
  96.9 26.1 %collective-permute-start.19 = (bf16[128,2048]{1,0:T(8,128)(2,1)S(1)}, bf16[128,2048]{1,0:T(8,128)(2,1)S(1)}, u32[]{:S(2)}, u32[]{:S(2)}) collective-permute-start(bf16[128,2048]{1,0:T(8,128)(2,1)S(1)} %shard_map.108), channel_id=1, source_target_pairs={{0,2},{1,3},{2,0},{3,1},{4,6},{5,7},{6,4},{7,5},{8,10},{9,11},{10,... | collective-permute-start | bytes 1572872 | tf_op jit(solution)/shard_map/ppermute | solution.py:268
  99.2 35.7 %collective-permute-start.8 = (bf16[128,2176]{1,0:T(8,128)(2,1)}, bf16[128,2176]{1,0:T(8,128)(2,1)S(1)}, u32[]{:S(2)}, u32[]{:S(2)}) collective-permute-start(bf16[128,2176]{1,0:T(8,128)(2,1)} %collective-permute-done.4.refs_2_), channel_id=1, source_target_pairs={{0,2},{1,3},{2,0},{3,1},{4,6},{5,7},{6,4},{7,5},{8,10},{9,11},{10,... | collective-permute-start | bytes 1671176 | tf_op jit(solution)/shard_map/ppermute | solution.py:268
  110.0 36.7 %collective-permute-start.14 = (bf16[128,2048]{1,0:T(8,128)(2,1)S(1)}, bf16[128,2048]{1,0:T(8,128)(2,1)S(1)}, u32[]{:S(2)}, u32[]{:S(2)}) collective-permute-start(bf16[128,2048]{1,0:T(8,128)(2,1)S(1)} %get-tuple-element.12), channel_id=1, source_target_pairs={{0,2},{1,3},{2,0},{3,1},{4,6},{5,7},{6,4},{7,5},{8,10},{9,11},{10,... | collective-permute-start | bytes 1572872 | tf_op jit(solution)/shard_map/ppermute | solution.py:268
  123.2 25.2 %collective-permute-start.20 = (bf16[128,2048]{1,0:T(8,128)(2,1)S(1)}, bf16[128,2048]{1,0:T(8,128)(2,1)S(1)}, u32[]{:S(2)}, u32[]{:S(2)}) collective-permute-start(bf16[128,2048]{1,0:T(8,128)(2,1)S(1)} %add_convert_fusion.3), channel_id=1, source_target_pairs={{0,4},{12,8},{1,5},{13,9},{2,6},{14,10},{3,7},{15,11},{16,20},{28,... | collective-permute-start | bytes 1572872 | tf_op jit(solution)/shard_map/ppermute | solution.py:264
  145.1 19.3 %collective-permute-start.17 = (bf16[128,2048]{1,0:T(8,128)(2,1)S(1)}, bf16[128,2048]{1,0:T(8,128)(2,1)S(1)}, u32[]{:S(2)}, u32[]{:S(2)}) collective-permute-start(bf16[128,2048]{1,0:T(8,128)(2,1)S(1)} %get-tuple-element.14), channel_id=1, source_target_pairs={{0,2},{1,3},{2,0},{3,1},{4,6},{5,7},{6,4},{7,5},{8,10},{9,11},{10,... | collective-permute-start | bytes 1572872 | tf_op jit(solution)/shard_map/ppermute | solution.py:268
  146.8 15.2 %collective-permute-start.15 = (bf16[128,2048]{1,0:T(8,128)(2,1)S(1)}, bf16[128,2048]{1,0:T(8,128)(2,1)S(1)}, u32[]{:S(2)}, u32[]{:S(2)}) collective-permute-start(bf16[128,2048]{1,0:T(8,128)(2,1)S(1)} %add_convert_fusion.5), channel_id=1, source_target_pairs={{0,4},{12,8},{1,5},{13,9},{2,6},{14,10},{3,7},{15,11},{16,20},{28,... | collective-permute-start | bytes 1572872 | tf_op jit(solution)/shard_map/ppermute | solution.py:264
  148.5 15.9 %collective-permute-start.21 = (bf16[128,2048]{1,0:T(8,128)(2,1)S(1)}, bf16[128,2048]{1,0:T(8,128)(2,1)S(1)}, u32[]{:S(2)}, u32[]{:S(2)}) collective-permute-start(bf16[128,2048]{1,0:T(8,128)(2,1)S(1)} %add_convert_fusion.2), channel_id=1, source_target_pairs={{4,8},{8,4},{5,9},{9,5},{6,10},{10,6},{7,11},{11,7},{20,24},{24,20... | collective-permute-start | bytes 1572872 | tf_op jit(solution)/shard_map/ppermute | solution.py:264
  161.4 9.4 %collective-permute-start.7 = (bf16[128,2048]{1,0:T(8,128)(2,1)S(1)}, bf16[128,2048]{1,0:T(8,128)(2,1)S(1)}, u32[]{:S(2)}, u32[]{:S(2)}) collective-permute-start(bf16[128,2048]{1,0:T(8,128)(2,1)S(1)} %get-tuple-element.10), channel_id=1, source_target_pairs={{0,2},{1,3},{2,0},{3,1},{4,6},{5,7},{6,4},{7,5},{8,10},{9,11},{10,... | collective-permute-start | bytes 1572872 | tf_op jit(solution)/shard_map/ppermute | solution.py:268
  162.9 7.9 %collective-permute-start.16 = (bf16[128,2048]{1,0:T(8,128)(2,1)}, bf16[128,2048]{1,0:T(8,128)(2,1)}, u32[]{:S(2)}, u32[]{:S(2)}) collective-permute-start(bf16[128,2048]{1,0:T(8,128)(2,1)} %add_convert_fusion.4), channel_id=1, source_target_pairs={{4,8},{8,4},{5,9},{9,5},{6,10},{10,6},{7,11},{11,7},{20,24},{24,20... | collective-permute-start | bytes 1572872 | tf_op jit(solution)/shard_map/ppermute | solution.py:264
  165.4 10.5 %collective-permute-start.22 = (bf16[128,2048]{1,0:T(8,128)(2,1)}, bf16[128,2048]{1,0:T(8,128)(2,1)}, u32[]{:S(2)}, u32[]{:S(2)}) collective-permute-start(bf16[128,2048]{1,0:T(8,128)(2,1)} %add_convert_fusion.1), channel_id=1, source_target_pairs={{0,4},{4,0},{8,12},{12,8},{1,5},{5,1},{9,13},{13,9},{2,6},{6,2},{1... | collective-permute-start | bytes 1572872 | tf_op jit(solution)/shard_map/ppermute | solution.py:264
  (4 other events, 116.2 us)

commit v2 on v0

--- a/solution.py
+++ b/solution.py
@@ -1,9 +1,14 @@
+import functools
 import math
 
 import jax
 import jax.numpy as jnp
 from jax import lax
+from jax.experimental import pallas as pl
+from jax.experimental.pallas import tpu as pltpu
 from jax.sharding import PartitionSpec as P
+
+TAG = 128
 
 
 def attention_shard(queries, key_rows, values, offset):
@@ -127,9 +132,249 @@
     return (attended, mixture)
 
 
+def prepare_kernel(tokens_ref, routes_ref, gate_ref, out_ref, *, expert_total):
+    rows, features = tokens_ref.shape
+    gate = gate_ref[...]
+    shares = gate / jnp.sum(gate, axis=0, keepdims=True)
+    line = lax.broadcasted_iota(jnp.int32, (TAG, rows), 0)
+    expert = lax.rem(line, expert_total)
+    dense = jnp.zeros((TAG, rows), jnp.float32)
+    for k in range(gate.shape[0]):
+        dense += jnp.where(routes_ref[k : k + 1, :] == expert, shares[k : k + 1, :], 0.0)
+    high = dense.astype(jnp.bfloat16).astype(jnp.float32)
+    tag = jnp.where(line < expert_total, high, jnp.where(line < 2 * expert_total, dense - high, 0.0))
+    out_ref[:, features:] = tag.T.astype(jnp.bfloat16)
+    for block in range(features // 128):
+        cols = slice(block * 128, (block + 1) * 128)
+        part = tokens_ref[:, cols].astype(jnp.float32)
+        scale = jnp.max(jnp.abs(part), axis=1, keepdims=True) + 1e-06
+        scale = scale.astype(jnp.bfloat16).astype(jnp.float32)
+        coded = (part / scale).astype(jnp.bfloat16).astype(jnp.float32)
+        out_ref[:, cols] = (coded * scale).astype(jnp.bfloat16)
+
+
+def prepare(tokens, routes, gate_share, expert_total):
+    rows, features = tokens.shape
+    return pl.pallas_call(
+        functools.partial(prepare_kernel, expert_total=expert_total),
+        out_shape=jax.ShapeDtypeStruct((rows, features + TAG), jnp.bfloat16),
+    )(tokens, routes.T, gate_share.T)
+
+
+def experts_kernel(ids_ref, *refs, count, expert_total):
+    blocks = refs[:count]
+    gates, downs = refs[count : count + 2], refs[count + 2 : count + 4]
+    outs = refs[count + 4 : 2 * count + 4]
+    rows_in, shares_in, hidden = refs[2 * count + 4 :]
+    rows, width = blocks[0].shape
+    features = width - TAG
+    units = gates[0].shape[1]
+    up_tile, down_tile = 256, 512
+    lane = lax.broadcasted_iota(jnp.int32, (rows, TAG), 1)
+    for i, block in enumerate(blocks):
+        here = slice(i * rows, (i + 1) * rows)
+        rows_in[here, :] = block[:, :features]
+        tag = block[:, features:].astype(jnp.float32)
+        for j in range(2):
+            mine = (lane == ids_ref[j]) | (lane == ids_ref[j] + expert_total)
+            share = jnp.sum(jnp.where(mine, tag, 0.0), axis=1, keepdims=True)
+            shares_in[j, here, :] = jnp.broadcast_to(share, (rows, TAG))
+    for j in range(2):
+        for start in range(0, units, up_tile):
+            value = jnp.dot(
+                rows_in[...],
+                gates[j][:, start : start + up_tile],
+                preferred_element_type=jnp.float32,
+            )
+            value = value / (1.0 + jnp.exp(-value)) * shares_in[j, :, :1]
+            first = j * units + start
+            hidden[:, first : first + up_tile] = value.astype(jnp.bfloat16)
+    for start in range(0, features, down_tile):
+        cols = slice(start, start + down_tile)
+        total = jnp.dot(hidden[:, :units], downs[0][:, cols], preferred_element_type=jnp.float32)
+        total += jnp.dot(hidden[:, units:], downs[1][:, cols], preferred_element_type=jnp.float32)
+        for i, out in enumerate(outs):
+            out[:, cols] = total[i * rows : (i + 1) * rows].astype(jnp.bfloat16)
+
+
+def experts(ids, blocks, gate_a, gate_b, down_a, down_b, expert_total):
+    count = len(blocks)
+    rows, width = blocks[0].shape
+    features, units = gate_a.shape
+    inside = pl.BlockSpec(memory_space=pltpu.VMEM)
+    return pl.pallas_call(
+        functools.partial(experts_kernel, count=count, expert_total=expert_total),
+        in_specs=[pl.BlockSpec(memory_space=pltpu.SMEM)] + [inside] * (count + 4),
+        out_specs=[inside] * count,
+        out_shape=[jax.ShapeDtypeStruct((rows, features), jnp.bfloat16)] * count,
+        scratch_shapes=[
+            pltpu.VMEM((count * rows, features), jnp.bfloat16),
+            pltpu.VMEM((2, count * rows, TAG), jnp.float32),
+            pltpu.VMEM((count * rows, 2 * units), jnp.bfloat16),
+        ],
+        compiler_params=pltpu.CompilerParams(vmem_limit_bytes=16 * 1024 * 1024),
+        cost_estimate=pl.CostEstimate(
+            flops=8 * count * rows * features * units,
+            bytes_accessed=8 * features * units,
+            transcendentals=0,
+        ),
+    )(ids, *blocks, gate_a, gate_b, down_a, down_b)
+
+
+def attention_kernel(where_ref, queries_ref, *refs, heads, head_size):
+    pieces, out_ref = refs[:-1], refs[-1]
+    query_rows, width = queries_ref.shape
+    groups = width // (heads * head_size)
+    span = pieces[0].shape[0]
+    row = lax.broadcasted_iota(jnp.int32, (query_rows, span), 0)
+    col = lax.broadcasted_iota(jnp.int32, (query_rows, span), 1)
+    seen = [
+        jnp.concatenate([where_ref[p] + col <= where_ref[len(pieces)] + row] * groups, axis=0)
+        for p in range(len(pieces))
+    ]
+    for h in range(heads):
+        first = h * groups * head_size
+        rows = jnp.concatenate(
+            [
+                queries_ref[:, first + g * head_size : first + (g + 1) * head_size]
+                for g in range(groups)
+            ],
+            axis=0,
+        )
+        scores = []
+        for p, piece in enumerate(pieces):
+            keys = piece[:, h * head_size : (h + 1) * head_size]
+            value = lax.dot_general(
+                rows, keys, (((1,), (1,)), ((), ())), preferred_element_type=jnp.float32
+            ) * (1.0 / math.sqrt(head_size))
+            scores.append(jnp.where(seen[p], value, -1e30))
+        top = scores[0].max(axis=1, keepdims=True)
+        for value in scores[1:]:
+            top = jnp.maximum(top, value.max(axis=1, keepdims=True))
+        running = jnp.zeros_like(top)
+        summed = jnp.zeros((rows.shape[0], head_size), jnp.float32)
+        for p, piece in enumerate(pieces):
+            weights = jnp.where(seen[p], jnp.exp(scores[p] - top), 0.0)
+            running += weights.sum(axis=1, keepdims=True)
+            content = piece[:, (heads + h) * head_size : (heads + h + 1) * head_size]
+            summed += jnp.dot(
+                weights.astype(jnp.bfloat16), content, preferred_element_type=jnp.float32
+            )
+        result = (summed / running).astype(jnp.bfloat16)
+        for g in range(groups):
+            out_ref[:, first + g * head_size : first + (g + 1) * head_size] = result[
+                g * query_rows : (g + 1) * query_rows
+            ]
+
+
+def attention_pieces(queries, pieces, positions, heads, head_size):
+    query_rows, width = queries.shape
+    inside = pl.BlockSpec(memory_space=pltpu.VMEM)
+    return pl.pallas_call(
+        functools.partial(attention_kernel, heads=heads, head_size=head_size),
+        in_specs=[pl.BlockSpec(memory_space=pltpu.SMEM)] + [inside] * (1 + len(pieces)),
+        out_specs=inside,
+        out_shape=jax.ShapeDtypeStruct((query_rows, width), jnp.bfloat16),
+        cost_estimate=pl.CostEstimate(
+            flops=10**9, bytes_accessed=4 * 10**6, transcendentals=0
+        ),
+    )(positions, queries, *pieces)
+
+
+NEAR = [(0, 1), (1, 0), (2, 3), (3, 2)]
+MIDDLE = [(1, 2), (2, 1)]
+OUTWARD = [(1, 0), (2, 3)]
+INWARD = [(0, 1), (3, 2)]
+ACROSS = [(i, i ^ 2) for i in range(4)]
+SIBLING = [(i, i ^ 1) for i in range(4)]
+
+
+def along_z(array, pairs):
+    return lax.ppermute(array, "ctx", pairs)
+
+
+def across(array):
+    return lax.ppermute(array, "ep", ACROSS)
+
+
+def added(*terms):
+    return sum(term.astype(jnp.float32) for term in terms).astype(jnp.bfloat16)
+
+
+def together(*arrays):
+    return lax.optimization_barrier(arrays)
+
+
+def plane_body(queries, key_rows, values, offset, tokens, routes, gate_share, expert_gate, expert_down):
+    expert_total = lax.axis_size("ctx") * lax.axis_size("ep")
+    z = lax.axis_index("ctx")
+    middle = (z == 1) | (z == 2)
+    own_expert = z * lax.axis_size("ep") + lax.axis_index("ep")
+    ids = jnp.stack([own_expert, own_expert ^ 1]).astype(jnp.int32)
+    span, heads, head_size = key_rows.shape
+    query_rows = queries.shape[0]
+    places = [z, z ^ 1, z ^ 2, z ^ 3]
+    positions = jnp.stack([p * span for p in places] + [offset[0] + z * query_rows])
+    gate_a, down_a = expert_gate[0], expert_down[0]
+    gate_b = lax.ppermute(gate_a, "ep", SIBLING)
+    down_b = lax.ppermute(down_a, "ep", SIBLING)
+
+    def run(*blocks):
+        return experts(ids, blocks, gate_a, gate_b, down_a, down_b, expert_total)
+
+    own = prepare(tokens, routes, gate_share, expert_total)
+    own_x = across(own)
+    near = along_z(own, NEAR)
+    mid_one = along_z(own, MIDDLE)
+    near, mid_one, own_x, gate_b, down_b = together(near, mid_one, own_x, gate_b, down_b)
+
+    near_x = across(near)
+    mid_two = along_z(near, MIDDLE)
+    end_one = along_z(mid_one, OUTWARD)
+    part_own, part_own_x, part_near = run(own, own_x, near)
+    second = jnp.where(middle, mid_one, end_one)
+    second, mid_two, near_x, part_own, part_own_x, part_near = together(
+        second, mid_two, near_x, part_own, part_own_x, part_near
+    )
+
+    second_x = across(second)
+    end_two = along_z(mid_two, OUTWARD)
+    part_near_x, part_second = run(near_x, second)
+    third = jnp.where(middle, mid_two, end_two)
+    keys = jnp.concatenate([key_rows.reshape(span, -1), values.reshape(span, -1)], axis=1)
+    flat = queries.reshape(query_rows, -1)
+    third, second_x, part_near_x, part_second, keys, flat = together(
+        third, second_x, part_near_x, part_second, keys, flat
+    )
+
+    third_x = across(third)
+    pieces = [keys] + [along_z(keys, [(i, i ^ j) for i in range(4)]) for j in (1, 2, 3)]
+    part_second_x, part_third = run(second_x, third)
+    third_x, part_second_x, part_third, *pieces = together(
+        third_x, part_second_x, part_third, *pieces
+    )
+    (part_third_x,) = run(third_x)
+
+    back_third = across(part_third_x)
+    attended = attention_pieces(flat, pieces, positions, heads, head_size).reshape(queries.shape)
+    back_third, attended = together(back_third, attended)
+    sum_third = added(part_third, back_third)
+    back_two = along_z(sum_third, INWARD)
+    sum_second = added(part_second, across(part_second_x))
+    back_mid_two = along_z(added(sum_third, back_two), MIDDLE)
+    back_one = along_z(sum_second, INWARD)
+    sum_near = added(part_near, across(part_near_x), back_mid_two)
+    back_mid_one = along_z(added(sum_second, back_one), MIDDLE)
+    back_near = along_z(sum_near, NEAR)
+    mixture = added(part_own, across(part_own_x), back_mid_one, back_near)
+    return (attended, mixture)
+
+
 def solution(mesh):
+    plane = dict(mesh.shape)
+    plane = plane["ctx"] == 4 and plane["ep"] == 4 and plane["tp"] == 1
     return jax.shard_map(
-        body,
+        plane_body if plane else body,
         mesh=mesh,
         in_specs=(
             P(("rep", "ctx"), "tp", "ep", None),

time: 331 us -> 130 us (0.39)
  blocking collectives: 138 us -> 0 us
  Pallas kernels: 0 us -> 28.6 us
  local copies, waits for them, and re-layouts: 36.1 us -> 8.9 us
  waiting for transfers between devices: 78 us -> 53.3 us
  matrix products: 23.3 us -> 0 us
  other arithmetic: 17.8 us -> 2.1 us
    all_gather x2 -> x0, blocking collectives: 138 us -> none  [the longest x1 123 us: attention_shard(): key_piece = lax.all_gather(key_rows, 'ctx', axis=0, tiled=True)]
    all_to_all x3 -> x0, waiting for transfers between devices: 78 us -> none  [the longest x1 76.7 us: body(): lax.all_to_all(outgoing, ('ctx', 'ep'), split_axis=0, concat_axis=0, tile...]
    ppermute x0 -> x23, waiting for transfers between devices: none -> 53.3 us  [the longest x13 29.6 us: along_z(): return lax.ppermute(array, 'ctx', pairs)]
    all_to_all x3 -> x0, starting transfers between devices: 36.1 us -> none  [the longest x1 24 us: body(): lax.all_to_all(computed, ('ctx', 'ep'), split_axis=0, concat_axis=0, tile...]
    ppermute x0 -> x23, starting transfers between devices: none -> 34.4 us  [the longest x13 24.3 us: along_z(): return lax.ppermute(array, 'ctx', pairs)]
    pallas_call x0 -> x6, Pallas kernels: none -> 28.6 us  [the longest x4 23.5 us: experts(): pl.pallas_call(functools.partial(experts_kernel, count=count, expert_tota...]
    dot_general x6 -> x0, matrix products: 23.3 us -> none  [the longest x1 15.5 us: expert_pass(): jnp.einsum('sfch,fhd->sfcd', hidden, expert_down, preferred_element_type=...]
    mul x4 -> x0, local copies, waits for them, and re-layouts: 18.4 us -> none  [the longest x2 18.2 us: expert_pass(): coded_in.astype(jnp.float32)]
  transfers between devices with their start and end apart: 3 -> 23, of which waited for: 2 -> 10; matrix products, arithmetic and copies ran while one was open for 8% -> 4% of each run, Pallas kernels for 0% -> 18%
where the time goes in v2:
time: 130 us; the launch traced here: 129 us
  waiting for transfers between devices  53.3 us (41%)
  starting transfers between devices  34.4 us (26%)
  Pallas kernels  28.6 us (22%)
  local copies, waits for them, and re-layouts  8.9 us (7%)
  other arithmetic  2.1 us (2%)
  between operations  1.73 us (1%)
    ppermute x13, waiting for transfers between devices, along_z(): return lax.ppermute(array, 'ctx', pairs)  29.6 us
    ppermute x13, starting transfers between devices, along_z(): return lax.ppermute(array, 'ctx', pairs)  24.3 us
    ppermute x8, waiting for transfers between devices, across(): return lax.ppermute(array, 'ep', ACROSS)  23.7 us
    pallas_call x4, Pallas kernels, experts(): pl.pallas_call(functools.partial(experts_kernel, count=count, expert_tota...  23.5 us
    ppermute x8, starting transfers between devices, across(): return lax.ppermute(array, 'ep', ACROSS)  9.45 us
    unnamed x48, local copies, waits for them, and re-layouts  4.91 us
    pallas_call x1, Pallas kernels, attention_pieces(): pl.pallas_call(functools.partial(attention_kernel, heads=heads, head_size...  2.74 us
  transfers between devices with their start and end apart: 23, of which 10 were waited for; matrix products, arithmetic and copies ran while one was open for 4% of the time, Pallas kernels for 18%

profile of v2, /device:TPU:0, one launch (start us, length us, event | category | flops | bytes accessed | tf_op | source)
XLA Modules:
  0.0 129.0 jit_solution(13918180352305059646)
XLA Ops:
  1.2 2.4 %shard_map.104.refs_0_ = bf16[128,2176]{1,0:T(8,128)(2,1)} custom-call(bf16[128,2048]{1,0:T(8,128)(2,1)} %tokens_ref.1, s32[8,128]{1,0:T(8,128)} %bitcast.31, f32[8,128]{1,0:T(8,128)} %bitcast.32), custom_call_target="tpu_custom_call" | custom-call | tf_op jit(solution)/shard_map/pallas_call | solution.py:158
  3.6 3.0 %collective-permute-start = (bf16[128,2176]{1,0:T(8,128)(2,1)}, bf16[128,2176]{1,0:T(8,128)(2,1)}, u32[]{:S(2)}, u32[]{:S(2)}) collective-permute-start(bf16[128,2176]{1,0:T(8,128)(2,1)} %shard_map.104.refs_0_), channel_id=1, source_target_pairs={{0,4},{4,0},{8,12},{12,8},{1,5},{5,1},{9,13},{13,9},{2,6},{6,2},{1... | collective-permute-start | bytes 1671176 | tf_op jit(solution)/shard_map/ppermute | solution.py:293
  11.2 8.6 %collective-permute-done.refs_2_ = bf16[128,2176]{1,0:T(8,128)(2,1)} collective-permute-done((bf16[128,2176]{1,0:T(8,128)(2,1)}, bf16[128,2176]{1,0:T(8,128)(2,1)}, u32[]{:S(2)}, u32[]{:S(2)}) %collective-permute-start) | collective-permute-done | bytes 557088 | tf_op jit(solution)/shard_map/ppermute | solution.py:293
  19.8 2.9 %collective-permute-done.2.refs_1_ = bf16[128,2176]{1,0:T(8,128)(2,1)} collective-permute-done((bf16[128,2176]{1,0:T(8,128)(2,1)}, bf16[128,2176]{1,0:T(8,128)(2,1)}, u32[]{:S(2)}, u32[]{:S(2)}) %collective-permute-start.2) | collective-permute-done | bytes 557088 | tf_op jit(solution)/shard_map/ppermute | solution.py:297
  26.3 1.9 %copy-done = bf16[1,2048,768]{2,1,0:T(8,128)(2,1)S(1)} copy-done((bf16[1,2048,768]{2,1,0:T(8,128)(2,1)S(1)}, bf16[1,2048,768]{2,1,0:T(8,128)(2,1)}, u32[]{:S(2)}) %copy-start) | copy-done | bytes 3145752
  28.2 1.9 %copy-done.2 = bf16[1,768,2048]{2,1,0:T(8,128)(2,1)S(1)} copy-done((bf16[1,768,2048]{2,1,0:T(8,128)(2,1)S(1)}, bf16[1,768,2048]{2,1,0:T(8,128)(2,1)}, u32[]{:S(2)}) %copy-start.2) | copy-done | bytes 3145752
  31.2 7.7 %shard_map.105 = (bf16[128,2048]{1,0:T(8,128)(2,1)S(1)}, bf16[128,2048]{1,0:T(8,128)(2,1)S(1)}, bf16[128,2048]{1,0:T(8,128)(2,1)S(1)}) custom-call(s32[2]{0:T(128)S(1)} %pad_add_fusion.ids_ref, bf16[128,2176]{1,0:T(8,128)(2,1)S(1)} %copy-done.4, bf16[128,2176]{1,0:T(8,128)(2,1)} %collective-permute-done.2.refs_1_, ...), custom_call_target="tpu_custom_call" | custom-call | flops 4831838208 | bytes 12582912 | tf_op jit(solution)/shard_map/pallas_call | solution.py:205
  42.2 5.5 %shard_map.106 = (bf16[128,2048]{1,0:T(8,128)(2,1)S(1)}, bf16[128,2048]{1,0:T(8,128)(2,1)S(1)}) custom-call(s32[2]{0:T(128)S(1)} %pad_add_fusion.ids_ref, bf16[128,2176]{1,0:T(8,128)(2,1)S(1)} %collective-permute-done.7.refs_0_, bf16[128,2176]{1,0:T(8,128)(2,1)S(1)} %broadcast_select_fusion.1.refs_1_, bf16[2048,768]{1,0:T(8,128)(2,1)S(1)} %bitcast.21, ...), custom_call_target="tpu_custom_call" | custom-call | flops 3221225472 | bytes 12582912 | tf_op jit(solution)/shard_map/pallas_call | solution.py:205
  47.7 10.4 %collective-permute-done.8 = bf16[128,2176]{1,0:T(8,128)(2,1)S(1)} collective-permute-done((bf16[128,2176]{1,0:T(8,128)(2,1)S(1)}, bf16[128,2176]{1,0:T(8,128)(2,1)S(1)}, u32[]{:S(2)}, u32[]{:S(2)}) %collective-permute-start.8) | collective-permute-done | bytes 557088 | tf_op jit(solution)/shard_map/ppermute | solution.py:293
  58.8 2.1 %collective-permute-start.11 = (bf16[128,512]{1,0:T(8,128)(2,1)S(1)}, bf16[128,512]{1,0:T(8,128)(2,1)S(1)}, u32[]{:S(2)}, u32[]{:S(2)}) collective-permute-start(bf16[128,512]{1,0:T(8,128)(2,1)S(1)} %pad_maximum_fusion.refs_0_), channel_id=1, source_target_pairs={{0,4},{4,0},{8,12},{12,8},{1,5},{5,1},{9,13},{13,9},{2,6},{6,2},{1... | collective-permute-start | bytes 393224 | tf_op jit(solution)/shard_map/ppermute | solution.py:293
  61.6 1.8 %collective-permute-start.13 = (bf16[128,512]{1,0:T(8,128)(2,1)S(1)}, bf16[128,512]{1,0:T(8,128)(2,1)S(1)}, u32[]{:S(2)}, u32[]{:S(2)}) collective-permute-start(bf16[128,512]{1,0:T(8,128)(2,1)S(1)} %pad_maximum_fusion.refs_0_), channel_id=1, source_target_pairs={{0,12},{4,8},{8,4},{12,0},{1,13},{5,9},{9,5},{13,1},{2,14},{6,10},... | collective-permute-start | bytes 393224 | tf_op jit(solution)/shard_map/ppermute | solution.py:293
  63.3 5.5 %shard_map.107 = (bf16[128,2048]{1,0:T(8,128)(2,1)S(1)}, bf16[128,2048]{1,0:T(8,128)(2,1)S(1)}) custom-call(s32[2]{0:T(128)S(1)} %pad_add_fusion.ids_ref, bf16[128,2176]{1,0:T(8,128)(2,1)S(1)} %collective-permute-done.9.refs_0_, bf16[128,2176]{1,0:T(8,128)(2,1)S(1)} %broadcast_select_fusion.refs_1_, bf16[2048,768]{1,0:T(8,128)(2,1)S(1)} %bitcast.22, ...), custom_call_target="tpu_custom_call" | custom-call | flops 3221225472 | bytes 12582912 | tf_op jit(solution)/shard_map/pallas_call | solution.py:205
  68.9 1.9 %collective-permute-done.12.refs_2_ = bf16[128,512]{1,0:T(8,128)(2,1)S(1)} collective-permute-done((bf16[128,512]{1,0:T(8,128)(2,1)S(1)}, bf16[128,512]{1,0:T(8,128)(2,1)S(1)}, u32[]{:S(2)}, u32[]{:S(2)}) %collective-permute-start.12) | collective-permute-done | bytes 131104 | tf_op jit(solution)/shard_map/ppermute | solution.py:293
  70.8 4.8 %shard_map.108 = bf16[128,2048]{1,0:T(8,128)(2,1)} custom-call(s32[2]{0:T(128)S(1)} %pad_add_fusion.ids_ref, bf16[128,2176]{1,0:T(8,128)(2,1)S(1)} %collective-permute-done.10.refs_0_, bf16[2048,768]{1,0:T(8,128)(2,1)S(1)} %bitcast.23, bf16[2048,768]{1,0:T(8,128)(2,1)S(1)} %collective-permute-done.3.refs_4_.refs_3_.refs_2_, bf16[768,2048]{1,0:T(8,128)(2,1)S(1)} %bitcast.28, ...), custom_call_target="tpu_custom_call" | custom-call | flops 1610612736 | bytes 12582912 | tf_op jit(solution)/shard_map/pallas_call | solution.py:205
  79.1 2.7 %shard_map.109 = bf16[64,1024]{1,0:T(8,128)(2,1)} custom-call(s32[5]{0:T(128)} %stack.35.where_ref, bf16[64,1024]{1,0:T(8,128)(2,1)} %reshape.18.queries_ref, bf16[128,512]{1,0:T(8,128)(2,1)} %copy-done.18, bf16[128,512]{1,0:T(8,128)(2,1)} %copy-done.21, bf16[128,512]{1,0:T(8,128)(2,1)} %copy-done.22, bf16[128,512]{1,0:T(8,128)(2,1)} %copy-done.23), custom_call_target="tpu_custom_call" | custom-call | flops 1000000000 | bytes 4000000 | tf_op jit(solution)/shard_map/pallas_call | solution.py:273
  81.8 1.7 %reshape.19 = bf16[64,2,4,128]{3,2,1,0:T(4,128)(2,1)} reshape(bf16[64,1024]{1,0:T(8,128)(2,1)} %shard_map.109) | data formatting | bytes 262144 | tf_op jit(solution)/shard_map/reshape | solution.py:359
  83.5 7.2 %collective-permute-done.14 = bf16[128,2048]{1,0:T(8,128)(2,1)S(1)} collective-permute-done((bf16[128,2048]{1,0:T(8,128)(2,1)}, bf16[128,2048]{1,0:T(8,128)(2,1)S(1)}, u32[]{:S(2)}, u32[]{:S(2)}) %collective-permute-start.14) | collective-permute-done | bytes 524320 | tf_op jit(solution)/shard_map/ppermute | solution.py:297
  90.9 4.0 %collective-permute-start.20 = (bf16[128,2048]{1,0:T(8,128)(2,1)S(1)}, bf16[128,2048]{1,0:T(8,128)(2,1)S(1)}, u32[]{:S(2)}, u32[]{:S(2)}) collective-permute-start(bf16[128,2048]{1,0:T(8,128)(2,1)S(1)} %add_convert_fusion.3), channel_id=1, source_target_pairs={{0,4},{12,8},{1,5},{13,9},{2,6},{14,10},{3,7},{15,11},{16,20},{28,... | collective-permute-start | bytes 1572872 | tf_op jit(solution)/shard_map/ppermute | solution.py:293
  94.9 2.0 %collective-permute-done.16 = bf16[128,2048]{1,0:T(8,128)(2,1)S(1)} collective-permute-done((bf16[128,2048]{1,0:T(8,128)(2,1)}, bf16[128,2048]{1,0:T(8,128)(2,1)S(1)}, u32[]{:S(2)}, u32[]{:S(2)}) %collective-permute-start.16) | collective-permute-done | bytes 524320 | tf_op jit(solution)/shard_map/ppermute | solution.py:297
  97.0 6.3 %collective-permute-start.17 = (bf16[128,2048]{1,0:T(8,128)(2,1)S(1)}, bf16[128,2048]{1,0:T(8,128)(2,1)S(1)}, u32[]{:S(2)}, u32[]{:S(2)}) collective-permute-start(bf16[128,2048]{1,0:T(8,128)(2,1)S(1)} %add_convert_fusion.5), channel_id=1, source_target_pairs={{0,4},{12,8},{1,5},{13,9},{2,6},{14,10},{3,7},{15,11},{16,20},{28,... | collective-permute-start | bytes 1572872 | tf_op jit(solution)/shard_map/ppermute | solution.py:293
  106.3 6.4 %collective-permute-done.17 = bf16[128,2048]{1,0:T(8,128)(2,1)S(1)} collective-permute-done((bf16[128,2048]{1,0:T(8,128)(2,1)S(1)}, bf16[128,2048]{1,0:T(8,128)(2,1)S(1)}, u32[]{:S(2)}, u32[]{:S(2)}) %collective-permute-start.17) | collective-permute-done | bytes 524320 | tf_op jit(solution)/shard_map/ppermute | solution.py:293
  113.6 4.6 %collective-permute-done.19 = bf16[128,2048]{1,0:T(8,128)(2,1)S(1)} collective-permute-done((bf16[128,2048]{1,0:T(8,128)(2,1)S(1)}, bf16[128,2048]{1,0:T(8,128)(2,1)S(1)}, u32[]{:S(2)}, u32[]{:S(2)}) %collective-permute-start.19) | collective-permute-done | bytes 524320 | tf_op jit(solution)/shard_map/ppermute | solution.py:297
  118.8 6.9 %collective-permute-done.15 = bf16[128,2048]{1,0:T(8,128)(2,1)S(1)} collective-permute-done((bf16[128,2048]{1,0:T(8,128)(2,1)S(1)}, bf16[128,2048]{1,0:T(8,128)(2,1)S(1)}, u32[]{:S(2)}, u32[]{:S(2)}) %collective-permute-start.15) | collective-permute-done | bytes 524320 | tf_op jit(solution)/shard_map/ppermute | solution.py:297
  125.6 2.2 %collective-permute-done.22 = bf16[128,2048]{1,0:T(8,128)(2,1)S(1)} collective-permute-done((bf16[128,2048]{1,0:T(8,128)(2,1)S(1)}, bf16[128,2048]{1,0:T(8,128)(2,1)S(1)}, u32[]{:S(2)}, u32[]{:S(2)}) %collective-permute-start.22) | collective-permute-done | bytes 524320 | tf_op jit(solution)/shard_map/ppermute | solution.py:293
  (90 shorter events, 22.8 us)
Async XLA Ops:
  0.6 22.1 %collective-permute-start.3 = (bf16[2048,768]{1,0:T(8,128)(2,1)}, bf16[2048,768]{1,0:T(8,128)(2,1)S(1)}, u32[]{:S(2)}, u32[]{:S(2)}) collective-permute-start(bf16[2048,768]{1,0:T(8,128)(2,1)} %bitcast.19), channel_id=1, source_target_pairs={{0,1},{1,0},{2,3},{3,2},{4,5},{5,4},{6,7},{7,6},{8,9},{9,8},{10,11... | collective-permute-start | bytes 9437192 | tf_op jit(solution)/shard_map/ppermute | solution.py:319
  1.1 21.6 %collective-permute-start.4 = (bf16[768,2048]{1,0:T(8,128)(2,1)}, bf16[768,2048]{1,0:T(8,128)(2,1)}, u32[]{:S(2)}, u32[]{:S(2)}) collective-permute-start(bf16[768,2048]{1,0:T(8,128)(2,1)} %bitcast.24), channel_id=1, source_target_pairs={{0,1},{1,0},{2,3},{3,2},{4,5},{5,4},{6,7},{7,6},{8,9},{9,8},{10,11... | collective-permute-start | bytes 9437192 | tf_op jit(solution)/shard_map/ppermute | solution.py:320
  3.6 16.2 %collective-permute-start = (bf16[128,2176]{1,0:T(8,128)(2,1)}, bf16[128,2176]{1,0:T(8,128)(2,1)}, u32[]{:S(2)}, u32[]{:S(2)}) collective-permute-start(bf16[128,2176]{1,0:T(8,128)(2,1)} %shard_map.104.refs_0_), channel_id=1, source_target_pairs={{0,4},{4,0},{8,12},{12,8},{1,5},{5,1},{9,13},{13,9},{2,6},{6,2},{1... | collective-permute-start | bytes 1671176 | tf_op jit(solution)/shard_map/ppermute | solution.py:293
  6.6 13.2 %collective-permute-start.1 = (bf16[128,2176]{1,0:T(8,128)(2,1)}, bf16[128,2176]{1,0:T(8,128)(2,1)}, u32[]{:S(2)}, u32[]{:S(2)}) collective-permute-start(bf16[128,2176]{1,0:T(8,128)(2,1)} %shard_map.104.refs_0_), channel_id=1, source_target_pairs={{4,8},{8,4},{5,9},{9,5},{6,10},{10,6},{7,11},{11,7},{20,24},{24,20... | collective-permute-start | bytes 1671176 | tf_op jit(solution)/shard_map/ppermute | solution.py:293
  8.1 14.6 %collective-permute-start.2 = (bf16[128,2176]{1,0:T(8,128)(2,1)}, bf16[128,2176]{1,0:T(8,128)(2,1)}, u32[]{:S(2)}, u32[]{:S(2)}) collective-permute-start(bf16[128,2176]{1,0:T(8,128)(2,1)} %shard_map.104.refs_0_), channel_id=1, source_target_pairs={{0,2},{1,3},{2,0},{3,1},{4,6},{5,7},{6,4},{7,5},{8,10},{9,11},{10,... | collective-permute-start | bytes 1671176 | tf_op jit(solution)/shard_map/ppermute | solution.py:297
  22.7 16.2 %collective-permute-start.5 = (bf16[128,2176]{1,0:T(8,128)(2,1)}, bf16[128,2176]{1,0:T(8,128)(2,1)S(1)}, u32[]{:S(2)}, u32[]{:S(2)}) collective-permute-start(bf16[128,2176]{1,0:T(8,128)(2,1)} %collective-permute-done.1), channel_id=1, source_target_pairs={{4,0},{8,12},{5,1},{9,13},{6,2},{10,14},{7,3},{11,15},{20,16},{24,... | collective-permute-start | bytes 1671176 | tf_op jit(solution)/shard_map/ppermute | solution.py:293
  24.1 15.0 %collective-permute-start.6 = (bf16[128,2176]{1,0:T(8,128)(2,1)}, bf16[128,2176]{1,0:T(8,128)(2,1)S(1)}, u32[]{:S(2)}, u32[]{:S(2)}) collective-permute-start(bf16[128,2176]{1,0:T(8,128)(2,1)} %collective-permute-done.refs_2_), channel_id=1, source_target_pairs={{4,8},{8,4},{5,9},{9,5},{6,10},{10,6},{7,11},{11,7},{20,24},{24,20... | collective-permute-start | bytes 1671176 | tf_op jit(solution)/shard_map/ppermute | solution.py:293
  24.8 14.3 %collective-permute-start.7 = (bf16[128,2176]{1,0:T(8,128)(2,1)}, bf16[128,2176]{1,0:T(8,128)(2,1)S(1)}, u32[]{:S(2)}, u32[]{:S(2)}) collective-permute-start(bf16[128,2176]{1,0:T(8,128)(2,1)} %collective-permute-done.refs_2_), channel_id=1, source_target_pairs={{0,2},{1,3},{2,0},{3,1},{4,6},{5,7},{6,4},{7,5},{8,10},{9,11},{10,... | collective-permute-start | bytes 1671176 | tf_op jit(solution)/shard_map/ppermute | solution.py:297
  39.1 19.1 %collective-permute-start.8 = (bf16[128,2176]{1,0:T(8,128)(2,1)S(1)}, bf16[128,2176]{1,0:T(8,128)(2,1)S(1)}, u32[]{:S(2)}, u32[]{:S(2)}) collective-permute-start(bf16[128,2176]{1,0:T(8,128)(2,1)S(1)} %collective-permute-done.6), channel_id=1, source_target_pairs={{4,0},{8,12},{5,1},{9,13},{6,2},{10,14},{7,3},{11,15},{20,16},{24,... | collective-permute-start | bytes 1671176 | tf_op jit(solution)/shard_map/ppermute | solution.py:293
  40.6 17.6 %collective-permute-start.9 = (bf16[128,2176]{1,0:T(8,128)(2,1)S(1)}, bf16[128,2176]{1,0:T(8,128)(2,1)S(1)}, u32[]{:S(2)}, u32[]{:S(2)}) collective-permute-start(bf16[128,2176]{1,0:T(8,128)(2,1)S(1)} %broadcast_select_fusion.1.refs_1_), channel_id=1, source_target_pairs={{0,2},{1,3},{2,0},{3,1},{4,6},{5,7},{6,4},{7,5},{8,10},{9,11},{10,... | collective-permute-start | bytes 1671176 | tf_op jit(solution)/shard_map/ppermute | solution.py:297
  58.2 12.6 %collective-permute-start.10 = (bf16[128,2176]{1,0:T(8,128)(2,1)S(1)}, bf16[128,2176]{1,0:T(8,128)(2,1)S(1)}, u32[]{:S(2)}, u32[]{:S(2)}) collective-permute-start(bf16[128,2176]{1,0:T(8,128)(2,1)S(1)} %broadcast_select_fusion.refs_1_), channel_id=1, source_target_pairs={{0,2},{1,3},{2,0},{3,1},{4,6},{5,7},{6,4},{7,5},{8,10},{9,11},{10,... | collective-permute-start | bytes 1671176 | tf_op jit(solution)/shard_map/ppermute | solution.py:297
  58.8 10.0 %collective-permute-start.11 = (bf16[128,512]{1,0:T(8,128)(2,1)S(1)}, bf16[128,512]{1,0:T(8,128)(2,1)S(1)}, u32[]{:S(2)}, u32[]{:S(2)}) collective-permute-start(bf16[128,512]{1,0:T(8,128)(2,1)S(1)} %pad_maximum_fusion.refs_0_), channel_id=1, source_target_pairs={{0,4},{4,0},{8,12},{12,8},{1,5},{5,1},{9,13},{13,9},{2,6},{6,2},{1... | collective-permute-start | bytes 393224 | tf_op jit(solution)/shard_map/ppermute | solution.py:293
  60.9 9.8 %collective-permute-start.12 = (bf16[128,512]{1,0:T(8,128)(2,1)S(1)}, bf16[128,512]{1,0:T(8,128)(2,1)S(1)}, u32[]{:S(2)}, u32[]{:S(2)}) collective-permute-start(bf16[128,512]{1,0:T(8,128)(2,1)S(1)} %pad_maximum_fusion.refs_0_), channel_id=1, source_target_pairs={{0,8},{4,12},{8,0},{12,4},{1,9},{5,13},{9,1},{13,5},{2,10},{6,14},... | collective-permute-start | bytes 393224 | tf_op jit(solution)/shard_map/ppermute | solution.py:293
  61.6 9.2 %collective-permute-start.13 = (bf16[128,512]{1,0:T(8,128)(2,1)S(1)}, bf16[128,512]{1,0:T(8,128)(2,1)S(1)}, u32[]{:S(2)}, u32[]{:S(2)}) collective-permute-start(bf16[128,512]{1,0:T(8,128)(2,1)S(1)} %pad_maximum_fusion.refs_0_), channel_id=1, source_target_pairs={{0,12},{4,8},{8,4},{12,0},{1,13},{5,9},{9,5},{13,1},{2,14},{6,10},... | collective-permute-start | bytes 393224 | tf_op jit(solution)/shard_map/ppermute | solution.py:293
  75.6 15.1 %collective-permute-start.14 = (bf16[128,2048]{1,0:T(8,128)(2,1)}, bf16[128,2048]{1,0:T(8,128)(2,1)S(1)}, u32[]{:S(2)}, u32[]{:S(2)}) collective-permute-start(bf16[128,2048]{1,0:T(8,128)(2,1)} %shard_map.108), channel_id=1, source_target_pairs={{0,2},{1,3},{2,0},{3,1},{4,6},{5,7},{6,4},{7,5},{8,10},{9,11},{10,... | collective-permute-start | bytes 1572872 | tf_op jit(solution)/shard_map/ppermute | solution.py:297
  78.6 18.3 %collective-permute-start.16 = (bf16[128,2048]{1,0:T(8,128)(2,1)}, bf16[128,2048]{1,0:T(8,128)(2,1)S(1)}, u32[]{:S(2)}, u32[]{:S(2)}) collective-permute-start(bf16[128,2048]{1,0:T(8,128)(2,1)} %copy-done.17), channel_id=1, source_target_pairs={{0,2},{1,3},{2,0},{3,1},{4,6},{5,7},{6,4},{7,5},{8,10},{9,11},{10,... | collective-permute-start | bytes 1572872 | tf_op jit(solution)/shard_map/ppermute | solution.py:297
  90.9 37.0 %copy-start.6 = (bf16[128,2048]{1,0:T(8,128)(2,1)S(1)}, bf16[128,2048]{1,0:T(8,128)(2,1)}, u32[]{:S(2)}) copy-start(bf16[128,2048]{1,0:T(8,128)(2,1)} %copy-done.5) | copy-start | bytes 1572868
  90.9 14.0 %collective-permute-start.20 = (bf16[128,2048]{1,0:T(8,128)(2,1)S(1)}, bf16[128,2048]{1,0:T(8,128)(2,1)S(1)}, u32[]{:S(2)}, u32[]{:S(2)}) collective-permute-start(bf16[128,2048]{1,0:T(8,128)(2,1)S(1)} %add_convert_fusion.3), channel_id=1, source_target_pairs={{0,4},{12,8},{1,5},{13,9},{2,6},{14,10},{3,7},{15,11},{16,20},{28,... | collective-permute-start | bytes 1572872 | tf_op jit(solution)/shard_map/ppermute | solution.py:293
  97.0 15.8 %collective-permute-start.17 = (bf16[128,2048]{1,0:T(8,128)(2,1)S(1)}, bf16[128,2048]{1,0:T(8,128)(2,1)S(1)}, u32[]{:S(2)}, u32[]{:S(2)}) collective-permute-start(bf16[128,2048]{1,0:T(8,128)(2,1)S(1)} %add_convert_fusion.5), channel_id=1, source_target_pairs={{0,4},{12,8},{1,5},{13,9},{2,6},{14,10},{3,7},{15,11},{16,20},{28,... | collective-permute-start | bytes 1572872 | tf_op jit(solution)/shard_map/ppermute | solution.py:293
  103.3 14.9 %collective-permute-start.19 = (bf16[128,2048]{1,0:T(8,128)(2,1)S(1)}, bf16[128,2048]{1,0:T(8,128)(2,1)S(1)}, u32[]{:S(2)}, u32[]{:S(2)}) collective-permute-start(bf16[128,2048]{1,0:T(8,128)(2,1)S(1)} %copy-done.16), channel_id=1, source_target_pairs={{0,2},{1,3},{2,0},{3,1},{4,6},{5,7},{6,4},{7,5},{8,10},{9,11},{10,... | collective-permute-start | bytes 1572872 | tf_op jit(solution)/shard_map/ppermute | solution.py:297
  105.0 13.2 %collective-permute-start.21 = (bf16[128,2048]{1,0:T(8,128)(2,1)S(1)}, bf16[128,2048]{1,0:T(8,128)(2,1)S(1)}, u32[]{:S(2)}, u32[]{:S(2)}) collective-permute-start(bf16[128,2048]{1,0:T(8,128)(2,1)S(1)} %add_convert_fusion.2), channel_id=1, source_target_pairs={{4,8},{8,4},{5,9},{9,5},{6,10},{10,6},{7,11},{11,7},{20,24},{24,20... | collective-permute-start | bytes 1572872 | tf_op jit(solution)/shard_map/ppermute | solution.py:293
  105.8 19.9 %collective-permute-start.15 = (bf16[128,2048]{1,0:T(8,128)(2,1)S(1)}, bf16[128,2048]{1,0:T(8,128)(2,1)S(1)}, u32[]{:S(2)}, u32[]{:S(2)}) collective-permute-start(bf16[128,2048]{1,0:T(8,128)(2,1)S(1)} %copy-done.14), channel_id=1, source_target_pairs={{0,2},{1,3},{2,0},{3,1},{4,6},{5,7},{6,4},{7,5},{8,10},{9,11},{10,... | collective-permute-start | bytes 1572872 | tf_op jit(solution)/shard_map/ppermute | solution.py:297
  112.9 12.7 %collective-permute-start.18 = (bf16[128,2048]{1,0:T(8,128)(2,1)S(1)}, bf16[128,2048]{1,0:T(8,128)(2,1)S(1)}, u32[]{:S(2)}, u32[]{:S(2)}) collective-permute-start(bf16[128,2048]{1,0:T(8,128)(2,1)S(1)} %add_convert_fusion.4), channel_id=1, source_target_pairs={{4,8},{8,4},{5,9},{9,5},{6,10},{10,6},{7,11},{11,7},{20,24},{24,20... | collective-permute-start | bytes 1572872 | tf_op jit(solution)/shard_map/ppermute | solution.py:293
  118.5 9.4 %collective-permute-start.22 = (bf16[128,2048]{1,0:T(8,128)(2,1)S(1)}, bf16[128,2048]{1,0:T(8,128)(2,1)S(1)}, u32[]{:S(2)}, u32[]{:S(2)}) collective-permute-start(bf16[128,2048]{1,0:T(8,128)(2,1)S(1)} %add_convert_fusion.1), channel_id=1, source_target_pairs={{0,4},{4,0},{8,12},{12,8},{1,5},{5,1},{9,13},{13,9},{2,6},{6,2},{1... | collective-permute-start | bytes 1572872 | tf_op jit(solution)/shard_map/ppermute | solution.py:293
  (23 other events, 265.6 us)

commit v3 on v2

--- a/solution.py
+++ b/solution.py
@@ -219,6 +219,26 @@
             transcendentals=0,
         ),
     )(ids, *blocks, gate_a, gate_b, down_a, down_b)
+
+
+def hold_kernel(*refs):
+    sources, kept, done = refs[:4], refs[4:8], refs[8]
+    copies = [pltpu.make_async_copy(sources[i], kept[i], done.at[i]) for i in range(4)]
+    for copy in copies:
+        copy.start()
+    for copy in copies:
+        copy.wait()
+
+
+def hold(*arrays):
+    return pl.pallas_call(
+        hold_kernel,
+        in_specs=[pl.BlockSpec(memory_space=pltpu.HBM)] * 4,
+        out_specs=[pl.BlockSpec(memory_space=pltpu.VMEM)] * 4,
+        out_shape=[jax.ShapeDtypeStruct(array.shape, array.dtype) for array in arrays],
+        scratch_shapes=[pltpu.SemaphoreType.DMA((4,))],
+        compiler_params=pltpu.CompilerParams(vmem_limit_bytes=16 * 1024 * 1024),
+    )(*arrays)
 
 
 def attention_kernel(where_ref, queries_ref, *refs, heads, head_size):
@@ -323,18 +343,21 @@
         return experts(ids, blocks, gate_a, gate_b, down_a, down_b, expert_total)
 
     own = prepare(tokens, routes, gate_share, expert_total)
-    own_x = across(own)
     near = along_z(own, NEAR)
     mid_one = along_z(own, MIDDLE)
-    near, mid_one, own_x, gate_b, down_b = together(near, mid_one, own_x, gate_b, down_b)
-
-    near_x = across(near)
+    own_x = across(own)
+    gate_a, gate_b, down_a, down_b = hold(gate_a, gate_b, down_a, down_b)
+    near, mid_one, gate_a, gate_b, down_a, down_b = together(
+        near, mid_one, gate_a, gate_b, down_a, down_b
+    )
+
     mid_two = along_z(near, MIDDLE)
     end_one = along_z(mid_one, OUTWARD)
+    near_x = across(near)
     part_own, part_own_x, part_near = run(own, own_x, near)
     second = jnp.where(middle, mid_one, end_one)
-    second, mid_two, near_x, part_own, part_own_x, part_near = together(
-        second, mid_two, near_x, part_own, part_own_x, part_near
+    second, mid_two, part_own, part_own_x, part_near = together(
+        second, mid_two, part_own, part_own_x, part_near
     )
 
     second_x = across(second)
@@ -343,8 +366,8 @@
     third = jnp.where(middle, mid_two, end_two)
     keys = jnp.concatenate([key_rows.reshape(span, -1), values.reshape(span, -1)], axis=1)
     flat = queries.reshape(query_rows, -1)
-    third, second_x, part_near_x, part_second, keys, flat = together(
-        third, second_x, part_near_x, part_second, keys, flat
+    third, part_near_x, part_second, keys, flat = together(
+        third, part_near_x, part_second, keys, flat
     )
 
     third_x = across(third)

time: 130 us -> 124 us (0.954)
  Pallas kernels: 28.6 us -> 25 us
  waiting for transfers between devices: 53.3 us -> 50.5 us
  other arithmetic: 2.1 us -> 4.18 us
    pallas_call x4, Pallas kernels: 23.5 us -> 17.3 us  [experts(): pl.pallas_call(functools.partial(experts_kernel, count=count, expert_tota...]
    ppermute x8, waiting for transfers between devices: 23.7 us -> 21 us  [across(): return lax.ppermute(array, 'ep', ACROSS)]
    pallas_call x0 -> x1, Pallas kernels: none -> 2.55 us  [hold(): pl.pallas_call(hold_kernel, in_specs=[pl.BlockSpec(memory_space=pltpu.HBM...]
    convert_element_type x6, other arithmetic: 1.87 us -> 3.95 us  [added(): sum((term.astype(jnp.float32) for term in terms)).astype(jnp.bfloat16)]
    unnamed x48 -> x24, local copies, waits for them, and re-layouts: 4.91 us -> 3.82 us
  transfers between devices with their start and end apart: 23 -> 23, of which waited for: 10 -> 11; matrix products, arithmetic and copies ran while one was open for 4% -> 6% of each run, Pallas kernels for 18% -> 18%
where the time goes in v3:
time: 124 us
  waiting for transfers between devices  50.5 us (41%)
  starting transfers between devices  34.6 us (28%)
  Pallas kernels  25 us (20%)
  local copies, waits for them, and re-layouts  7.76 us (6%)
  other arithmetic  4.18 us (3%)
  between operations  1.58 us (1%)
    ppermute x13, waiting for transfers between devices, along_z(): return lax.ppermute(array, 'ctx', pairs)  29.4 us
    ppermute x13, starting transfers between devices, along_z(): return lax.ppermute(array, 'ctx', pairs)  23.4 us
    ppermute x8, waiting for transfers between devices, across(): return lax.ppermute(array, 'ep', ACROSS)  21 us
    pallas_call x4, Pallas kernels, experts(): pl.pallas_call(functools.partial(experts_kernel, count=count, expert_tota...  17.3 us
    ppermute x8, starting transfers between devices, across(): return lax.ppermute(array, 'ep', ACROSS)  10.6 us
    convert_element_type x6, other arithmetic, added(): sum((term.astype(jnp.float32) for term in terms)).astype(jnp.bfloat16)  3.95 us
    unnamed x24, local copies, waits for them, and re-layouts  3.82 us
    pallas_call x1, Pallas kernels, attention_pieces(): pl.pallas_call(functools.partial(attention_kernel, heads=heads, head_size...  2.74 us
  transfers between devices with their start and end apart: 23, of which 11 were waited for; matrix products, arithmetic and copies ran while one was open for 6% of the time, Pallas kernels for 18%

profile of v3, /device:TPU:0, one launch (start us, length us, event | category | flops | bytes accessed | tf_op | source)
XLA Modules:
  0.0 123.6 jit_solution(4695510269877070457)
XLA Ops:
  1.2 2.4 %shard_map.104.refs_0_ = bf16[128,2176]{1,0:T(8,128)(2,1)} custom-call(bf16[128,2048]{1,0:T(8,128)(2,1)} %tokens_ref.1, s32[8,128]{1,0:T(8,128)} %bitcast.25, f32[8,128]{1,0:T(8,128)} %bitcast.26), custom_call_target="tpu_custom_call" | custom-call | tf_op jit(solution)/shard_map/pallas_call | solution.py:158
  3.6 3.0 %collective-permute-start = (bf16[128,2176]{1,0:T(8,128)(2,1)}, bf16[128,2176]{1,0:T(8,128)(2,1)}, u32[]{:S(2)}, u32[]{:S(2)}) collective-permute-start(bf16[128,2176]{1,0:T(8,128)(2,1)} %shard_map.104.refs_0_), channel_id=1, source_target_pairs={{0,4},{4,0},{8,12},{12,8},{1,5},{5,1},{9,13},{13,9},{2,6},{6,2},{1... | collective-permute-start | bytes 1671176 | tf_op jit(solution)/shard_map/ppermute | solution.py:313
  11.3 1.9 %copy-done = bf16[1,2048,768]{2,1,0:T(8,128)(2,1)S(1)} copy-done((bf16[1,2048,768]{2,1,0:T(8,128)(2,1)S(1)}, bf16[1,2048,768]{2,1,0:T(8,128)(2,1)}, u32[]{:S(2)}) %copy-start) | copy-done | bytes 3145752
  13.2 1.9 %copy-done.1 = bf16[1,768,2048]{2,1,0:T(8,128)(2,1)S(1)} copy-done((bf16[1,768,2048]{2,1,0:T(8,128)(2,1)S(1)}, bf16[1,768,2048]{2,1,0:T(8,128)(2,1)}, u32[]{:S(2)}) %copy-start.1) | copy-done | bytes 3145752
  15.1 2.6 %shard_map.105 = (bf16[2048,768]{1,0:T(8,128)(2,1)S(1)}, bf16[2048,768]{1,0:T(8,128)(2,1)S(1)}, bf16[768,2048]{1,0:T(8,128)(2,1)S(1)}, bf16[768,2048]{1,0:T(8,128)(2,1)S(1)}) custom-call(bf16[2048,768]{1,0:T(8,128)(2,1)S(1)} %bitcast.20, bf16[2048,768]{1,0:T(8,128)(2,1)S(1)} %collective-permute-done.2.refs_1_, bf16[768,2048]{1,0:T(8,128)(2,1)S(1)} %bitcast.22, ...), custom_call_target="tpu_custom_call" | custom-call | tf_op jit(solution)/shard_map/pallas_call | solution.py:234
  17.6 2.2 %collective-permute-done.refs_2_ = bf16[128,2176]{1,0:T(8,128)(2,1)} collective-permute-done((bf16[128,2176]{1,0:T(8,128)(2,1)}, bf16[128,2176]{1,0:T(8,128)(2,1)}, u32[]{:S(2)}, u32[]{:S(2)}) %collective-permute-start) | collective-permute-done | bytes 557088 | tf_op jit(solution)/shard_map/ppermute | solution.py:313
  23.7 6.5 %shard_map.106 = (bf16[128,2048]{1,0:T(8,128)(2,1)S(1)}, bf16[128,2048]{1,0:T(8,128)(2,1)S(1)}, bf16[128,2048]{1,0:T(8,128)(2,1)S(1)}) custom-call(s32[2]{0:T(128)S(1)} %pad_add_fusion.ids_ref, bf16[128,2176]{1,0:T(8,128)(2,1)S(1)} %copy-done.2, bf16[128,2176]{1,0:T(8,128)(2,1)} %collective-permute-done.6.refs_1_, ...), custom_call_target="tpu_custom_call" | custom-call | flops 4831838208 | bytes 12582912 | tf_op jit(solution)/shard_map/pallas_call | solution.py:205
  30.2 7.8 %collective-permute-done.4 = bf16[128,2176]{1,0:T(8,128)(2,1)S(1)} collective-permute-done((bf16[128,2176]{1,0:T(8,128)(2,1)}, bf16[128,2176]{1,0:T(8,128)(2,1)S(1)}, u32[]{:S(2)}, u32[]{:S(2)}) %collective-permute-start.4) | collective-permute-done | bytes 557088 | tf_op jit(solution)/shard_map/ppermute | solution.py:313
  41.2 4.1 %shard_map.107 = (bf16[128,2048]{1,0:T(8,128)(2,1)S(1)}, bf16[128,2048]{1,0:T(8,128)(2,1)S(1)}) custom-call(s32[2]{0:T(128)S(1)} %pad_add_fusion.ids_ref, bf16[128,2176]{1,0:T(8,128)(2,1)S(1)} %collective-permute-done.8.refs_0_, bf16[128,2176]{1,0:T(8,128)(2,1)S(1)} %broadcast_select_fusion.1.refs_1_, ...), custom_call_target="tpu_custom_call" | custom-call | flops 3221225472 | bytes 12582912 | tf_op jit(solution)/shard_map/pallas_call | solution.py:205
  45.4 8.9 %collective-permute-done.7 = bf16[128,2176]{1,0:T(8,128)(2,1)S(1)} collective-permute-done((bf16[128,2176]{1,0:T(8,128)(2,1)S(1)}, bf16[128,2176]{1,0:T(8,128)(2,1)S(1)}, u32[]{:S(2)}, u32[]{:S(2)}) %collective-permute-start.7) | collective-permute-done | bytes 557088 | tf_op jit(solution)/shard_map/ppermute | solution.py:313
  55.9 2.6 %collective-permute-start.12 = (bf16[128,512]{1,0:T(8,128)(2,1)S(1)}, bf16[128,512]{1,0:T(8,128)(2,1)S(1)}, u32[]{:S(2)}, u32[]{:S(2)}) collective-permute-start(bf16[128,512]{1,0:T(8,128)(2,1)S(1)} %pad_maximum_fusion.refs_0_), channel_id=1, source_target_pairs={{0,8},{4,12},{8,0},{12,4},{1,9},{5,13},{9,1},{13,5},{2,10},{6,14},... | collective-permute-start | bytes 393224 | tf_op jit(solution)/shard_map/ppermute | solution.py:313
  58.5 1.8 %collective-permute-start.13 = (bf16[128,512]{1,0:T(8,128)(2,1)S(1)}, bf16[128,512]{1,0:T(8,128)(2,1)S(1)}, u32[]{:S(2)}, u32[]{:S(2)}) collective-permute-start(bf16[128,512]{1,0:T(8,128)(2,1)S(1)} %pad_maximum_fusion.refs_0_), channel_id=1, source_target_pairs={{0,12},{4,8},{8,4},{12,0},{1,13},{5,9},{9,5},{13,1},{2,14},{6,10},... | collective-permute-start | bytes 393224 | tf_op jit(solution)/shard_map/ppermute | solution.py:313
  60.3 4.1 %shard_map.108 = (bf16[128,2048]{1,0:T(8,128)(2,1)S(1)}, bf16[128,2048]{1,0:T(8,128)(2,1)S(1)}) custom-call(s32[2]{0:T(128)S(1)} %pad_add_fusion.ids_ref, bf16[128,2176]{1,0:T(8,128)(2,1)S(1)} %collective-permute-done.10.refs_0_, bf16[128,2176]{1,0:T(8,128)(2,1)S(1)} %broadcast_select_fusion.refs_1_, ...), custom_call_target="tpu_custom_call" | custom-call | flops 3221225472 | bytes 12582912 | tf_op jit(solution)/shard_map/pallas_call | solution.py:205
  64.5 2.2 %collective-permute-done.12.refs_2_ = bf16[128,512]{1,0:T(8,128)(2,1)S(1)} collective-permute-done((bf16[128,512]{1,0:T(8,128)(2,1)S(1)}, bf16[128,512]{1,0:T(8,128)(2,1)S(1)}, u32[]{:S(2)}, u32[]{:S(2)}) %collective-permute-start.12) | collective-permute-done | bytes 131104 | tf_op jit(solution)/shard_map/ppermute | solution.py:313
  66.7 2.5 %shard_map.109 = bf16[128,2048]{1,0:T(8,128)(2,1)S(1)} custom-call(s32[2]{0:T(128)S(1)} %pad_add_fusion.ids_ref, bf16[128,2176]{1,0:T(8,128)(2,1)S(1)} %collective-permute-done.9.refs_0_, bf16[2048,768]{1,0:T(8,128)(2,1)S(1)} %get-tuple-element.44.refs_3_.refs_2_.refs_1_, bf16[2048,768]{1,0:T(8,128)(2,1)S(1)} %get-tuple-element.45.refs_4_.refs_3_.refs_2_, ...), custom_call_target="tpu_custom_call" | custom-call | flops 1610612736 | bytes 12582912 | tf_op jit(solution)/shard_map/pallas_call | solution.py:205
  72.7 2.7 %shard_map.110 = bf16[64,1024]{1,0:T(8,128)(2,1)} custom-call(s32[5]{0:T(128)} %stack.35.where_ref, bf16[64,1024]{1,0:T(8,128)(2,1)} %reshape.18.queries_ref, bf16[128,512]{1,0:T(8,128)(2,1)} %copy-done.6, bf16[128,512]{1,0:T(8,128)(2,1)} %copy-done.9, bf16[128,512]{1,0:T(8,128)(2,1)} %copy-done.10, bf16[128,512]{1,0:T(8,128)(2,1)} %copy-done.11), custom_call_target="tpu_custom_call" | custom-call | flops 1000000000 | bytes 4000000 | tf_op jit(solution)/shard_map/pallas_call | solution.py:293
  77.1 7.2 %collective-permute-done.14 = bf16[128,2048]{1,0:T(8,128)(2,1)} collective-permute-done((bf16[128,2048]{1,0:T(8,128)(2,1)S(1)}, bf16[128,2048]{1,0:T(8,128)(2,1)}, u32[]{:S(2)}, u32[]{:S(2)}) %collective-permute-start.14) | collective-permute-done | bytes 524320 | tf_op jit(solution)/shard_map/ppermute | solution.py:317
  85.5 3.9 %collective-permute-start.20 = (bf16[128,2048]{1,0:T(8,128)(2,1)S(1)}, bf16[128,2048]{1,0:T(8,128)(2,1)S(1)}, u32[]{:S(2)}, u32[]{:S(2)}) collective-permute-start(bf16[128,2048]{1,0:T(8,128)(2,1)S(1)} %add_convert_fusion.3), channel_id=1, source_target_pairs={{0,4},{12,8},{1,5},{13,9},{2,6},{14,10},{3,7},{15,11},{16,20},{28,... | collective-permute-start | bytes 1572872 | tf_op jit(solution)/shard_map/ppermute | solution.py:313
  89.4 1.8 %collective-permute-done.16 = bf16[128,2048]{1,0:T(8,128)(2,1)} collective-permute-done((bf16[128,2048]{1,0:T(8,128)(2,1)}, bf16[128,2048]{1,0:T(8,128)(2,1)}, u32[]{:S(2)}, u32[]{:S(2)}) %collective-permute-start.16) | collective-permute-done | bytes 524320 | tf_op jit(solution)/shard_map/ppermute | solution.py:317
  92.4 5.6 %collective-permute-start.17 = (bf16[128,2048]{1,0:T(8,128)(2,1)S(1)}, bf16[128,2048]{1,0:T(8,128)(2,1)S(1)}, u32[]{:S(2)}, u32[]{:S(2)}) collective-permute-start(bf16[128,2048]{1,0:T(8,128)(2,1)S(1)} %add_convert_fusion.5), channel_id=1, source_target_pairs={{0,4},{12,8},{1,5},{13,9},{2,6},{14,10},{3,7},{15,11},{16,20},{28,... | collective-permute-start | bytes 1572872 | tf_op jit(solution)/shard_map/ppermute | solution.py:313
  101.0 6.3 %collective-permute-done.17 = bf16[128,2048]{1,0:T(8,128)(2,1)S(1)} collective-permute-done((bf16[128,2048]{1,0:T(8,128)(2,1)S(1)}, bf16[128,2048]{1,0:T(8,128)(2,1)S(1)}, u32[]{:S(2)}, u32[]{:S(2)}) %collective-permute-start.17) | collective-permute-done | bytes 524320 | tf_op jit(solution)/shard_map/ppermute | solution.py:313
  108.1 4.8 %collective-permute-done.19 = bf16[128,2048]{1,0:T(8,128)(2,1)S(1)} collective-permute-done((bf16[128,2048]{1,0:T(8,128)(2,1)S(1)}, bf16[128,2048]{1,0:T(8,128)(2,1)S(1)}, u32[]{:S(2)}, u32[]{:S(2)}) %collective-permute-start.19) | collective-permute-done | bytes 524320 | tf_op jit(solution)/shard_map/ppermute | solution.py:317
  113.3 7.1 %collective-permute-done.15 = bf16[128,2048]{1,0:T(8,128)(2,1)S(1)} collective-permute-done((bf16[128,2048]{1,0:T(8,128)(2,1)S(1)}, bf16[128,2048]{1,0:T(8,128)(2,1)S(1)}, u32[]{:S(2)}, u32[]{:S(2)}) %collective-permute-start.15) | collective-permute-done | bytes 524320 | tf_op jit(solution)/shard_map/ppermute | solution.py:317
  120.4 2.1 %collective-permute-done.22 = bf16[128,2048]{1,0:T(8,128)(2,1)S(1)} collective-permute-done((bf16[128,2048]{1,0:T(8,128)(2,1)S(1)}, bf16[128,2048]{1,0:T(8,128)(2,1)S(1)}, u32[]{:S(2)}, u32[]{:S(2)}) %collective-permute-start.22) | collective-permute-done | bytes 524320 | tf_op jit(solution)/shard_map/ppermute | solution.py:313
  (67 shorter events, 26.0 us)
Async XLA Ops:
  0.6 10.5 %collective-permute-start.2 = (bf16[2048,768]{1,0:T(8,128)(2,1)}, bf16[2048,768]{1,0:T(8,128)(2,1)S(1)}, u32[]{:S(2)}, u32[]{:S(2)}) collective-permute-start(bf16[2048,768]{1,0:T(8,128)(2,1)} %bitcast.19), channel_id=1, source_target_pairs={{0,1},{1,0},{2,3},{3,2},{4,5},{5,4},{6,7},{7,6},{8,9},{9,8},{10,11... | collective-permute-start | bytes 9437192 | tf_op jit(solution)/shard_map/ppermute | solution.py:339
  1.1 10.1 %collective-permute-start.3 = (bf16[768,2048]{1,0:T(8,128)(2,1)}, bf16[768,2048]{1,0:T(8,128)(2,1)}, u32[]{:S(2)}, u32[]{:S(2)}) collective-permute-start(bf16[768,2048]{1,0:T(8,128)(2,1)} %bitcast.21), channel_id=1, source_target_pairs={{0,1},{1,0},{2,3},{3,2},{4,5},{5,4},{6,7},{7,6},{8,9},{9,8},{10,11... | collective-permute-start | bytes 9437192 | tf_op jit(solution)/shard_map/ppermute | solution.py:340
  3.6 16.2 %collective-permute-start = (bf16[128,2176]{1,0:T(8,128)(2,1)}, bf16[128,2176]{1,0:T(8,128)(2,1)}, u32[]{:S(2)}, u32[]{:S(2)}) collective-permute-start(bf16[128,2176]{1,0:T(8,128)(2,1)} %shard_map.104.refs_0_), channel_id=1, source_target_pairs={{0,4},{4,0},{8,12},{12,8},{1,5},{5,1},{9,13},{13,9},{2,6},{6,2},{1... | collective-permute-start | bytes 1671176 | tf_op jit(solution)/shard_map/ppermute | solution.py:313
  6.6 13.2 %collective-permute-start.1 = (bf16[128,2176]{1,0:T(8,128)(2,1)}, bf16[128,2176]{1,0:T(8,128)(2,1)}, u32[]{:S(2)}, u32[]{:S(2)}) collective-permute-start(bf16[128,2176]{1,0:T(8,128)(2,1)} %shard_map.104.refs_0_), channel_id=1, source_target_pairs={{4,8},{8,4},{5,9},{9,5},{6,10},{10,6},{7,11},{11,7},{20,24},{24,20... | collective-permute-start | bytes 1671176 | tf_op jit(solution)/shard_map/ppermute | solution.py:313
  8.0 15.6 %collective-permute-start.6 = (bf16[128,2176]{1,0:T(8,128)(2,1)}, bf16[128,2176]{1,0:T(8,128)(2,1)}, u32[]{:S(2)}, u32[]{:S(2)}) collective-permute-start(bf16[128,2176]{1,0:T(8,128)(2,1)} %shard_map.104.refs_0_), channel_id=1, source_target_pairs={{0,2},{1,3},{2,0},{3,1},{4,6},{5,7},{6,4},{7,5},{8,10},{9,11},{10,... | collective-permute-start | bytes 1671176 | tf_op jit(solution)/shard_map/ppermute | solution.py:317
  19.8 18.3 %collective-permute-start.4 = (bf16[128,2176]{1,0:T(8,128)(2,1)}, bf16[128,2176]{1,0:T(8,128)(2,1)S(1)}, u32[]{:S(2)}, u32[]{:S(2)}) collective-permute-start(bf16[128,2176]{1,0:T(8,128)(2,1)} %collective-permute-done.1), channel_id=1, source_target_pairs={{4,0},{8,12},{5,1},{9,13},{6,2},{10,14},{7,3},{11,15},{20,16},{24,... | collective-permute-start | bytes 1671176 | tf_op jit(solution)/shard_map/ppermute | solution.py:313
  21.1 17.0 %collective-permute-start.5 = (bf16[128,2176]{1,0:T(8,128)(2,1)}, bf16[128,2176]{1,0:T(8,128)(2,1)S(1)}, u32[]{:S(2)}, u32[]{:S(2)}) collective-permute-start(bf16[128,2176]{1,0:T(8,128)(2,1)} %collective-permute-done.refs_2_), channel_id=1, source_target_pairs={{4,8},{8,4},{5,9},{9,5},{6,10},{10,6},{7,11},{11,7},{20,24},{24,20... | collective-permute-start | bytes 1671176 | tf_op jit(solution)/shard_map/ppermute | solution.py:313
  22.0 19.3 %collective-permute-start.8 = (bf16[128,2176]{1,0:T(8,128)(2,1)}, bf16[128,2176]{1,0:T(8,128)(2,1)S(1)}, u32[]{:S(2)}, u32[]{:S(2)}) collective-permute-start(bf16[128,2176]{1,0:T(8,128)(2,1)} %collective-permute-done.refs_2_), channel_id=1, source_target_pairs={{0,2},{1,3},{2,0},{3,1},{4,6},{5,7},{6,4},{7,5},{8,10},{9,11},{10,... | collective-permute-start | bytes 1671176 | tf_op jit(solution)/shard_map/ppermute | solution.py:317
  38.1 16.2 %collective-permute-start.7 = (bf16[128,2176]{1,0:T(8,128)(2,1)S(1)}, bf16[128,2176]{1,0:T(8,128)(2,1)S(1)}, u32[]{:S(2)}, u32[]{:S(2)}) collective-permute-start(bf16[128,2176]{1,0:T(8,128)(2,1)S(1)} %collective-permute-done.5), channel_id=1, source_target_pairs={{4,0},{8,12},{5,1},{9,13},{6,2},{10,14},{7,3},{11,15},{20,16},{24,... | collective-permute-start | bytes 1671176 | tf_op jit(solution)/shard_map/ppermute | solution.py:313
  39.7 20.6 %collective-permute-start.10 = (bf16[128,2176]{1,0:T(8,128)(2,1)S(1)}, bf16[128,2176]{1,0:T(8,128)(2,1)S(1)}, u32[]{:S(2)}, u32[]{:S(2)}) collective-permute-start(bf16[128,2176]{1,0:T(8,128)(2,1)S(1)} %broadcast_select_fusion.1.refs_1_), channel_id=1, source_target_pairs={{0,2},{1,3},{2,0},{3,1},{4,6},{5,7},{6,4},{7,5},{8,10},{9,11},{10,... | collective-permute-start | bytes 1671176 | tf_op jit(solution)/shard_map/ppermute | solution.py:317
  54.4 12.3 %collective-permute-start.9 = (bf16[128,2176]{1,0:T(8,128)(2,1)S(1)}, bf16[128,2176]{1,0:T(8,128)(2,1)S(1)}, u32[]{:S(2)}, u32[]{:S(2)}) collective-permute-start(bf16[128,2176]{1,0:T(8,128)(2,1)S(1)} %broadcast_select_fusion.refs_1_), channel_id=1, source_target_pairs={{0,2},{1,3},{2,0},{3,1},{4,6},{5,7},{6,4},{7,5},{8,10},{9,11},{10,... | collective-permute-start | bytes 1671176 | tf_op jit(solution)/shard_map/ppermute | solution.py:317
  55.9 8.6 %collective-permute-start.11 = (bf16[128,512]{1,0:T(8,128)(2,1)S(1)}, bf16[128,512]{1,0:T(8,128)(2,1)S(1)}, u32[]{:S(2)}, u32[]{:S(2)}) collective-permute-start(bf16[128,512]{1,0:T(8,128)(2,1)S(1)} %pad_maximum_fusion.refs_0_), channel_id=1, source_target_pairs={{0,4},{4,0},{8,12},{12,8},{1,5},{5,1},{9,13},{13,9},{2,6},{6,2},{1... | collective-permute-start | bytes 393224 | tf_op jit(solution)/shard_map/ppermute | solution.py:313
  55.9 10.8 %collective-permute-start.12 = (bf16[128,512]{1,0:T(8,128)(2,1)S(1)}, bf16[128,512]{1,0:T(8,128)(2,1)S(1)}, u32[]{:S(2)}, u32[]{:S(2)}) collective-permute-start(bf16[128,512]{1,0:T(8,128)(2,1)S(1)} %pad_maximum_fusion.refs_0_), channel_id=1, source_target_pairs={{0,8},{4,12},{8,0},{12,4},{1,9},{5,13},{9,1},{13,5},{2,10},{6,14},... | collective-permute-start | bytes 393224 | tf_op jit(solution)/shard_map/ppermute | solution.py:313
  58.5 8.2 %collective-permute-start.13 = (bf16[128,512]{1,0:T(8,128)(2,1)S(1)}, bf16[128,512]{1,0:T(8,128)(2,1)S(1)}, u32[]{:S(2)}, u32[]{:S(2)}) collective-permute-start(bf16[128,512]{1,0:T(8,128)(2,1)S(1)} %pad_maximum_fusion.refs_0_), channel_id=1, source_target_pairs={{0,12},{4,8},{8,4},{12,0},{1,13},{5,9},{9,5},{13,1},{2,14},{6,10},... | collective-permute-start | bytes 393224 | tf_op jit(solution)/shard_map/ppermute | solution.py:313
  69.3 15.0 %collective-permute-start.14 = (bf16[128,2048]{1,0:T(8,128)(2,1)S(1)}, bf16[128,2048]{1,0:T(8,128)(2,1)}, u32[]{:S(2)}, u32[]{:S(2)}) collective-permute-start(bf16[128,2048]{1,0:T(8,128)(2,1)S(1)} %shard_map.109), channel_id=1, source_target_pairs={{0,2},{1,3},{2,0},{3,1},{4,6},{5,7},{6,4},{7,5},{8,10},{9,11},{10,... | collective-permute-start | bytes 1572872 | tf_op jit(solution)/shard_map/ppermute | solution.py:317
  72.1 19.1 %collective-permute-start.16 = (bf16[128,2048]{1,0:T(8,128)(2,1)}, bf16[128,2048]{1,0:T(8,128)(2,1)}, u32[]{:S(2)}, u32[]{:S(2)}) collective-permute-start(bf16[128,2048]{1,0:T(8,128)(2,1)} %copy-done.5), channel_id=1, source_target_pairs={{0,2},{1,3},{2,0},{3,1},{4,6},{5,7},{6,4},{7,5},{8,10},{9,11},{10,... | collective-permute-start | bytes 1572872 | tf_op jit(solution)/shard_map/ppermute | solution.py:317
  77.1 21.0 %copy-start.4 = (bf16[128,2048]{1,0:T(8,128)(2,1)S(1)}, bf16[128,2048]{1,0:T(8,128)(2,1)}, u32[]{:S(2)}) copy-start(bf16[128,2048]{1,0:T(8,128)(2,1)} %copy-done.3) | copy-start | bytes 1572868
  85.5 13.4 %collective-permute-start.20 = (bf16[128,2048]{1,0:T(8,128)(2,1)S(1)}, bf16[128,2048]{1,0:T(8,128)(2,1)S(1)}, u32[]{:S(2)}, u32[]{:S(2)}) collective-permute-start(bf16[128,2048]{1,0:T(8,128)(2,1)S(1)} %add_convert_fusion.3), channel_id=1, source_target_pairs={{0,4},{12,8},{1,5},{13,9},{2,6},{14,10},{3,7},{15,11},{16,20},{28,... | collective-permute-start | bytes 1572872 | tf_op jit(solution)/shard_map/ppermute | solution.py:313
  92.4 14.9 %collective-permute-start.17 = (bf16[128,2048]{1,0:T(8,128)(2,1)S(1)}, bf16[128,2048]{1,0:T(8,128)(2,1)S(1)}, u32[]{:S(2)}, u32[]{:S(2)}) collective-permute-start(bf16[128,2048]{1,0:T(8,128)(2,1)S(1)} %add_convert_fusion.5), channel_id=1, source_target_pairs={{0,4},{12,8},{1,5},{13,9},{2,6},{14,10},{3,7},{15,11},{16,20},{28,... | collective-permute-start | bytes 1572872 | tf_op jit(solution)/shard_map/ppermute | solution.py:313
  98.1 14.9 %collective-permute-start.19 = (bf16[128,2048]{1,0:T(8,128)(2,1)S(1)}, bf16[128,2048]{1,0:T(8,128)(2,1)S(1)}, u32[]{:S(2)}, u32[]{:S(2)}) collective-permute-start(bf16[128,2048]{1,0:T(8,128)(2,1)S(1)} %copy-done.4), channel_id=1, source_target_pairs={{0,2},{1,3},{2,0},{3,1},{4,6},{5,7},{6,4},{7,5},{8,10},{9,11},{10,... | collective-permute-start | bytes 1572872 | tf_op jit(solution)/shard_map/ppermute | solution.py:317
  99.0 14.0 %collective-permute-start.21 = (bf16[128,2048]{1,0:T(8,128)(2,1)S(1)}, bf16[128,2048]{1,0:T(8,128)(2,1)S(1)}, u32[]{:S(2)}, u32[]{:S(2)}) collective-permute-start(bf16[128,2048]{1,0:T(8,128)(2,1)S(1)} %add_convert_fusion.2), channel_id=1, source_target_pairs={{4,8},{8,4},{5,9},{9,5},{6,10},{10,6},{7,11},{11,7},{20,24},{24,20... | collective-permute-start | bytes 1572872 | tf_op jit(solution)/shard_map/ppermute | solution.py:313
  99.7 20.7 %collective-permute-start.15 = (bf16[128,2048]{1,0:T(8,128)(2,1)S(1)}, bf16[128,2048]{1,0:T(8,128)(2,1)S(1)}, u32[]{:S(2)}, u32[]{:S(2)}) collective-permute-start(bf16[128,2048]{1,0:T(8,128)(2,1)S(1)} %get-tuple-element.67), channel_id=1, source_target_pairs={{0,2},{1,3},{2,0},{3,1},{4,6},{5,7},{6,4},{7,5},{8,10},{9,11},{10,... | collective-permute-start | bytes 1572872 | tf_op jit(solution)/shard_map/ppermute | solution.py:317
  107.4 13.0 %collective-permute-start.18 = (bf16[128,2048]{1,0:T(8,128)(2,1)S(1)}, bf16[128,2048]{1,0:T(8,128)(2,1)S(1)}, u32[]{:S(2)}, u32[]{:S(2)}) collective-permute-start(bf16[128,2048]{1,0:T(8,128)(2,1)S(1)} %add_convert_fusion.4), channel_id=1, source_target_pairs={{4,8},{8,4},{5,9},{9,5},{6,10},{10,6},{7,11},{11,7},{20,24},{24,20... | collective-permute-start | bytes 1572872 | tf_op jit(solution)/shard_map/ppermute | solution.py:313
  113.2 9.2 %collective-permute-start.22 = (bf16[128,2048]{1,0:T(8,128)(2,1)S(1)}, bf16[128,2048]{1,0:T(8,128)(2,1)S(1)}, u32[]{:S(2)}, u32[]{:S(2)}) collective-permute-start(bf16[128,2048]{1,0:T(8,128)(2,1)S(1)} %add_convert_fusion.1), channel_id=1, source_target_pairs={{0,4},{4,0},{8,12},{12,8},{1,5},{5,1},{9,13},{13,9},{2,6},{6,2},{1... | collective-permute-start | bytes 1572872 | tf_op jit(solution)/shard_map/ppermute | solution.py:313
  (11 other events, 97.9 us)

commit v4 on v3

--- a/solution.py
+++ b/solution.py
@@ -158,17 +158,18 @@
     return pl.pallas_call(
         functools.partial(prepare_kernel, expert_total=expert_total),
         out_shape=jax.ShapeDtypeStruct((rows, features + TAG), jnp.bfloat16),
+        compiler_params=pltpu.CompilerParams(vmem_limit_bytes=8 * 1024 * 1024),
     )(tokens, routes.T, gate_share.T)
 
 
 def experts_kernel(ids_ref, *refs, count, expert_total):
     blocks = refs[:count]
-    gates, downs = refs[count : count + 2], refs[count + 2 : count + 4]
-    outs = refs[count + 4 : 2 * count + 4]
-    rows_in, shares_in, hidden = refs[2 * count + 4 :]
+    gates, downs = refs[count : count + 2]
+    outs = refs[count + 2 : 2 * count + 2]
+    rows_in, shares_in, hidden = refs[2 * count + 2 :]
     rows, width = blocks[0].shape
     features = width - TAG
-    units = gates[0].shape[1]
+    units = gates.shape[2]
     up_tile, down_tile = 256, 512
     lane = lax.broadcasted_iota(jnp.int32, (rows, TAG), 1)
     for i, block in enumerate(blocks):
@@ -183,7 +184,7 @@
         for start in range(0, units, up_tile):
             value = jnp.dot(
                 rows_in[...],
-                gates[j][:, start : start + up_tile],
+                gates[j, :, start : start + up_tile],
                 preferred_element_type=jnp.float32,
             )
             value = value / (1.0 + jnp.exp(-value)) * shares_in[j, :, :1]
@@ -191,20 +192,20 @@
             hidden[:, first : first + up_tile] = value.astype(jnp.bfloat16)
     for start in range(0, features, down_tile):
         cols = slice(start, start + down_tile)
-        total = jnp.dot(hidden[:, :units], downs[0][:, cols], preferred_element_type=jnp.float32)
-        total += jnp.dot(hidden[:, units:], downs[1][:, cols], preferred_element_type=jnp.float32)
+        total = jnp.dot(hidden[:, :units], downs[0, :, cols], preferred_element_type=jnp.float32)
+        total += jnp.dot(hidden[:, units:], downs[1, :, cols], preferred_element_type=jnp.float32)
         for i, out in enumerate(outs):
             out[:, cols] = total[i * rows : (i + 1) * rows].astype(jnp.bfloat16)
 
 
-def experts(ids, blocks, gate_a, gate_b, down_a, down_b, expert_total):
+def experts(ids, blocks, gates, downs, expert_total, weight):
     count = len(blocks)
     rows, width = blocks[0].shape
-    features, units = gate_a.shape
+    features, units = gates.shape[1:]
     inside = pl.BlockSpec(memory_space=pltpu.VMEM)
     return pl.pallas_call(
         functools.partial(experts_kernel, count=count, expert_total=expert_total),
-        in_specs=[pl.BlockSpec(memory_space=pltpu.SMEM)] + [inside] * (count + 4),
+        in_specs=[pl.BlockSpec(memory_space=pltpu.SMEM)] + [inside] * (count + 2),
         out_specs=[inside] * count,
         out_shape=[jax.ShapeDtypeStruct((rows, features), jnp.bfloat16)] * count,
         scratch_shapes=[
@@ -214,44 +215,51 @@
         ],
         compiler_params=pltpu.CompilerParams(vmem_limit_bytes=16 * 1024 * 1024),
         cost_estimate=pl.CostEstimate(
-            flops=8 * count * rows * features * units,
+            flops=weight * 8 * count * rows * features * units,
             bytes_accessed=8 * features * units,
             transcendentals=0,
         ),
-    )(ids, *blocks, gate_a, gate_b, down_a, down_b)
+    )(ids, *blocks, gates, downs)
 
 
 def hold_kernel(*refs):
-    sources, kept, done = refs[:4], refs[4:8], refs[8]
-    copies = [pltpu.make_async_copy(sources[i], kept[i], done.at[i]) for i in range(4)]
+    sources, kept, done = refs[:4], refs[4:6], refs[6]
+    copies = [
+        pltpu.make_async_copy(sources[i], kept[i // 2].at[i % 2], done.at[i]) for i in range(4)
+    ]
     for copy in copies:
         copy.start()
     for copy in copies:
         copy.wait()
 
 
-def hold(*arrays):
+def hold(gate_a, gate_b, down_a, down_b):
     return pl.pallas_call(
         hold_kernel,
         in_specs=[pl.BlockSpec(memory_space=pltpu.HBM)] * 4,
-        out_specs=[pl.BlockSpec(memory_space=pltpu.VMEM)] * 4,
-        out_shape=[jax.ShapeDtypeStruct(array.shape, array.dtype) for array in arrays],
+        out_specs=[pl.BlockSpec(memory_space=pltpu.VMEM)] * 2,
+        out_shape=[
+            jax.ShapeDtypeStruct((2, *array.shape), array.dtype) for array in (gate_a, down_a)
+        ],
         scratch_shapes=[pltpu.SemaphoreType.DMA((4,))],
         compiler_params=pltpu.CompilerParams(vmem_limit_bytes=16 * 1024 * 1024),
-    )(*arrays)
-
-
-def attention_kernel(where_ref, queries_ref, *refs, heads, head_size):
-    pieces, out_ref = refs[:-1], refs[-1]
+    )(gate_a, gate_b, down_a, down_b)
+
+
+def attention_kernel(where_ref, queries_ref, own_ref, mine_ref, other_ref, out_ref, *, heads, head_size):
     query_rows, width = queries_ref.shape
     groups = width // (heads * head_size)
-    span = pieces[0].shape[0]
-    row = lax.broadcasted_iota(jnp.int32, (query_rows, span), 0)
-    col = lax.broadcasted_iota(jnp.int32, (query_rows, span), 1)
-    seen = [
-        jnp.concatenate([where_ref[p] + col <= where_ref[len(pieces)] + row] * groups, axis=0)
-        for p in range(len(pieces))
-    ]
+    half = mine_ref.shape[0] // 3
+    pieces = [own_ref]
+    for ref in (mine_ref, other_ref):
+        pieces += [ref.at[pl.ds(i * half, half)] for i in range(3)]
+    seen = []
+    for p, piece in enumerate(pieces):
+        extent = (query_rows, piece.shape[0])
+        row = lax.broadcasted_iota(jnp.int32, extent, 0)
+        col = lax.broadcasted_iota(jnp.int32, extent, 1)
+        mask = where_ref[p] + col <= where_ref[len(pieces)] + row
+        seen.append(jnp.concatenate([mask] * groups, axis=0))
     for h in range(heads):
         first = h * groups * head_size
         rows = jnp.concatenate(
@@ -295,6 +303,7 @@
         in_specs=[pl.BlockSpec(memory_space=pltpu.SMEM)] + [inside] * (1 + len(pieces)),
         out_specs=inside,
         out_shape=jax.ShapeDtypeStruct((query_rows, width), jnp.bfloat16),
+        compiler_params=pltpu.CompilerParams(vmem_limit_bytes=12 * 1024 * 1024),
         cost_estimate=pl.CostEstimate(
             flops=10**9, bytes_accessed=4 * 10**6, transcendentals=0
         ),
@@ -315,6 +324,11 @@
 
 def across(array):
     return lax.ppermute(array, "ep", ACROSS)
+
+
+def across_at(places, array):
+    pairs = [(4 * z + i, 4 * z + j) for z in places for i, j in ACROSS]
+    return lax.ppermute(array, ("ctx", "ep"), pairs)
 
 
 def added(*terms):
@@ -333,23 +347,31 @@
     ids = jnp.stack([own_expert, own_expert ^ 1]).astype(jnp.int32)
     span, heads, head_size = key_rows.shape
     query_rows = queries.shape[0]
-    places = [z, z ^ 1, z ^ 2, z ^ 3]
-    positions = jnp.stack([p * span for p in places] + [offset[0] + z * query_rows])
+    core = lax.axis_index("ep") % 2
+    half = span // 2
+    places = [z * span]
+    places += [(z ^ j) * span + core * half for j in (1, 2, 3)]
+    places += [(z ^ j) * span + (1 - core) * half for j in (1, 2, 3)]
+    positions = jnp.stack(places + [offset[0] + z * query_rows])
     gate_a, down_a = expert_gate[0], expert_down[0]
     gate_b = lax.ppermute(gate_a, "ep", SIBLING)
     down_b = lax.ppermute(down_a, "ep", SIBLING)
 
-    def run(*blocks):
-        return experts(ids, blocks, gate_a, gate_b, down_a, down_b, expert_total)
+    def run(*blocks, weight=1):
+        return experts(ids, blocks, gates, downs, expert_total, weight)
 
     own = prepare(tokens, routes, gate_share, expert_total)
     near = along_z(own, NEAR)
     mid_one = along_z(own, MIDDLE)
     own_x = across(own)
-    gate_a, gate_b, down_a, down_b = hold(gate_a, gate_b, down_a, down_b)
-    near, mid_one, gate_a, gate_b, down_a, down_b = together(
-        near, mid_one, gate_a, gate_b, down_a, down_b
-    )
+    keys = jnp.concatenate([key_rows.reshape(span, -1), values.reshape(span, -1)], axis=1)
+    flat = queries.reshape(query_rows, -1)
+    part = jnp.where(core == 0, keys[:half], keys[half:])
+    gate_a, keys, part, flat, positions, ids, middle = together(
+        gate_a, keys, part, flat, positions, ids, middle
+    )
+    gates, downs = hold(gate_a, gate_b, down_a, down_b)
+    near, mid_one, gates, downs = together(near, mid_one, gates, downs)
 
     mid_two = along_z(near, MIDDLE)
     end_one = along_z(mid_one, OUTWARD)
@@ -364,32 +386,40 @@
     end_two = along_z(mid_two, OUTWARD)
     part_near_x, part_second = run(near_x, second)
     third = jnp.where(middle, mid_two, end_two)
-    keys = jnp.concatenate([key_rows.reshape(span, -1), values.reshape(span, -1)], axis=1)
-    flat = queries.reshape(query_rows, -1)
-    third, part_near_x, part_second, keys, flat = together(
-        third, part_near_x, part_second, keys, flat
+    third, part_near_x, part_second, keys, part = together(
+        third, part_near_x, part_second, keys, part
     )
 
     third_x = across(third)
-    pieces = [keys] + [along_z(keys, [(i, i ^ j) for i in range(4)]) for j in (1, 2, 3)]
+    mine = [along_z(part, [(i, i ^ j) for i in range(4)]) for j in (1, 2, 3)]
     part_second_x, part_third = run(second_x, third)
-    third_x, part_second_x, part_third, *pieces = together(
-        third_x, part_second_x, part_third, *pieces
-    )
-    (part_third_x,) = run(third_x)
-
-    back_third = across(part_third_x)
-    attended = attention_pieces(flat, pieces, positions, heads, head_size).reshape(queries.shape)
-    back_third, attended = together(back_third, attended)
-    sum_third = added(part_third, back_third)
-    back_two = along_z(sum_third, INWARD)
-    sum_second = added(part_second, across(part_second_x))
-    back_mid_two = along_z(added(sum_third, back_two), MIDDLE)
+    back_in = along_z(part_third, INWARD)
+    back_side = along_z(part_second_x, MIDDLE)
+    third_x, part_second_x, part_third, *mine = together(
+        third_x, part_second_x, part_third, *mine
+    )
+    mine = jnp.concatenate(mine, axis=0)
+    (part_third_x,) = run(third_x, weight=10)
+    part_third_x, part_second_x = together(part_third_x, part_second_x)
+
+    back_far = along_z(part_third_x, [(0, 2), (3, 1)])
+    back_third = across_at((1, 2), part_third_x)
+    other = lax.ppermute(mine, "ep", SIBLING)
+    back_second = across_at((0, 3), part_second_x)
+    back_in, back_side, back_far, back_third, flat = together(
+        back_in, back_side, back_far, back_third, flat
+    )
+    back_near_x = across(added(part_near_x, back_far))
+    back_mid_two = along_z(added(part_third, back_third, back_in), MIDDLE)
+    attended = attention_pieces(flat, [keys, mine, other], positions, heads, head_size).reshape(queries.shape)
+    sum_second = added(part_second, back_second)
     back_one = along_z(sum_second, INWARD)
-    sum_near = added(part_near, across(part_near_x), back_mid_two)
+    back_near = along_z(added(part_near, back_near_x, back_mid_two), NEAR)
     back_mid_one = along_z(added(sum_second, back_one), MIDDLE)
-    back_near = along_z(sum_near, NEAR)
-    mixture = added(part_own, across(part_own_x), back_mid_one, back_near)
+    back_own = across(added(part_own_x, back_side))
+    terms = [term.astype(jnp.float32) for term in (part_own, back_own, back_mid_one)]
+    (gathered,) = together(sum(terms))
+    mixture = added(gathered, back_near)
     return (attended, mixture)
 
 

time: 124 us -> 120 us (0.968)
  waiting for transfers between devices: 50.5 us -> 40.3 us
  starting transfers between devices: 34.6 us -> 39.7 us
  local copies, waits for them, and re-layouts: 7.76 us -> 9.7 us
  Pallas kernels: 25 us -> 23.3 us
    ppermute x8 -> x6, waiting for transfers between devices: 21 us -> 0.09 us  [across(): return lax.ppermute(array, 'ep', ACROSS)]
    ppermute x13 -> x15, waiting for transfers between devices: 29.4 us -> 37.2 us  [along_z(): return lax.ppermute(array, 'ctx', pairs)]
    ppermute x0 -> x3, starting transfers between devices: none -> 4.16 us  [the longest x2 4.09 us: across_at(): return lax.ppermute(array, ('ctx', 'ep'), pairs)]
    unnamed x24 -> x13, local copies, waits for them, and re-layouts: 3.82 us -> 7.05 us
    ppermute x13 -> x15, starting transfers between devices: 23.4 us -> 26.5 us  [along_z(): return lax.ppermute(array, 'ctx', pairs)]
    ppermute x0 -> x3, waiting for transfers between devices: none -> 3.06 us  [the longest x2 3.05 us: across_at(): return lax.ppermute(array, ('ctx', 'ep'), pairs)]
    ppermute x8 -> x6, starting transfers between devices: 10.6 us -> 8.48 us  [across(): return lax.ppermute(array, 'ep', ACROSS)]
    convert_element_type x6 -> x7, other arithmetic: 3.95 us -> 3.73 us  [added(): sum((term.astype(jnp.float32) for term in terms)).astype(jnp.bfloat16)]
  transfers between devices with their start and end apart: 23 -> 26, of which waited for: 11 -> 8; matrix products, arithmetic and copies ran while one was open for 6% -> 5% of each run, Pallas kernels for 18% -> 20%
where the time goes in v4:
time: 120 us; the launch traced here: 119 us
  waiting for transfers between devices  40.3 us (34%)
  starting transfers between devices  39.7 us (33%)
  Pallas kernels  23.3 us (19%)
  local copies, waits for them, and re-layouts  9.7 us (8%)
  other arithmetic  4.21 us (4%)
  between operations  1.65 us (1%)
    ppermute x15, waiting for transfers between devices, along_z(): return lax.ppermute(array, 'ctx', pairs)  37.2 us
    ppermute x15, starting transfers between devices, along_z(): return lax.ppermute(array, 'ctx', pairs)  26.5 us
    pallas_call x4, Pallas kernels, experts(): pl.pallas_call(functools.partial(experts_kernel, count=count, expert_tota...  17.6 us
    ppermute x6, starting transfers between devices, across(): return lax.ppermute(array, 'ep', ACROSS)  8.48 us
    unnamed x13, local copies, waits for them, and re-layouts  7.05 us
    ppermute x2, starting transfers between devices, across_at(): return lax.ppermute(array, ('ctx', 'ep'), pairs)  4.09 us
    convert_element_type x7, other arithmetic, added(): sum((term.astype(jnp.float32) for term in terms)).astype(jnp.bfloat16)  3.73 us
    ppermute x2, waiting for transfers between devices, across_at(): return lax.ppermute(array, ('ctx', 'ep'), pairs)  3.05 us
  transfers between devices with their start and end apart: 26, of which 8 were waited for; matrix products, arithmetic and copies ran while one was open for 5% of the time, Pallas kernels for 20%

profile of v4, /device:TPU:0, one launch (start us, length us, event | category | flops | bytes accessed | tf_op | source)
XLA Modules:
  0.0 118.9 jit_solution(777159285509112722)
XLA Ops:
  5.0 3.0 %collective-permute-start = (bf16[128,2176]{1,0:T(8,128)(2,1)}, bf16[128,2176]{1,0:T(8,128)(2,1)}, u32[]{:S(2)}, u32[]{:S(2)}) collective-permute-start(bf16[128,2176]{1,0:T(8,128)(2,1)} %shard_map.104.refs_0_), channel_id=1, source_target_pairs={{0,4},{4,0},{8,12},{12,8},{1,5},{5,1},{9,13},{13,9},{2,6},{6,2},{1... | collective-permute-start | bytes 1671176 | tf_op jit(solution)/shard_map/ppermute | solution.py:322
  14.5 1.9 %copy-done = bf16[1,2048,768]{2,1,0:T(8,128)(2,1)S(1)} copy-done((bf16[1,2048,768]{2,1,0:T(8,128)(2,1)S(1)}, bf16[1,2048,768]{2,1,0:T(8,128)(2,1)}, u32[]{:S(2)}) %copy-start) | copy-done | bytes 3145752
  16.4 1.9 %copy-done.1 = bf16[1,768,2048]{2,1,0:T(8,128)(2,1)S(1)} copy-done((bf16[1,768,2048]{2,1,0:T(8,128)(2,1)S(1)}, bf16[1,768,2048]{2,1,0:T(8,128)(2,1)}, u32[]{:S(2)}) %copy-start.1) | copy-done | bytes 3145752
  18.2 2.6 %shard_map.105 = (bf16[2,2048,768]{2,1,0:T(8,128)(2,1)S(1)}, bf16[2,768,2048]{2,1,0:T(8,128)(2,1)S(1)}) custom-call(bf16[2048,768]{1,0:T(8,128)(2,1)S(1)} %bitcast.23, bf16[2048,768]{1,0:T(8,128)(2,1)S(1)} %collective-permute-done.2.refs_1_, bf16[768,2048]{1,0:T(8,128)(2,1)S(1)} %bitcast.25, bf16[768,2048]{1,0:T(8,128)(2,1)} %collective-permute-done.3.refs_3_), custom_call_target="tpu_custom_call" | custom-call | tf_op jit(solution)/shard_map/pallas_call | solution.py:237
  23.1 1.7 %collective-permute-start.9 = (bf16[128,2176]{1,0:T(8,128)(2,1)}, bf16[128,2176]{1,0:T(8,128)(2,1)S(1)}, u32[]{:S(2)}, u32[]{:S(2)}) collective-permute-start(bf16[128,2176]{1,0:T(8,128)(2,1)} %collective-permute-done.refs_2_), channel_id=1, source_target_pairs={{0,2},{1,3},{2,0},{3,1},{4,6},{5,7},{6,4},{7,5},{8,10},{9,11},{10,... | collective-permute-start | bytes 1671176 | tf_op jit(solution)/shard_map/ppermute | solution.py:326
  24.9 6.7 %shard_map.106 = (bf16[128,2048]{1,0:T(8,128)(2,1)S(1)}, bf16[128,2048]{1,0:T(8,128)(2,1)S(1)}, bf16[128,2048]{1,0:T(8,128)(2,1)S(1)}) custom-call(s32[2]{0:T(128)S(1)} %pad_add_fusion.ids_ref, bf16[128,2176]{1,0:T(8,128)(2,1)} %shard_map.104.refs_0_, bf16[128,2176]{1,0:T(8,128)(2,1)} %collective-permute-done.6.refs_1_, ...), custom_call_target="tpu_custom_call" | custom-call | flops 4831838208 | bytes 12582912 | tf_op jit(solution)/shard_map/pallas_call | solution.py:206
  31.5 7.9 %collective-permute-done.4 = bf16[128,2176]{1,0:T(8,128)(2,1)S(1)} collective-permute-done((bf16[128,2176]{1,0:T(8,128)(2,1)}, bf16[128,2176]{1,0:T(8,128)(2,1)S(1)}, u32[]{:S(2)}, u32[]{:S(2)}) %collective-permute-start.4) | collective-permute-done | bytes 557088 | tf_op jit(solution)/shard_map/ppermute | solution.py:322
  42.4 4.2 %shard_map.107 = (bf16[128,2048]{1,0:T(8,128)(2,1)S(1)}, bf16[128,2048]{1,0:T(8,128)(2,1)S(1)}) custom-call(s32[2]{0:T(128)S(1)} %pad_add_fusion.ids_ref, bf16[128,2176]{1,0:T(8,128)(2,1)S(1)} %collective-permute-done.9.refs_0_, bf16[128,2176]{1,0:T(8,128)(2,1)S(1)} %broadcast_select_fusion.1.refs_1_, ...), custom_call_target="tpu_custom_call" | custom-call | flops 3221225472 | bytes 12582912 | tf_op jit(solution)/shard_map/pallas_call | solution.py:206
  46.5 8.9 %collective-permute-done.8 = bf16[128,2176]{1,0:T(8,128)(2,1)S(1)} collective-permute-done((bf16[128,2176]{1,0:T(8,128)(2,1)S(1)}, bf16[128,2176]{1,0:T(8,128)(2,1)S(1)}, u32[]{:S(2)}, u32[]{:S(2)}) %collective-permute-start.8) | collective-permute-done | bytes 557088 | tf_op jit(solution)/shard_map/ppermute | solution.py:322
  57.1 2.6 %collective-permute-start.14 = (bf16[64,512]{1,0:T(8,128)(2,1)S(1)}, bf16[64,512]{1,0:T(8,128)(2,1)S(1)}, u32[]{:S(2)}, u32[]{:S(2)}) collective-permute-start(bf16[64,512]{1,0:T(8,128)(2,1)S(1)} %slice_select_fusion), channel_id=1, source_target_pairs={{0,8},{4,12},{8,0},{12,4},{1,9},{5,13},{9,1},{13,5},{2,10},{6,14},... | collective-permute-start | bytes 196616 | tf_op jit(solution)/shard_map/ppermute | solution.py:322
  59.7 1.8 %collective-permute-start.15 = (bf16[64,512]{1,0:T(8,128)(2,1)S(1)}, bf16[64,512]{1,0:T(8,128)(2,1)S(1)}, u32[]{:S(2)}, u32[]{:S(2)}) collective-permute-start(bf16[64,512]{1,0:T(8,128)(2,1)S(1)} %slice_select_fusion), channel_id=1, source_target_pairs={{0,12},{4,8},{8,4},{12,0},{1,13},{5,9},{9,5},{13,1},{2,14},{6,10},... | collective-permute-start | bytes 196616 | tf_op jit(solution)/shard_map/ppermute | solution.py:322
  61.5 4.2 %shard_map.108 = (bf16[128,2048]{1,0:T(8,128)(2,1)S(1)}, bf16[128,2048]{1,0:T(8,128)(2,1)S(1)}) custom-call(s32[2]{0:T(128)S(1)} %pad_add_fusion.ids_ref, bf16[128,2176]{1,0:T(8,128)(2,1)S(1)} %collective-permute-done.7.refs_0_, bf16[128,2176]{1,0:T(8,128)(2,1)S(1)} %broadcast_select_fusion.refs_1_, ...), custom_call_target="tpu_custom_call" | custom-call | flops 3221225472 | bytes 12582912 | tf_op jit(solution)/shard_map/pallas_call | solution.py:206
  67.9 2.6 %shard_map.109 = bf16[128,2048]{1,0:T(8,128)(2,1)S(1)} custom-call(s32[2]{0:T(128)S(1)} %pad_add_fusion.ids_ref, bf16[128,2176]{1,0:T(8,128)(2,1)S(1)} %collective-permute-done.12.refs_0_, bf16[2,2048,768]{2,1,0:T(8,128)(2,1)S(1)} %get-tuple-element.53.refs_3_.refs_2_.refs_1_, bf16[2,768,2048]{2,1,0:T(8,128)(2,1)S(1)} %get-tuple-element.54.refs_4_.refs_3_.refs_2_), custom_call_target="tpu_custom_call" | custom-call | flops 16106127360 | bytes 12582912 | tf_op jit(solution)/shard_map/pallas_call | solution.py:206
  70.5 3.8 %collective-permute-start.16 = (bf16[128,2048]{1,0:T(8,128)(2,1)S(1)}, bf16[128,2048]{1,0:T(8,128)(2,1)S(1)}, u32[]{:S(2)}, u32[]{:S(2)}) collective-permute-start(bf16[128,2048]{1,0:T(8,128)(2,1)S(1)} %shard_map.109), channel_id=1, source_target_pairs={{0,8},{12,4},{1,9},{13,5},{2,10},{14,6},{3,11},{15,7},{16,24},{28,... | collective-permute-start | bytes 1572872 | tf_op jit(solution)/shard_map/ppermute | solution.py:322
  75.0 3.4 %collective-permute-start.20 = (bf16[128,2048]{1,0:T(8,128)(2,1)S(1)}, bf16[128,2048]{1,0:T(8,128)(2,1)S(1)}, u32[]{:S(2)}, u32[]{:S(2)}) collective-permute-start(bf16[128,2048]{1,0:T(8,128)(2,1)S(1)} %get-tuple-element.81), channel_id=1, source_target_pairs={{0,2},{1,3},{2,0},{3,1},{12,14},{13,15},{14,12},{15,13},{16,18},{1... | collective-permute-start | bytes 1572872 | tf_op jit(solution)/shard_map/ppermute | solution.py:331
  78.6 7.8 %collective-permute-done.16 = bf16[128,2048]{1,0:T(8,128)(2,1)S(1)} collective-permute-done((bf16[128,2048]{1,0:T(8,128)(2,1)S(1)}, bf16[128,2048]{1,0:T(8,128)(2,1)S(1)}, u32[]{:S(2)}, u32[]{:S(2)}) %collective-permute-start.16) | collective-permute-done | bytes 524320 | tf_op jit(solution)/shard_map/ppermute | solution.py:322
  87.2 3.1 %collective-permute-done.20 = bf16[128,2048]{1,0:T(8,128)(2,1)S(1)} collective-permute-done((bf16[128,2048]{1,0:T(8,128)(2,1)S(1)}, bf16[128,2048]{1,0:T(8,128)(2,1)S(1)}, u32[]{:S(2)}, u32[]{:S(2)}) %collective-permute-start.20) | collective-permute-done | bytes 524320 | tf_op jit(solution)/shard_map/ppermute | solution.py:331
  90.3 2.4 %collective-permute-start.21 = (bf16[128,2048]{1,0:T(8,128)(2,1)S(1)}, bf16[128,2048]{1,0:T(8,128)(2,1)S(1)}, u32[]{:S(2)}, u32[]{:S(2)}) collective-permute-start(bf16[128,2048]{1,0:T(8,128)(2,1)S(1)} %add_convert_fusion.5), channel_id=1, source_target_pairs={{0,4},{12,8},{1,5},{13,9},{2,6},{14,10},{3,7},{15,11},{16,20},{28,... | collective-permute-start | bytes 1572872 | tf_op jit(solution)/shard_map/ppermute | solution.py:322
  93.8 1.6 %collective-permute-start.19 = (bf16[128,2048]{1,0:T(8,128)(2,1)S(1)}, bf16[128,2048]{1,0:T(8,128)(2,1)S(1)}, u32[]{:S(2)}, u32[]{:S(2)}) collective-permute-start(bf16[128,2048]{1,0:T(8,128)(2,1)S(1)} %add_convert_fusion.6), channel_id=1, source_target_pairs={{0,2},{1,3},{2,0},{3,1},{4,6},{5,7},{6,4},{7,5},{8,10},{9,11},{10,... | collective-permute-start | bytes 1572872 | tf_op jit(solution)/shard_map/ppermute | solution.py:326
  95.4 6.3 %collective-permute-done.21 = bf16[128,2048]{1,0:T(8,128)(2,1)S(1)} collective-permute-done((bf16[128,2048]{1,0:T(8,128)(2,1)S(1)}, bf16[128,2048]{1,0:T(8,128)(2,1)S(1)}, u32[]{:S(2)}, u32[]{:S(2)}) %collective-permute-start.21) | collective-permute-done | bytes 524320 | tf_op jit(solution)/shard_map/ppermute | solution.py:322
  103.6 4.6 %collective-permute-start.25 = (bf16[128,2048]{1,0:T(8,128)(2,1)S(1)}, bf16[128,2048]{1,0:T(8,128)(2,1)}, u32[]{:S(2)}, u32[]{:S(2)}) collective-permute-start(bf16[128,2048]{1,0:T(8,128)(2,1)S(1)} %add_convert_fusion.1), channel_id=1, source_target_pairs={{0,4},{4,0},{8,12},{12,8},{1,5},{5,1},{9,13},{13,9},{2,6},{6,2},{1... | collective-permute-start | bytes 1572872 | tf_op jit(solution)/shard_map/ppermute | solution.py:322
  108.2 1.9 %shard_map.110 = bf16[64,1024]{1,0:T(8,128)(2,1)S(1)} custom-call(s32[8]{0:T(128)S(1)} %stack.44.where_ref, bf16[64,1024]{1,0:T(8,128)(2,1)S(1)} %reshape.18.queries_ref, bf16[128,512]{1,0:T(8,128)(2,1)S(1)} %bitcast_dynamic-update-slice_fusion.own_ref, bf16[192,512]{1,0:T(8,128)(2,1)S(1)} %constant_dynamic-update-slice_fusion.mine_ref, ...), custom_call_target="tpu_custom_call" | custom-call | flops 1000000000 | bytes 4000000 | tf_op jit(solution)/shard_map/pallas_call | solution.py:301
  111.1 5.8 %collective-permute-done.25 = bf16[128,2048]{1,0:T(8,128)(2,1)} collective-permute-done((bf16[128,2048]{1,0:T(8,128)(2,1)S(1)}, bf16[128,2048]{1,0:T(8,128)(2,1)}, u32[]{:S(2)}, u32[]{:S(2)}) %collective-permute-start.25) | collective-permute-done | bytes 524320 | tf_op jit(solution)/shard_map/ppermute | solution.py:322
  117.0 1.9 %add_convert_fusion = bf16[128,2048]{1,0:T(8,128)(2,1)} fusion(f32[128,2048]{1,0:T(8,128)S(1)} %convert_add_fusion, bf16[128,2048]{1,0:T(8,128)(2,1)} %collective-permute-done.25), kind=kLoop, calls=%fused_computation | loop fusion | flops 786432 | bytes 2097152 | tf_op jit(solution)/shard_map/convert_element_type | solution.py:335
  (65 shorter events, 24.8 us)
Async XLA Ops:
  0.6 13.8 %collective-permute-start.2 = (bf16[2048,768]{1,0:T(8,128)(2,1)}, bf16[2048,768]{1,0:T(8,128)(2,1)S(1)}, u32[]{:S(2)}, u32[]{:S(2)}) collective-permute-start(bf16[2048,768]{1,0:T(8,128)(2,1)} %bitcast.22), channel_id=1, source_target_pairs={{0,1},{1,0},{2,3},{3,2},{4,5},{5,4},{6,7},{7,6},{8,9},{9,8},{10,11... | collective-permute-start | bytes 9437192 | tf_op jit(solution)/shard_map/ppermute | solution.py:357
  1.1 13.3 %collective-permute-start.3 = (bf16[768,2048]{1,0:T(8,128)(2,1)}, bf16[768,2048]{1,0:T(8,128)(2,1)}, u32[]{:S(2)}, u32[]{:S(2)}) collective-permute-start(bf16[768,2048]{1,0:T(8,128)(2,1)} %bitcast.24), channel_id=1, source_target_pairs={{0,1},{1,0},{2,3},{3,2},{4,5},{5,4},{6,7},{7,6},{8,9},{9,8},{10,11... | collective-permute-start | bytes 9437192 | tf_op jit(solution)/shard_map/ppermute | solution.py:358
  5.0 16.2 %collective-permute-start = (bf16[128,2176]{1,0:T(8,128)(2,1)}, bf16[128,2176]{1,0:T(8,128)(2,1)}, u32[]{:S(2)}, u32[]{:S(2)}) collective-permute-start(bf16[128,2176]{1,0:T(8,128)(2,1)} %shard_map.104.refs_0_), channel_id=1, source_target_pairs={{0,4},{4,0},{8,12},{12,8},{1,5},{5,1},{9,13},{13,9},{2,6},{6,2},{1... | collective-permute-start | bytes 1671176 | tf_op jit(solution)/shard_map/ppermute | solution.py:322
  8.0 13.2 %collective-permute-start.1 = (bf16[128,2176]{1,0:T(8,128)(2,1)}, bf16[128,2176]{1,0:T(8,128)(2,1)}, u32[]{:S(2)}, u32[]{:S(2)}) collective-permute-start(bf16[128,2176]{1,0:T(8,128)(2,1)} %shard_map.104.refs_0_), channel_id=1, source_target_pairs={{4,8},{8,4},{5,9},{9,5},{6,10},{10,6},{7,11},{11,7},{20,24},{24,20... | collective-permute-start | bytes 1671176 | tf_op jit(solution)/shard_map/ppermute | solution.py:322
  9.4 15.4 %collective-permute-start.6 = (bf16[128,2176]{1,0:T(8,128)(2,1)}, bf16[128,2176]{1,0:T(8,128)(2,1)}, u32[]{:S(2)}, u32[]{:S(2)}) collective-permute-start(bf16[128,2176]{1,0:T(8,128)(2,1)} %shard_map.104.refs_0_), channel_id=1, source_target_pairs={{0,2},{1,3},{2,0},{3,1},{4,6},{5,7},{6,4},{7,5},{8,10},{9,11},{10,... | collective-permute-start | bytes 1671176 | tf_op jit(solution)/shard_map/ppermute | solution.py:326
  21.1 18.3 %collective-permute-start.4 = (bf16[128,2176]{1,0:T(8,128)(2,1)}, bf16[128,2176]{1,0:T(8,128)(2,1)S(1)}, u32[]{:S(2)}, u32[]{:S(2)}) collective-permute-start(bf16[128,2176]{1,0:T(8,128)(2,1)} %collective-permute-done.1), channel_id=1, source_target_pairs={{4,0},{8,12},{5,1},{9,13},{6,2},{10,14},{7,3},{11,15},{20,16},{24,... | collective-permute-start | bytes 1671176 | tf_op jit(solution)/shard_map/ppermute | solution.py:322
  22.4 17.1 %collective-permute-start.5 = (bf16[128,2176]{1,0:T(8,128)(2,1)}, bf16[128,2176]{1,0:T(8,128)(2,1)S(1)}, u32[]{:S(2)}, u32[]{:S(2)}) collective-permute-start(bf16[128,2176]{1,0:T(8,128)(2,1)} %collective-permute-done.refs_2_), channel_id=1, source_target_pairs={{4,8},{8,4},{5,9},{9,5},{6,10},{10,6},{7,11},{11,7},{20,24},{24,20... | collective-permute-start | bytes 1671176 | tf_op jit(solution)/shard_map/ppermute | solution.py:322
  23.1 19.2 %collective-permute-start.9 = (bf16[128,2176]{1,0:T(8,128)(2,1)}, bf16[128,2176]{1,0:T(8,128)(2,1)S(1)}, u32[]{:S(2)}, u32[]{:S(2)}) collective-permute-start(bf16[128,2176]{1,0:T(8,128)(2,1)} %collective-permute-done.refs_2_), channel_id=1, source_target_pairs={{0,2},{1,3},{2,0},{3,1},{4,6},{5,7},{6,4},{7,5},{8,10},{9,11},{10,... | collective-permute-start | bytes 1671176 | tf_op jit(solution)/shard_map/ppermute | solution.py:326
  39.5 16.0 %collective-permute-start.8 = (bf16[128,2176]{1,0:T(8,128)(2,1)S(1)}, bf16[128,2176]{1,0:T(8,128)(2,1)S(1)}, u32[]{:S(2)}, u32[]{:S(2)}) collective-permute-start(bf16[128,2176]{1,0:T(8,128)(2,1)S(1)} %collective-permute-done.5), channel_id=1, source_target_pairs={{4,0},{8,12},{5,1},{9,13},{6,2},{10,14},{7,3},{11,15},{20,16},{24,... | collective-permute-start | bytes 1671176 | tf_op jit(solution)/shard_map/ppermute | solution.py:322
  40.8 20.7 %collective-permute-start.7 = (bf16[128,2176]{1,0:T(8,128)(2,1)S(1)}, bf16[128,2176]{1,0:T(8,128)(2,1)S(1)}, u32[]{:S(2)}, u32[]{:S(2)}) collective-permute-start(bf16[128,2176]{1,0:T(8,128)(2,1)S(1)} %broadcast_select_fusion.1.refs_1_), channel_id=1, source_target_pairs={{0,2},{1,3},{2,0},{3,1},{4,6},{5,7},{6,4},{7,5},{8,10},{9,11},{10,... | collective-permute-start | bytes 1671176 | tf_op jit(solution)/shard_map/ppermute | solution.py:326
  55.6 12.4 %collective-permute-start.12 = (bf16[128,2176]{1,0:T(8,128)(2,1)S(1)}, bf16[128,2176]{1,0:T(8,128)(2,1)S(1)}, u32[]{:S(2)}, u32[]{:S(2)}) collective-permute-start(bf16[128,2176]{1,0:T(8,128)(2,1)S(1)} %broadcast_select_fusion.refs_1_), channel_id=1, source_target_pairs={{0,2},{1,3},{2,0},{3,1},{4,6},{5,7},{6,4},{7,5},{8,10},{9,11},{10,... | collective-permute-start | bytes 1671176 | tf_op jit(solution)/shard_map/ppermute | solution.py:326
  57.1 9.9 %collective-permute-start.13 = (bf16[64,512]{1,0:T(8,128)(2,1)S(1)}, bf16[64,512]{1,0:T(8,128)(2,1)S(1)}, u32[]{:S(2)}, u32[]{:S(2)}) collective-permute-start(bf16[64,512]{1,0:T(8,128)(2,1)S(1)} %slice_select_fusion), channel_id=1, source_target_pairs={{0,4},{4,0},{8,12},{12,8},{1,5},{5,1},{9,13},{13,9},{2,6},{6,2},{1... | collective-permute-start | bytes 196616 | tf_op jit(solution)/shard_map/ppermute | solution.py:322
  57.1 10.8 %collective-permute-start.14 = (bf16[64,512]{1,0:T(8,128)(2,1)S(1)}, bf16[64,512]{1,0:T(8,128)(2,1)S(1)}, u32[]{:S(2)}, u32[]{:S(2)}) collective-permute-start(bf16[64,512]{1,0:T(8,128)(2,1)S(1)} %slice_select_fusion), channel_id=1, source_target_pairs={{0,8},{4,12},{8,0},{12,4},{1,9},{5,13},{9,1},{13,5},{2,10},{6,14},... | collective-permute-start | bytes 196616 | tf_op jit(solution)/shard_map/ppermute | solution.py:322
  65.7 12.8 %collective-permute-start.10 = (bf16[128,2048]{1,0:T(8,128)(2,1)S(1)}, bf16[128,2048]{1,0:T(8,128)(2,1)S(1)}, u32[]{:S(2)}, u32[]{:S(2)}) collective-permute-start(bf16[128,2048]{1,0:T(8,128)(2,1)S(1)} %get-tuple-element.85), channel_id=1, source_target_pairs={{0,4},{12,8},{1,5},{13,9},{2,6},{14,10},{3,7},{15,11},{16,20},{28,... | collective-permute-start | bytes 1572872 | tf_op jit(solution)/shard_map/ppermute | solution.py:322
  67.0 11.5 %collective-permute-start.11 = (bf16[128,2048]{1,0:T(8,128)(2,1)S(1)}, bf16[128,2048]{1,0:T(8,128)(2,1)S(1)}, u32[]{:S(2)}, u32[]{:S(2)}) collective-permute-start(bf16[128,2048]{1,0:T(8,128)(2,1)S(1)} %get-tuple-element.81), channel_id=1, source_target_pairs={{4,8},{8,4},{5,9},{9,5},{6,10},{10,6},{7,11},{11,7},{20,24},{24,20... | collective-permute-start | bytes 1572872 | tf_op jit(solution)/shard_map/ppermute | solution.py:322
  70.5 15.9 %collective-permute-start.16 = (bf16[128,2048]{1,0:T(8,128)(2,1)S(1)}, bf16[128,2048]{1,0:T(8,128)(2,1)S(1)}, u32[]{:S(2)}, u32[]{:S(2)}) collective-permute-start(bf16[128,2048]{1,0:T(8,128)(2,1)S(1)} %shard_map.109), channel_id=1, source_target_pairs={{0,8},{12,4},{1,9},{13,5},{2,10},{14,6},{3,11},{15,7},{16,24},{28,... | collective-permute-start | bytes 1572872 | tf_op jit(solution)/shard_map/ppermute | solution.py:322
  74.3 12.1 %collective-permute-start.17 = (bf16[128,2048]{1,0:T(8,128)(2,1)S(1)}, bf16[128,2048]{1,0:T(8,128)(2,1)S(1)}, u32[]{:S(2)}, u32[]{:S(2)}) collective-permute-start(bf16[128,2048]{1,0:T(8,128)(2,1)S(1)} %shard_map.109), channel_id=1, source_target_pairs={{4,6},{5,7},{6,4},{7,5},{8,10},{9,11},{10,8},{11,9},{20,22},{21,23... | collective-permute-start | bytes 1572872 | tf_op jit(solution)/shard_map/ppermute | solution.py:331
  75.0 15.2 %collective-permute-start.20 = (bf16[128,2048]{1,0:T(8,128)(2,1)S(1)}, bf16[128,2048]{1,0:T(8,128)(2,1)S(1)}, u32[]{:S(2)}, u32[]{:S(2)}) collective-permute-start(bf16[128,2048]{1,0:T(8,128)(2,1)S(1)} %get-tuple-element.81), channel_id=1, source_target_pairs={{0,2},{1,3},{2,0},{3,1},{12,14},{13,15},{14,12},{15,13},{16,18},{1... | collective-permute-start | bytes 1572872 | tf_op jit(solution)/shard_map/ppermute | solution.py:331
  78.5 29.7 %collective-permute-start.18 = (bf16[192,512]{1,0:T(8,128)(2,1)S(1)}, bf16[192,512]{1,0:T(8,128)(2,1)S(1)}, u32[]{:S(2)}, u32[]{:S(2)}) collective-permute-start(bf16[192,512]{1,0:T(8,128)(2,1)S(1)} %constant_dynamic-update-slice_fusion.mine_ref), channel_id=1, source_target_pairs={{0,1},{1,0},{2,3},{3,2},{4,5},{5,4},{6,7},{7,6},{8,9},{9,8},{10,11... | collective-permute-start | bytes 589832 | tf_op jit(solution)/shard_map/ppermute | solution.py:407
  86.6 16.7 %collective-permute-start.23 = (bf16[128,2048]{1,0:T(8,128)(2,1)S(1)}, bf16[128,2048]{1,0:T(8,128)(2,1)S(1)}, u32[]{:S(2)}, u32[]{:S(2)}) collective-permute-start(bf16[128,2048]{1,0:T(8,128)(2,1)S(1)} %add_convert_fusion.3), channel_id=1, source_target_pairs={{0,2},{1,3},{2,0},{3,1},{4,6},{5,7},{6,4},{7,5},{8,10},{9,11},{10,... | collective-permute-start | bytes 1572872 | tf_op jit(solution)/shard_map/ppermute | solution.py:326
  90.3 11.3 %collective-permute-start.21 = (bf16[128,2048]{1,0:T(8,128)(2,1)S(1)}, bf16[128,2048]{1,0:T(8,128)(2,1)S(1)}, u32[]{:S(2)}, u32[]{:S(2)}) collective-permute-start(bf16[128,2048]{1,0:T(8,128)(2,1)S(1)} %add_convert_fusion.5), channel_id=1, source_target_pairs={{0,4},{12,8},{1,5},{13,9},{2,6},{14,10},{3,7},{15,11},{16,20},{28,... | collective-permute-start | bytes 1572872 | tf_op jit(solution)/shard_map/ppermute | solution.py:322
  93.0 10.4 %collective-permute-start.24 = (bf16[128,2048]{1,0:T(8,128)(2,1)S(1)}, bf16[128,2048]{1,0:T(8,128)(2,1)S(1)}, u32[]{:S(2)}, u32[]{:S(2)}) collective-permute-start(bf16[128,2048]{1,0:T(8,128)(2,1)S(1)} %add_convert_fusion.2), channel_id=1, source_target_pairs={{4,8},{8,4},{5,9},{9,5},{6,10},{10,6},{7,11},{11,7},{20,24},{24,20... | collective-permute-start | bytes 1572872 | tf_op jit(solution)/shard_map/ppermute | solution.py:322
  93.8 17.1 %collective-permute-start.19 = (bf16[128,2048]{1,0:T(8,128)(2,1)S(1)}, bf16[128,2048]{1,0:T(8,128)(2,1)S(1)}, u32[]{:S(2)}, u32[]{:S(2)}) collective-permute-start(bf16[128,2048]{1,0:T(8,128)(2,1)S(1)} %add_convert_fusion.6), channel_id=1, source_target_pairs={{0,2},{1,3},{2,0},{3,1},{4,6},{5,7},{6,4},{7,5},{8,10},{9,11},{10,... | collective-permute-start | bytes 1572872 | tf_op jit(solution)/shard_map/ppermute | solution.py:326
  103.6 13.4 %collective-permute-start.25 = (bf16[128,2048]{1,0:T(8,128)(2,1)S(1)}, bf16[128,2048]{1,0:T(8,128)(2,1)}, u32[]{:S(2)}, u32[]{:S(2)}) collective-permute-start(bf16[128,2048]{1,0:T(8,128)(2,1)S(1)} %add_convert_fusion.1), channel_id=1, source_target_pairs={{0,4},{4,0},{8,12},{12,8},{1,5},{5,1},{9,13},{13,9},{2,6},{6,2},{1... | collective-permute-start | bytes 1572872 | tf_op jit(solution)/shard_map/ppermute | solution.py:322
  (7 other events, 22.7 us)

commit v5 on v4

--- a/solution.py
+++ b/solution.py
@@ -158,7 +158,6 @@
     return pl.pallas_call(
         functools.partial(prepare_kernel, expert_total=expert_total),
         out_shape=jax.ShapeDtypeStruct((rows, features + TAG), jnp.bfloat16),
-        compiler_params=pltpu.CompilerParams(vmem_limit_bytes=8 * 1024 * 1024),
     )(tokens, routes.T, gate_share.T)
 
 
@@ -249,10 +248,10 @@
 def attention_kernel(where_ref, queries_ref, own_ref, mine_ref, other_ref, out_ref, *, heads, head_size):
     query_rows, width = queries_ref.shape
     groups = width // (heads * head_size)
-    half = mine_ref.shape[0] // 3
+    span = own_ref.shape[0]
     pieces = [own_ref]
     for ref in (mine_ref, other_ref):
-        pieces += [ref.at[pl.ds(i * half, half)] for i in range(3)]
+        pieces += [ref.at[pl.ds(0, span)], ref.at[pl.ds(span, span // 2)]]
     seen = []
     for p, piece in enumerate(pieces):
         extent = (query_rows, piece.shape[0])
@@ -315,6 +314,7 @@
 OUTWARD = [(1, 0), (2, 3)]
 INWARD = [(0, 1), (3, 2)]
 ACROSS = [(i, i ^ 2) for i in range(4)]
+KEYS = [(4 * z + i, 4 * (z ^ (1 + i % 2)) + i) for z in range(4) for i in range(4)]
 SIBLING = [(i, i ^ 1) for i in range(4)]
 
 
@@ -349,9 +349,8 @@
     query_rows = queries.shape[0]
     core = lax.axis_index("ep") % 2
     half = span // 2
-    places = [z * span]
-    places += [(z ^ j) * span + core * half for j in (1, 2, 3)]
-    places += [(z ^ j) * span + (1 - core) * half for j in (1, 2, 3)]
+    places = [z * span, (z ^ (1 + core)) * span, (z ^ 3) * span + core * half]
+    places += [(z ^ (2 - core)) * span, (z ^ 3) * span + (1 - core) * half]
     positions = jnp.stack(places + [offset[0] + z * query_rows])
     gate_a, down_a = expert_gate[0], expert_down[0]
     gate_b = lax.ppermute(gate_a, "ep", SIBLING)
@@ -391,7 +390,10 @@
     )
 
     third_x = across(third)
-    mine = [along_z(part, [(i, i ^ j) for i in range(4)]) for j in (1, 2, 3)]
+    mine = [
+        lax.ppermute(keys, ("ctx", "ep"), KEYS),
+        along_z(part, [(i, i ^ 3) for i in range(4)]),
+    ]
     part_second_x, part_third = run(second_x, third)
     back_in = along_z(part_third, INWARD)
     back_side = along_z(part_second_x, MIDDLE)

time: 120 us -> 118 us (0.983)
  local copies, waits for them, and re-layouts: 9.7 us -> 7.29 us
    unnamed x13 -> x8, local copies, waits for them, and re-layouts: 7.05 us -> 4.64 us
    ppermute x15 -> x13, waiting for transfers between devices: 37.2 us -> 36.4 us  [along_z(): return lax.ppermute(array, 'ctx', pairs)]
    ppermute x15 -> x13, starting transfers between devices: 26.5 us -> 26.4 us  [along_z(): return lax.ppermute(array, 'ctx', pairs)]
  transfers between devices with their start and end apart: 26 -> 25, of which waited for: 8 -> 9; matrix products, arithmetic and copies ran while one was open for 5% -> 5% of each run, Pallas kernels for 20% -> 20%
where the time goes in v5:
time: 118 us; the launch traced here: 117 us
  waiting for transfers between devices  40.9 us (35%)
  starting transfers between devices  39.6 us (34%)
  Pallas kernels  23.8 us (20%)
  local copies, waits for them, and re-layouts  7.29 us (6%)
  other arithmetic  4.15 us (4%)
  between operations  1.62 us (1%)
    ppermute x13, waiting for transfers between devices, along_z(): return lax.ppermute(array, 'ctx', pairs)  36.4 us
    ppermute x13, starting transfers between devices, along_z(): return lax.ppermute(array, 'ctx', pairs)  26.4 us
    pallas_call x4, Pallas kernels, experts(): pl.pallas_call(functools.partial(experts_kernel, count=count, expert_tota...  17.3 us
    ppermute x6, starting transfers between devices, across(): return lax.ppermute(array, 'ep', ACROSS)  8.49 us
    unnamed x8, local copies, waits for them, and re-layouts  4.64 us
    ppermute x2, starting transfers between devices, across_at(): return lax.ppermute(array, ('ctx', 'ep'), pairs)  4.07 us
    convert_element_type x7, other arithmetic, added(): sum((term.astype(jnp.float32) for term in terms)).astype(jnp.bfloat16)  3.72 us
    ppermute x2, waiting for transfers between devices, across_at(): return lax.ppermute(array, ('ctx', 'ep'), pairs)  3.35 us
  transfers between devices with their start and end apart: 25, of which 9 were waited for; matrix products, arithmetic and copies ran while one was open for 5% of the time, Pallas kernels for 20%

profile of v5, /device:TPU:0, one launch (start us, length us, event | category | flops | bytes accessed | tf_op | source)
XLA Modules:
  0.0 117.4 jit_solution(5760688087665669014)
XLA Ops:
  1.2 2.4 %shard_map.104.refs_0_ = bf16[128,2176]{1,0:T(8,128)(2,1)} custom-call(bf16[128,2048]{1,0:T(8,128)(2,1)} %tokens_ref.1, s32[8,128]{1,0:T(8,128)} %bitcast.26, f32[8,128]{1,0:T(8,128)} %bitcast.27), custom_call_target="tpu_custom_call" | custom-call | tf_op jit(solution)/shard_map/pallas_call | solution.py:158
  3.6 3.0 %collective-permute-start = (bf16[128,2176]{1,0:T(8,128)(2,1)}, bf16[128,2176]{1,0:T(8,128)(2,1)}, u32[]{:S(2)}, u32[]{:S(2)}) collective-permute-start(bf16[128,2176]{1,0:T(8,128)(2,1)} %shard_map.104.refs_0_), channel_id=1, source_target_pairs={{0,4},{4,0},{8,12},{12,8},{1,5},{5,1},{9,13},{13,9},{2,6},{6,2},{1... | collective-permute-start | bytes 1671176 | tf_op jit(solution)/shard_map/ppermute | solution.py:322
  13.1 1.9 %copy-done = bf16[1,2048,768]{2,1,0:T(8,128)(2,1)S(1)} copy-done((bf16[1,2048,768]{2,1,0:T(8,128)(2,1)S(1)}, bf16[1,2048,768]{2,1,0:T(8,128)(2,1)}, u32[]{:S(2)}) %copy-start) | copy-done | bytes 3145752
  15.0 1.9 %copy-done.1 = bf16[1,768,2048]{2,1,0:T(8,128)(2,1)S(1)} copy-done((bf16[1,768,2048]{2,1,0:T(8,128)(2,1)S(1)}, bf16[1,768,2048]{2,1,0:T(8,128)(2,1)}, u32[]{:S(2)}) %copy-start.1) | copy-done | bytes 3145752
  16.9 2.6 %shard_map.105 = (bf16[2,2048,768]{2,1,0:T(8,128)(2,1)S(1)}, bf16[2,768,2048]{2,1,0:T(8,128)(2,1)S(1)}) custom-call(bf16[2048,768]{1,0:T(8,128)(2,1)S(1)} %bitcast.21, bf16[2048,768]{1,0:T(8,128)(2,1)S(1)} %collective-permute-done.2.refs_1_, bf16[768,2048]{1,0:T(8,128)(2,1)S(1)} %bitcast.23, bf16[768,2048]{1,0:T(8,128)(2,1)} %collective-permute-done.3.refs_3_), custom_call_target="tpu_custom_call" | custom-call | tf_op jit(solution)/shard_map/pallas_call | solution.py:236
  21.8 1.7 %collective-permute-start.9 = (bf16[128,2176]{1,0:T(8,128)(2,1)}, bf16[128,2176]{1,0:T(8,128)(2,1)S(1)}, u32[]{:S(2)}, u32[]{:S(2)}) collective-permute-start(bf16[128,2176]{1,0:T(8,128)(2,1)} %collective-permute-done.refs_2_), channel_id=1, source_target_pairs={{0,2},{1,3},{2,0},{3,1},{4,6},{5,7},{6,4},{7,5},{8,10},{9,11},{10,... | collective-permute-start | bytes 1671176 | tf_op jit(solution)/shard_map/ppermute | solution.py:326
  23.5 6.5 %shard_map.106 = (bf16[128,2048]{1,0:T(8,128)(2,1)S(1)}, bf16[128,2048]{1,0:T(8,128)(2,1)S(1)}, bf16[128,2048]{1,0:T(8,128)(2,1)S(1)}) custom-call(s32[2]{0:T(128)S(1)} %pad_add_fusion.ids_ref, bf16[128,2176]{1,0:T(8,128)(2,1)S(1)} %copy-done.2, bf16[128,2176]{1,0:T(8,128)(2,1)} %collective-permute-done.6.refs_1_, ...), custom_call_target="tpu_custom_call" | custom-call | flops 4831838208 | bytes 12582912 | tf_op jit(solution)/shard_map/pallas_call | solution.py:205
  30.0 8.1 %collective-permute-done.4 = bf16[128,2176]{1,0:T(8,128)(2,1)S(1)} collective-permute-done((bf16[128,2176]{1,0:T(8,128)(2,1)}, bf16[128,2176]{1,0:T(8,128)(2,1)S(1)}, u32[]{:S(2)}, u32[]{:S(2)}) %collective-permute-start.4) | collective-permute-done | bytes 557088 | tf_op jit(solution)/shard_map/ppermute | solution.py:322
  41.0 4.1 %shard_map.107 = (bf16[128,2048]{1,0:T(8,128)(2,1)S(1)}, bf16[128,2048]{1,0:T(8,128)(2,1)S(1)}) custom-call(s32[2]{0:T(128)S(1)} %pad_add_fusion.ids_ref, bf16[128,2176]{1,0:T(8,128)(2,1)S(1)} %collective-permute-done.9.refs_0_, bf16[128,2176]{1,0:T(8,128)(2,1)S(1)} %broadcast_select_fusion.1.refs_1_, ...), custom_call_target="tpu_custom_call" | custom-call | flops 3221225472 | bytes 12582912 | tf_op jit(solution)/shard_map/pallas_call | solution.py:205
  45.1 9.0 %collective-permute-done.8 = bf16[128,2176]{1,0:T(8,128)(2,1)S(1)} collective-permute-done((bf16[128,2176]{1,0:T(8,128)(2,1)S(1)}, bf16[128,2176]{1,0:T(8,128)(2,1)S(1)}, u32[]{:S(2)}, u32[]{:S(2)}) %collective-permute-start.8) | collective-permute-done | bytes 557088 | tf_op jit(solution)/shard_map/ppermute | solution.py:322
  55.7 2.0 %collective-permute-start.14 = (bf16[64,512]{1,0:T(8,128)(2,1)S(1)}, bf16[64,512]{1,0:T(8,128)(2,1)S(1)}, u32[]{:S(2)}, u32[]{:S(2)}) collective-permute-start(bf16[64,512]{1,0:T(8,128)(2,1)S(1)} %slice_select_fusion), channel_id=1, source_target_pairs={{0,12},{4,8},{8,4},{12,0},{1,13},{5,9},{9,5},{13,1},{2,14},{6,10},... | collective-permute-start | bytes 196616 | tf_op jit(solution)/shard_map/ppermute | solution.py:322
  57.7 4.1 %shard_map.108 = (bf16[128,2048]{1,0:T(8,128)(2,1)S(1)}, bf16[128,2048]{1,0:T(8,128)(2,1)S(1)}) custom-call(s32[2]{0:T(128)S(1)} %pad_add_fusion.ids_ref, bf16[128,2176]{1,0:T(8,128)(2,1)S(1)} %collective-permute-done.7.refs_0_, bf16[128,2176]{1,0:T(8,128)(2,1)S(1)} %broadcast_select_fusion.refs_1_, ...), custom_call_target="tpu_custom_call" | custom-call | flops 3221225472 | bytes 12582912 | tf_op jit(solution)/shard_map/pallas_call | solution.py:205
  61.9 3.1 %collective-permute-start.10 = (bf16[128,2048]{1,0:T(8,128)(2,1)S(1)}, bf16[128,2048]{1,0:T(8,128)(2,1)S(1)}, u32[]{:S(2)}, u32[]{:S(2)}) collective-permute-start(bf16[128,2048]{1,0:T(8,128)(2,1)S(1)} %get-tuple-element.83), channel_id=1, source_target_pairs={{0,4},{12,8},{1,5},{13,9},{2,6},{14,10},{3,7},{15,11},{16,20},{28,... | collective-permute-start | bytes 1572872 | tf_op jit(solution)/shard_map/ppermute | solution.py:322
  66.4 2.6 %shard_map.109 = bf16[128,2048]{1,0:T(8,128)(2,1)S(1)} custom-call(s32[2]{0:T(128)S(1)} %pad_add_fusion.ids_ref, bf16[128,2176]{1,0:T(8,128)(2,1)S(1)} %collective-permute-done.12.refs_0_, bf16[2,2048,768]{2,1,0:T(8,128)(2,1)S(1)} %get-tuple-element.52.refs_3_.refs_2_.refs_1_, bf16[2,768,2048]{2,1,0:T(8,128)(2,1)S(1)} %get-tuple-element.53.refs_4_.refs_3_.refs_2_), custom_call_target="tpu_custom_call" | custom-call | flops 16106127360 | bytes 12582912 | tf_op jit(solution)/shard_map/pallas_call | solution.py:205
  69.0 3.9 %collective-permute-start.15 = (bf16[128,2048]{1,0:T(8,128)(2,1)S(1)}, bf16[128,2048]{1,0:T(8,128)(2,1)S(1)}, u32[]{:S(2)}, u32[]{:S(2)}) collective-permute-start(bf16[128,2048]{1,0:T(8,128)(2,1)S(1)} %shard_map.109), channel_id=1, source_target_pairs={{0,8},{12,4},{1,9},{13,5},{2,10},{14,6},{3,11},{15,7},{16,24},{28,... | collective-permute-start | bytes 1572872 | tf_op jit(solution)/shard_map/ppermute | solution.py:322
  73.7 3.4 %collective-permute-start.19 = (bf16[128,2048]{1,0:T(8,128)(2,1)S(1)}, bf16[128,2048]{1,0:T(8,128)(2,1)S(1)}, u32[]{:S(2)}, u32[]{:S(2)}) collective-permute-start(bf16[128,2048]{1,0:T(8,128)(2,1)S(1)} %get-tuple-element.79), channel_id=1, source_target_pairs={{0,2},{1,3},{2,0},{3,1},{12,14},{13,15},{14,12},{15,13},{16,18},{1... | collective-permute-start | bytes 1572872 | tf_op jit(solution)/shard_map/ppermute | solution.py:331
  77.2 7.5 %collective-permute-done.15 = bf16[128,2048]{1,0:T(8,128)(2,1)S(1)} collective-permute-done((bf16[128,2048]{1,0:T(8,128)(2,1)S(1)}, bf16[128,2048]{1,0:T(8,128)(2,1)S(1)}, u32[]{:S(2)}, u32[]{:S(2)}) %collective-permute-start.15) | collective-permute-done | bytes 524320 | tf_op jit(solution)/shard_map/ppermute | solution.py:322
  85.4 3.3 %collective-permute-done.19 = bf16[128,2048]{1,0:T(8,128)(2,1)S(1)} collective-permute-done((bf16[128,2048]{1,0:T(8,128)(2,1)S(1)}, bf16[128,2048]{1,0:T(8,128)(2,1)S(1)}, u32[]{:S(2)}, u32[]{:S(2)}) %collective-permute-start.19) | collective-permute-done | bytes 524320 | tf_op jit(solution)/shard_map/ppermute | solution.py:331
  88.9 2.3 %collective-permute-start.20 = (bf16[128,2048]{1,0:T(8,128)(2,1)S(1)}, bf16[128,2048]{1,0:T(8,128)(2,1)S(1)}, u32[]{:S(2)}, u32[]{:S(2)}) collective-permute-start(bf16[128,2048]{1,0:T(8,128)(2,1)S(1)} %add_convert_fusion.5), channel_id=1, source_target_pairs={{0,4},{12,8},{1,5},{13,9},{2,6},{14,10},{3,7},{15,11},{16,20},{28,... | collective-permute-start | bytes 1572872 | tf_op jit(solution)/shard_map/ppermute | solution.py:322
  93.9 5.7 %collective-permute-done.20 = bf16[128,2048]{1,0:T(8,128)(2,1)S(1)} collective-permute-done((bf16[128,2048]{1,0:T(8,128)(2,1)S(1)}, bf16[128,2048]{1,0:T(8,128)(2,1)S(1)}, u32[]{:S(2)}, u32[]{:S(2)}) %collective-permute-start.20) | collective-permute-done | bytes 524320 | tf_op jit(solution)/shard_map/ppermute | solution.py:322
  101.5 5.1 %collective-permute-start.24 = (bf16[128,2048]{1,0:T(8,128)(2,1)}, bf16[128,2048]{1,0:T(8,128)(2,1)}, u32[]{:S(2)}, u32[]{:S(2)}) collective-permute-start(bf16[128,2048]{1,0:T(8,128)(2,1)} %add_convert_fusion.1), channel_id=1, source_target_pairs={{0,4},{4,0},{8,12},{12,8},{1,5},{5,1},{9,13},{13,9},{2,6},{6,2},{1... | collective-permute-start | bytes 1572872 | tf_op jit(solution)/shard_map/ppermute | solution.py:322
  106.6 1.6 %shard_map.110 = bf16[64,1024]{1,0:T(8,128)(2,1)S(1)} custom-call(s32[6]{0:T(128)S(1)} %stack.36.where_ref, bf16[64,1024]{1,0:T(8,128)(2,1)S(1)} %reshape.18.queries_ref, bf16[128,512]{1,0:T(8,128)(2,1)S(1)} %bitcast_dynamic-update-slice_fusion.own_ref, bf16[192,512]{1,0:T(8,128)(2,1)S(1)} %constant_dynamic-update-slice_fusion.mine_ref, ...), custom_call_target="tpu_custom_call" | custom-call | flops 1000000000 | bytes 4000000 | tf_op jit(solution)/shard_map/pallas_call | solution.py:300
  109.7 5.8 %collective-permute-done.24 = bf16[128,2048]{1,0:T(8,128)(2,1)} collective-permute-done((bf16[128,2048]{1,0:T(8,128)(2,1)}, bf16[128,2048]{1,0:T(8,128)(2,1)}, u32[]{:S(2)}, u32[]{:S(2)}) %collective-permute-start.24) | collective-permute-done | bytes 524320 | tf_op jit(solution)/shard_map/ppermute | solution.py:322
  115.5 1.9 %add_convert_fusion = bf16[128,2048]{1,0:T(8,128)(2,1)} fusion(f32[128,2048]{1,0:T(8,128)S(1)} %convert_add_fusion, bf16[128,2048]{1,0:T(8,128)(2,1)} %collective-permute-done.24), kind=kLoop, calls=%fused_computation | loop fusion | flops 786432 | bytes 2097152 | tf_op jit(solution)/shard_map/convert_element_type | solution.py:335
  (58 shorter events, 22.4 us)
Async XLA Ops:
  0.6 12.5 %collective-permute-start.2 = (bf16[2048,768]{1,0:T(8,128)(2,1)}, bf16[2048,768]{1,0:T(8,128)(2,1)S(1)}, u32[]{:S(2)}, u32[]{:S(2)}) collective-permute-start(bf16[2048,768]{1,0:T(8,128)(2,1)} %bitcast.20), channel_id=1, source_target_pairs={{0,1},{1,0},{2,3},{3,2},{4,5},{5,4},{6,7},{7,6},{8,9},{9,8},{10,11... | collective-permute-start | bytes 9437192 | tf_op jit(solution)/shard_map/ppermute | solution.py:356
  1.1 12.0 %collective-permute-start.3 = (bf16[768,2048]{1,0:T(8,128)(2,1)}, bf16[768,2048]{1,0:T(8,128)(2,1)}, u32[]{:S(2)}, u32[]{:S(2)}) collective-permute-start(bf16[768,2048]{1,0:T(8,128)(2,1)} %bitcast.22), channel_id=1, source_target_pairs={{0,1},{1,0},{2,3},{3,2},{4,5},{5,4},{6,7},{7,6},{8,9},{9,8},{10,11... | collective-permute-start | bytes 9437192 | tf_op jit(solution)/shard_map/ppermute | solution.py:357
  3.6 16.2 %collective-permute-start = (bf16[128,2176]{1,0:T(8,128)(2,1)}, bf16[128,2176]{1,0:T(8,128)(2,1)}, u32[]{:S(2)}, u32[]{:S(2)}) collective-permute-start(bf16[128,2176]{1,0:T(8,128)(2,1)} %shard_map.104.refs_0_), channel_id=1, source_target_pairs={{0,4},{4,0},{8,12},{12,8},{1,5},{5,1},{9,13},{13,9},{2,6},{6,2},{1... | collective-permute-start | bytes 1671176 | tf_op jit(solution)/shard_map/ppermute | solution.py:322
  6.6 13.2 %collective-permute-start.1 = (bf16[128,2176]{1,0:T(8,128)(2,1)}, bf16[128,2176]{1,0:T(8,128)(2,1)}, u32[]{:S(2)}, u32[]{:S(2)}) collective-permute-start(bf16[128,2176]{1,0:T(8,128)(2,1)} %shard_map.104.refs_0_), channel_id=1, source_target_pairs={{4,8},{8,4},{5,9},{9,5},{6,10},{10,6},{7,11},{11,7},{20,24},{24,20... | collective-permute-start | bytes 1671176 | tf_op jit(solution)/shard_map/ppermute | solution.py:322
  8.1 15.4 %collective-permute-start.6 = (bf16[128,2176]{1,0:T(8,128)(2,1)}, bf16[128,2176]{1,0:T(8,128)(2,1)}, u32[]{:S(2)}, u32[]{:S(2)}) collective-permute-start(bf16[128,2176]{1,0:T(8,128)(2,1)} %shard_map.104.refs_0_), channel_id=1, source_target_pairs={{0,2},{1,3},{2,0},{3,1},{4,6},{5,7},{6,4},{7,5},{8,10},{9,11},{10,... | collective-permute-start | bytes 1671176 | tf_op jit(solution)/shard_map/ppermute | solution.py:326
  19.8 18.3 %collective-permute-start.4 = (bf16[128,2176]{1,0:T(8,128)(2,1)}, bf16[128,2176]{1,0:T(8,128)(2,1)S(1)}, u32[]{:S(2)}, u32[]{:S(2)}) collective-permute-start(bf16[128,2176]{1,0:T(8,128)(2,1)} %collective-permute-done.1), channel_id=1, source_target_pairs={{4,0},{8,12},{5,1},{9,13},{6,2},{10,14},{7,3},{11,15},{20,16},{24,... | collective-permute-start | bytes 1671176 | tf_op jit(solution)/shard_map/ppermute | solution.py:322
  21.1 17.0 %collective-permute-start.5 = (bf16[128,2176]{1,0:T(8,128)(2,1)}, bf16[128,2176]{1,0:T(8,128)(2,1)S(1)}, u32[]{:S(2)}, u32[]{:S(2)}) collective-permute-start(bf16[128,2176]{1,0:T(8,128)(2,1)} %collective-permute-done.refs_2_), channel_id=1, source_target_pairs={{4,8},{8,4},{5,9},{9,5},{6,10},{10,6},{7,11},{11,7},{20,24},{24,20... | collective-permute-start | bytes 1671176 | tf_op jit(solution)/shard_map/ppermute | solution.py:322
  21.8 19.2 %collective-permute-start.9 = (bf16[128,2176]{1,0:T(8,128)(2,1)}, bf16[128,2176]{1,0:T(8,128)(2,1)S(1)}, u32[]{:S(2)}, u32[]{:S(2)}) collective-permute-start(bf16[128,2176]{1,0:T(8,128)(2,1)} %collective-permute-done.refs_2_), channel_id=1, source_target_pairs={{0,2},{1,3},{2,0},{3,1},{4,6},{5,7},{6,4},{7,5},{8,10},{9,11},{10,... | collective-permute-start | bytes 1671176 | tf_op jit(solution)/shard_map/ppermute | solution.py:326
  38.1 16.0 %collective-permute-start.8 = (bf16[128,2176]{1,0:T(8,128)(2,1)S(1)}, bf16[128,2176]{1,0:T(8,128)(2,1)S(1)}, u32[]{:S(2)}, u32[]{:S(2)}) collective-permute-start(bf16[128,2176]{1,0:T(8,128)(2,1)S(1)} %collective-permute-done.5), channel_id=1, source_target_pairs={{4,0},{8,12},{5,1},{9,13},{6,2},{10,14},{7,3},{11,15},{20,16},{24,... | collective-permute-start | bytes 1671176 | tf_op jit(solution)/shard_map/ppermute | solution.py:322
  39.4 18.3 %collective-permute-start.7 = (bf16[128,2176]{1,0:T(8,128)(2,1)S(1)}, bf16[128,2176]{1,0:T(8,128)(2,1)S(1)}, u32[]{:S(2)}, u32[]{:S(2)}) collective-permute-start(bf16[128,2176]{1,0:T(8,128)(2,1)S(1)} %broadcast_select_fusion.1.refs_1_), channel_id=1, source_target_pairs={{0,2},{1,3},{2,0},{3,1},{4,6},{5,7},{6,4},{7,5},{8,10},{9,11},{10,... | collective-permute-start | bytes 1671176 | tf_op jit(solution)/shard_map/ppermute | solution.py:326
  54.2 12.3 %collective-permute-start.12 = (bf16[128,2176]{1,0:T(8,128)(2,1)S(1)}, bf16[128,2176]{1,0:T(8,128)(2,1)S(1)}, u32[]{:S(2)}, u32[]{:S(2)}) collective-permute-start(bf16[128,2176]{1,0:T(8,128)(2,1)S(1)} %broadcast_select_fusion.refs_1_), channel_id=1, source_target_pairs={{0,2},{1,3},{2,0},{3,1},{4,6},{5,7},{6,4},{7,5},{8,10},{9,11},{10,... | collective-permute-start | bytes 1671176 | tf_op jit(solution)/shard_map/ppermute | solution.py:326
  55.7 10.1 %collective-permute-start.13 = (bf16[128,512]{1,0:T(8,128)(2,1)S(1)}, bf16[128,512]{1,0:T(8,128)(2,1)S(1)}, u32[]{:S(2)}, u32[]{:S(2)}) collective-permute-start(bf16[128,512]{1,0:T(8,128)(2,1)S(1)} %bitcast_dynamic-update-slice_fusion.own_ref), channel_id=1, source_target_pairs={{0,4},{1,9},{2,6},{3,11},{4,0},{5,13},{6,2},{7,15},{8,12},{9,1},{1... | collective-permute-start | bytes 393224 | tf_op jit(solution)/shard_map/ppermute | solution.py:394
  55.7 10.1 %collective-permute-start.14 = (bf16[64,512]{1,0:T(8,128)(2,1)S(1)}, bf16[64,512]{1,0:T(8,128)(2,1)S(1)}, u32[]{:S(2)}, u32[]{:S(2)}) collective-permute-start(bf16[64,512]{1,0:T(8,128)(2,1)S(1)} %slice_select_fusion), channel_id=1, source_target_pairs={{0,12},{4,8},{8,4},{12,0},{1,13},{5,9},{9,5},{13,1},{2,14},{6,10},... | collective-permute-start | bytes 196616 | tf_op jit(solution)/shard_map/ppermute | solution.py:322
  61.9 15.2 %collective-permute-start.10 = (bf16[128,2048]{1,0:T(8,128)(2,1)S(1)}, bf16[128,2048]{1,0:T(8,128)(2,1)S(1)}, u32[]{:S(2)}, u32[]{:S(2)}) collective-permute-start(bf16[128,2048]{1,0:T(8,128)(2,1)S(1)} %get-tuple-element.83), channel_id=1, source_target_pairs={{0,4},{12,8},{1,5},{13,9},{2,6},{14,10},{3,7},{15,11},{16,20},{28,... | collective-permute-start | bytes 1572872 | tf_op jit(solution)/shard_map/ppermute | solution.py:322
  64.9 12.2 %collective-permute-start.11 = (bf16[128,2048]{1,0:T(8,128)(2,1)S(1)}, bf16[128,2048]{1,0:T(8,128)(2,1)S(1)}, u32[]{:S(2)}, u32[]{:S(2)}) collective-permute-start(bf16[128,2048]{1,0:T(8,128)(2,1)S(1)} %get-tuple-element.79), channel_id=1, source_target_pairs={{4,8},{8,4},{5,9},{9,5},{6,10},{10,6},{7,11},{11,7},{20,24},{24,20... | collective-permute-start | bytes 1572872 | tf_op jit(solution)/shard_map/ppermute | solution.py:322
  69.0 15.7 %collective-permute-start.15 = (bf16[128,2048]{1,0:T(8,128)(2,1)S(1)}, bf16[128,2048]{1,0:T(8,128)(2,1)S(1)}, u32[]{:S(2)}, u32[]{:S(2)}) collective-permute-start(bf16[128,2048]{1,0:T(8,128)(2,1)S(1)} %shard_map.109), channel_id=1, source_target_pairs={{0,8},{12,4},{1,9},{13,5},{2,10},{14,6},{3,11},{15,7},{16,24},{28,... | collective-permute-start | bytes 1572872 | tf_op jit(solution)/shard_map/ppermute | solution.py:322
  73.0 11.7 %collective-permute-start.16 = (bf16[128,2048]{1,0:T(8,128)(2,1)S(1)}, bf16[128,2048]{1,0:T(8,128)(2,1)S(1)}, u32[]{:S(2)}, u32[]{:S(2)}) collective-permute-start(bf16[128,2048]{1,0:T(8,128)(2,1)S(1)} %shard_map.109), channel_id=1, source_target_pairs={{4,6},{5,7},{6,4},{7,5},{8,10},{9,11},{10,8},{11,9},{20,22},{21,23... | collective-permute-start | bytes 1572872 | tf_op jit(solution)/shard_map/ppermute | solution.py:331
  73.7 15.1 %collective-permute-start.19 = (bf16[128,2048]{1,0:T(8,128)(2,1)S(1)}, bf16[128,2048]{1,0:T(8,128)(2,1)S(1)}, u32[]{:S(2)}, u32[]{:S(2)}) collective-permute-start(bf16[128,2048]{1,0:T(8,128)(2,1)S(1)} %get-tuple-element.79), channel_id=1, source_target_pairs={{0,2},{1,3},{2,0},{3,1},{12,14},{13,15},{14,12},{15,13},{16,18},{1... | collective-permute-start | bytes 1572872 | tf_op jit(solution)/shard_map/ppermute | solution.py:331
  77.1 29.5 %collective-permute-start.17 = (bf16[192,512]{1,0:T(8,128)(2,1)S(1)}, bf16[192,512]{1,0:T(8,128)(2,1)S(1)}, u32[]{:S(2)}, u32[]{:S(2)}) collective-permute-start(bf16[192,512]{1,0:T(8,128)(2,1)S(1)} %constant_dynamic-update-slice_fusion.mine_ref), channel_id=1, source_target_pairs={{0,1},{1,0},{2,3},{3,2},{4,5},{5,4},{6,7},{7,6},{8,9},{9,8},{10,11... | collective-permute-start | bytes 589832 | tf_op jit(solution)/shard_map/ppermute | solution.py:409
  84.8 15.6 %collective-permute-start.22 = (bf16[128,2048]{1,0:T(8,128)(2,1)S(1)}, bf16[128,2048]{1,0:T(8,128)(2,1)S(1)}, u32[]{:S(2)}, u32[]{:S(2)}) collective-permute-start(bf16[128,2048]{1,0:T(8,128)(2,1)S(1)} %add_convert_fusion.3), channel_id=1, source_target_pairs={{0,2},{1,3},{2,0},{3,1},{4,6},{5,7},{6,4},{7,5},{8,10},{9,11},{10,... | collective-permute-start | bytes 1572872 | tf_op jit(solution)/shard_map/ppermute | solution.py:326
  88.9 10.7 %collective-permute-start.20 = (bf16[128,2048]{1,0:T(8,128)(2,1)S(1)}, bf16[128,2048]{1,0:T(8,128)(2,1)S(1)}, u32[]{:S(2)}, u32[]{:S(2)}) collective-permute-start(bf16[128,2048]{1,0:T(8,128)(2,1)S(1)} %add_convert_fusion.5), channel_id=1, source_target_pairs={{0,4},{12,8},{1,5},{13,9},{2,6},{14,10},{3,7},{15,11},{16,20},{28,... | collective-permute-start | bytes 1572872 | tf_op jit(solution)/shard_map/ppermute | solution.py:322
  92.3 17.2 %collective-permute-start.18 = (bf16[128,2048]{1,0:T(8,128)(2,1)S(1)}, bf16[128,2048]{1,0:T(8,128)(2,1)S(1)}, u32[]{:S(2)}, u32[]{:S(2)}) collective-permute-start(bf16[128,2048]{1,0:T(8,128)(2,1)S(1)} %add_convert_fusion.6), channel_id=1, source_target_pairs={{0,2},{1,3},{2,0},{3,1},{4,6},{5,7},{6,4},{7,5},{8,10},{9,11},{10,... | collective-permute-start | bytes 1572872 | tf_op jit(solution)/shard_map/ppermute | solution.py:326
  99.8 9.7 %collective-permute-start.21 = (bf16[128,2048]{1,0:T(8,128)(2,1)S(1)}, bf16[128,2048]{1,0:T(8,128)(2,1)S(1)}, u32[]{:S(2)}, u32[]{:S(2)}) collective-permute-start(bf16[128,2048]{1,0:T(8,128)(2,1)S(1)} %add_convert_fusion.4), channel_id=1, source_target_pairs={{4,8},{8,4},{5,9},{9,5},{6,10},{10,6},{7,11},{11,7},{20,24},{24,20... | collective-permute-start | bytes 1572872 | tf_op jit(solution)/shard_map/ppermute | solution.py:322
  101.5 14.0 %collective-permute-start.24 = (bf16[128,2048]{1,0:T(8,128)(2,1)}, bf16[128,2048]{1,0:T(8,128)(2,1)}, u32[]{:S(2)}, u32[]{:S(2)}) collective-permute-start(bf16[128,2048]{1,0:T(8,128)(2,1)} %add_convert_fusion.1), channel_id=1, source_target_pairs={{0,4},{4,0},{8,12},{12,8},{1,5},{5,1},{9,13},{13,9},{2,6},{6,2},{1... | collective-permute-start | bytes 1572872 | tf_op jit(solution)/shard_map/ppermute | solution.py:322
  (4 other events, 19.4 us)

commit v6 on v5

--- a/solution.py
+++ b/solution.py
@@ -309,6 +309,25 @@
     )(positions, queries, *pieces)
 
 
+def combine_kernel(*refs):
+    out = refs[-1]
+    step = 16
+    for first in range(0, out.shape[0], step):
+        here = slice(first, first + step)
+        total = refs[0][here, :].astype(jnp.float32)
+        for ref in refs[1:-1]:
+            total += ref[here, :].astype(jnp.float32)
+        out[here, :] = total.astype(jnp.bfloat16)
+
+
+def combined(*terms):
+    return pl.pallas_call(
+        combine_kernel,
+        out_shape=jax.ShapeDtypeStruct(terms[0].shape, jnp.bfloat16),
+        compiler_params=pltpu.CompilerParams(vmem_limit_bytes=16 * 1024 * 1024),
+    )(*terms)
+
+
 NEAR = [(0, 1), (1, 0), (2, 3), (3, 2)]
 MIDDLE = [(1, 2), (2, 1)]
 OUTWARD = [(1, 0), (2, 3)]
@@ -421,7 +440,7 @@
     back_own = across(added(part_own_x, back_side))
     terms = [term.astype(jnp.float32) for term in (part_own, back_own, back_mid_one)]
     (gathered,) = together(sum(terms))
-    mixture = added(gathered, back_near)
+    mixture = combined(gathered, back_near)
     return (attended, mixture)
 
 

time: 118 us -> 118 us (level)
    convert_element_type x7 -> x6, other arithmetic: 3.72 us -> 2.59 us  [added(): sum((term.astype(jnp.float32) for term in terms)).astype(jnp.bfloat16)]
  transfers between devices with their start and end apart: 25 -> 25, of which waited for: 9 -> 8; matrix products, arithmetic and copies ran while one was open for 5% -> 6% of each run, Pallas kernels for 20% -> 20%
where the time goes in v6:
time: 118 us; the launch traced here: 117 us
  waiting for transfers between devices  40.8 us (35%)
  starting transfers between devices  39.6 us (34%)
  Pallas kernels  24.7 us (21%)
  local copies, waits for them, and re-layouts  7.29 us (6%)
  other arithmetic  3.03 us (3%)
  between operations  1.61 us (1%)
    ppermute x13, waiting for transfers between devices, along_z(): return lax.ppermute(array, 'ctx', pairs)  36.8 us
    ppermute x13, starting transfers between devices, along_z(): return lax.ppermute(array, 'ctx', pairs)  26.4 us
    pallas_call x4, Pallas kernels, experts(): pl.pallas_call(functools.partial(experts_kernel, count=count, expert_tota...  17.3 us
    ppermute x6, starting transfers between devices, across(): return lax.ppermute(array, 'ep', ACROSS)  8.49 us
    unnamed x8, local copies, waits for them, and re-layouts  4.64 us
    ppermute x2, starting transfers between devices, across_at(): return lax.ppermute(array, ('ctx', 'ep'), pairs)  4.07 us
    ppermute x2, waiting for transfers between devices, across_at(): return lax.ppermute(array, ('ctx', 'ep'), pairs)  3.35 us
    convert_element_type x6, other arithmetic, added(): sum((term.astype(jnp.float32) for term in terms)).astype(jnp.bfloat16)  2.59 us
  transfers between devices with their start and end apart: 25, of which 8 were waited for; matrix products, arithmetic and copies ran while one was open for 6% of the time, Pallas kernels for 20%

profile of v6, /device:TPU:0, one launch (start us, length us, event | category | flops | bytes accessed | tf_op | source)
XLA Modules:
  0.0 117.1 jit_solution(10802215438214181932)
XLA Ops:
  1.2 2.4 %shard_map.104.refs_0_ = bf16[128,2176]{1,0:T(8,128)(2,1)} custom-call(bf16[128,2048]{1,0:T(8,128)(2,1)} %tokens_ref.1, s32[8,128]{1,0:T(8,128)} %bitcast.26, f32[8,128]{1,0:T(8,128)} %bitcast.27), custom_call_target="tpu_custom_call" | custom-call | tf_op jit(solution)/shard_map/pallas_call | solution.py:158
  3.6 3.0 %collective-permute-start = (bf16[128,2176]{1,0:T(8,128)(2,1)}, bf16[128,2176]{1,0:T(8,128)(2,1)}, u32[]{:S(2)}, u32[]{:S(2)}) collective-permute-start(bf16[128,2176]{1,0:T(8,128)(2,1)} %shard_map.104.refs_0_), channel_id=1, source_target_pairs={{0,4},{4,0},{8,12},{12,8},{1,5},{5,1},{9,13},{13,9},{2,6},{6,2},{1... | collective-permute-start | bytes 1671176 | tf_op jit(solution)/shard_map/ppermute | solution.py:341
  13.1 1.9 %copy-done = bf16[1,2048,768]{2,1,0:T(8,128)(2,1)S(1)} copy-done((bf16[1,2048,768]{2,1,0:T(8,128)(2,1)S(1)}, bf16[1,2048,768]{2,1,0:T(8,128)(2,1)}, u32[]{:S(2)}) %copy-start) | copy-done | bytes 3145752
  15.0 1.9 %copy-done.1 = bf16[1,768,2048]{2,1,0:T(8,128)(2,1)S(1)} copy-done((bf16[1,768,2048]{2,1,0:T(8,128)(2,1)S(1)}, bf16[1,768,2048]{2,1,0:T(8,128)(2,1)}, u32[]{:S(2)}) %copy-start.1) | copy-done | bytes 3145752
  16.9 2.6 %shard_map.105 = (bf16[2,2048,768]{2,1,0:T(8,128)(2,1)S(1)}, bf16[2,768,2048]{2,1,0:T(8,128)(2,1)S(1)}) custom-call(bf16[2048,768]{1,0:T(8,128)(2,1)S(1)} %bitcast.21, bf16[2048,768]{1,0:T(8,128)(2,1)S(1)} %collective-permute-done.2.refs_1_, bf16[768,2048]{1,0:T(8,128)(2,1)S(1)} %bitcast.23, bf16[768,2048]{1,0:T(8,128)(2,1)} %collective-permute-done.3.refs_3_), custom_call_target="tpu_custom_call" | custom-call | tf_op jit(solution)/shard_map/pallas_call | solution.py:236
  21.8 1.7 %collective-permute-start.9 = (bf16[128,2176]{1,0:T(8,128)(2,1)}, bf16[128,2176]{1,0:T(8,128)(2,1)S(1)}, u32[]{:S(2)}, u32[]{:S(2)}) collective-permute-start(bf16[128,2176]{1,0:T(8,128)(2,1)} %collective-permute-done.refs_2_), channel_id=1, source_target_pairs={{0,2},{1,3},{2,0},{3,1},{4,6},{5,7},{6,4},{7,5},{8,10},{9,11},{10,... | collective-permute-start | bytes 1671176 | tf_op jit(solution)/shard_map/ppermute | solution.py:345
  23.5 6.5 %shard_map.106 = (bf16[128,2048]{1,0:T(8,128)(2,1)S(1)}, bf16[128,2048]{1,0:T(8,128)(2,1)S(1)}, bf16[128,2048]{1,0:T(8,128)(2,1)S(1)}) custom-call(s32[2]{0:T(128)S(1)} %pad_add_fusion.ids_ref, bf16[128,2176]{1,0:T(8,128)(2,1)S(1)} %copy-done.2, bf16[128,2176]{1,0:T(8,128)(2,1)} %collective-permute-done.6.refs_1_, ...), custom_call_target="tpu_custom_call" | custom-call | flops 4831838208 | bytes 12582912 | tf_op jit(solution)/shard_map/pallas_call | solution.py:205
  30.0 8.1 %collective-permute-done.4 = bf16[128,2176]{1,0:T(8,128)(2,1)S(1)} collective-permute-done((bf16[128,2176]{1,0:T(8,128)(2,1)}, bf16[128,2176]{1,0:T(8,128)(2,1)S(1)}, u32[]{:S(2)}, u32[]{:S(2)}) %collective-permute-start.4) | collective-permute-done | bytes 557088 | tf_op jit(solution)/shard_map/ppermute | solution.py:341
  41.0 4.1 %shard_map.107 = (bf16[128,2048]{1,0:T(8,128)(2,1)S(1)}, bf16[128,2048]{1,0:T(8,128)(2,1)S(1)}) custom-call(s32[2]{0:T(128)S(1)} %pad_add_fusion.ids_ref, bf16[128,2176]{1,0:T(8,128)(2,1)S(1)} %collective-permute-done.9.refs_0_, bf16[128,2176]{1,0:T(8,128)(2,1)S(1)} %broadcast_select_fusion.1.refs_1_, ...), custom_call_target="tpu_custom_call" | custom-call | flops 3221225472 | bytes 12582912 | tf_op jit(solution)/shard_map/pallas_call | solution.py:205
  45.1 9.0 %collective-permute-done.8 = bf16[128,2176]{1,0:T(8,128)(2,1)S(1)} collective-permute-done((bf16[128,2176]{1,0:T(8,128)(2,1)S(1)}, bf16[128,2176]{1,0:T(8,128)(2,1)S(1)}, u32[]{:S(2)}, u32[]{:S(2)}) %collective-permute-start.8) | collective-permute-done | bytes 557088 | tf_op jit(solution)/shard_map/ppermute | solution.py:341
  55.7 2.0 %collective-permute-start.14 = (bf16[64,512]{1,0:T(8,128)(2,1)S(1)}, bf16[64,512]{1,0:T(8,128)(2,1)S(1)}, u32[]{:S(2)}, u32[]{:S(2)}) collective-permute-start(bf16[64,512]{1,0:T(8,128)(2,1)S(1)} %slice_select_fusion), channel_id=1, source_target_pairs={{0,12},{4,8},{8,4},{12,0},{1,13},{5,9},{9,5},{13,1},{2,14},{6,10},... | collective-permute-start | bytes 196616 | tf_op jit(solution)/shard_map/ppermute | solution.py:341
  57.7 4.1 %shard_map.108 = (bf16[128,2048]{1,0:T(8,128)(2,1)S(1)}, bf16[128,2048]{1,0:T(8,128)(2,1)S(1)}) custom-call(s32[2]{0:T(128)S(1)} %pad_add_fusion.ids_ref, bf16[128,2176]{1,0:T(8,128)(2,1)S(1)} %collective-permute-done.7.refs_0_, bf16[128,2176]{1,0:T(8,128)(2,1)S(1)} %broadcast_select_fusion.refs_1_, ...), custom_call_target="tpu_custom_call" | custom-call | flops 3221225472 | bytes 12582912 | tf_op jit(solution)/shard_map/pallas_call | solution.py:205
  61.9 3.1 %collective-permute-start.10 = (bf16[128,2048]{1,0:T(8,128)(2,1)S(1)}, bf16[128,2048]{1,0:T(8,128)(2,1)S(1)}, u32[]{:S(2)}, u32[]{:S(2)}) collective-permute-start(bf16[128,2048]{1,0:T(8,128)(2,1)S(1)} %get-tuple-element.83), channel_id=1, source_target_pairs={{0,4},{12,8},{1,5},{13,9},{2,6},{14,10},{3,7},{15,11},{16,20},{28,... | collective-permute-start | bytes 1572872 | tf_op jit(solution)/shard_map/ppermute | solution.py:341
  66.4 2.6 %shard_map.109 = bf16[128,2048]{1,0:T(8,128)(2,1)S(1)} custom-call(s32[2]{0:T(128)S(1)} %pad_add_fusion.ids_ref, bf16[128,2176]{1,0:T(8,128)(2,1)S(1)} %collective-permute-done.12.refs_0_, bf16[2,2048,768]{2,1,0:T(8,128)(2,1)S(1)} %get-tuple-element.52.refs_3_.refs_2_.refs_1_, bf16[2,768,2048]{2,1,0:T(8,128)(2,1)S(1)} %get-tuple-element.53.refs_4_.refs_3_.refs_2_), custom_call_target="tpu_custom_call" | custom-call | flops 16106127360 | bytes 12582912 | tf_op jit(solution)/shard_map/pallas_call | solution.py:205
  69.0 3.9 %collective-permute-start.15 = (bf16[128,2048]{1,0:T(8,128)(2,1)S(1)}, bf16[128,2048]{1,0:T(8,128)(2,1)S(1)}, u32[]{:S(2)}, u32[]{:S(2)}) collective-permute-start(bf16[128,2048]{1,0:T(8,128)(2,1)S(1)} %shard_map.109), channel_id=1, source_target_pairs={{0,8},{12,4},{1,9},{13,5},{2,10},{14,6},{3,11},{15,7},{16,24},{28,... | collective-permute-start | bytes 1572872 | tf_op jit(solution)/shard_map/ppermute | solution.py:341
  73.7 3.4 %collective-permute-start.19 = (bf16[128,2048]{1,0:T(8,128)(2,1)S(1)}, bf16[128,2048]{1,0:T(8,128)(2,1)S(1)}, u32[]{:S(2)}, u32[]{:S(2)}) collective-permute-start(bf16[128,2048]{1,0:T(8,128)(2,1)S(1)} %get-tuple-element.79), channel_id=1, source_target_pairs={{0,2},{1,3},{2,0},{3,1},{12,14},{13,15},{14,12},{15,13},{16,18},{1... | collective-permute-start | bytes 1572872 | tf_op jit(solution)/shard_map/ppermute | solution.py:350
  77.2 7.5 %collective-permute-done.15 = bf16[128,2048]{1,0:T(8,128)(2,1)S(1)} collective-permute-done((bf16[128,2048]{1,0:T(8,128)(2,1)S(1)}, bf16[128,2048]{1,0:T(8,128)(2,1)S(1)}, u32[]{:S(2)}, u32[]{:S(2)}) %collective-permute-start.15) | collective-permute-done | bytes 524320 | tf_op jit(solution)/shard_map/ppermute | solution.py:341
  85.4 3.3 %collective-permute-done.19 = bf16[128,2048]{1,0:T(8,128)(2,1)S(1)} collective-permute-done((bf16[128,2048]{1,0:T(8,128)(2,1)S(1)}, bf16[128,2048]{1,0:T(8,128)(2,1)S(1)}, u32[]{:S(2)}, u32[]{:S(2)}) %collective-permute-start.19) | collective-permute-done | bytes 524320 | tf_op jit(solution)/shard_map/ppermute | solution.py:350
  88.9 2.3 %collective-permute-start.20 = (bf16[128,2048]{1,0:T(8,128)(2,1)S(1)}, bf16[128,2048]{1,0:T(8,128)(2,1)S(1)}, u32[]{:S(2)}, u32[]{:S(2)}) collective-permute-start(bf16[128,2048]{1,0:T(8,128)(2,1)S(1)} %add_convert_fusion.4), channel_id=1, source_target_pairs={{0,4},{12,8},{1,5},{13,9},{2,6},{14,10},{3,7},{15,11},{16,20},{28,... | collective-permute-start | bytes 1572872 | tf_op jit(solution)/shard_map/ppermute | solution.py:341
  92.3 1.6 %collective-permute-start.18 = (bf16[128,2048]{1,0:T(8,128)(2,1)S(1)}, bf16[128,2048]{1,0:T(8,128)(2,1)S(1)}, u32[]{:S(2)}, u32[]{:S(2)}) collective-permute-start(bf16[128,2048]{1,0:T(8,128)(2,1)S(1)} %add_convert_fusion.5), channel_id=1, source_target_pairs={{0,2},{1,3},{2,0},{3,1},{4,6},{5,7},{6,4},{7,5},{8,10},{9,11},{10,... | collective-permute-start | bytes 1572872 | tf_op jit(solution)/shard_map/ppermute | solution.py:345
  93.9 5.7 %collective-permute-done.20 = bf16[128,2048]{1,0:T(8,128)(2,1)S(1)} collective-permute-done((bf16[128,2048]{1,0:T(8,128)(2,1)S(1)}, bf16[128,2048]{1,0:T(8,128)(2,1)S(1)}, u32[]{:S(2)}, u32[]{:S(2)}) %collective-permute-start.20) | collective-permute-done | bytes 524320 | tf_op jit(solution)/shard_map/ppermute | solution.py:341
  102.3 5.1 %collective-permute-start.24 = (bf16[128,2048]{1,0:T(8,128)(2,1)}, bf16[128,2048]{1,0:T(8,128)(2,1)S(1)}, u32[]{:S(2)}, u32[]{:S(2)}) collective-permute-start(bf16[128,2048]{1,0:T(8,128)(2,1)} %add_convert_fusion), channel_id=1, source_target_pairs={{0,4},{4,0},{8,12},{12,8},{1,5},{5,1},{9,13},{13,9},{2,6},{6,2},{1... | collective-permute-start | bytes 1572872 | tf_op jit(solution)/shard_map/ppermute | solution.py:341
  107.4 1.6 %shard_map.110 = bf16[64,1024]{1,0:T(8,128)(2,1)S(1)} custom-call(s32[6]{0:T(128)S(1)} %stack.36.where_ref, bf16[64,1024]{1,0:T(8,128)(2,1)S(1)} %reshape.18.queries_ref, bf16[128,512]{1,0:T(8,128)(2,1)S(1)} %bitcast_dynamic-update-slice_fusion.own_ref, bf16[192,512]{1,0:T(8,128)(2,1)S(1)} %constant_dynamic-update-slice_fusion.mine_ref, ...), custom_call_target="tpu_custom_call" | custom-call | flops 1000000000 | bytes 4000000 | tf_op jit(solution)/shard_map/pallas_call | solution.py:300
  110.0 6.2 %collective-permute-done.24.refs_1_ = bf16[128,2048]{1,0:T(8,128)(2,1)S(1)} collective-permute-done((bf16[128,2048]{1,0:T(8,128)(2,1)}, bf16[128,2048]{1,0:T(8,128)(2,1)S(1)}, u32[]{:S(2)}, u32[]{:S(2)}) %collective-permute-start.24) | collective-permute-done | bytes 524320 | tf_op jit(solution)/shard_map/ppermute | solution.py:341
  (58 shorter events, 22.0 us)
Async XLA Ops:
  0.6 12.5 %collective-permute-start.2 = (bf16[2048,768]{1,0:T(8,128)(2,1)}, bf16[2048,768]{1,0:T(8,128)(2,1)S(1)}, u32[]{:S(2)}, u32[]{:S(2)}) collective-permute-start(bf16[2048,768]{1,0:T(8,128)(2,1)} %bitcast.20), channel_id=1, source_target_pairs={{0,1},{1,0},{2,3},{3,2},{4,5},{5,4},{6,7},{7,6},{8,9},{9,8},{10,11... | collective-permute-start | bytes 9437192 | tf_op jit(solution)/shard_map/ppermute | solution.py:375
  1.1 12.0 %collective-permute-start.3 = (bf16[768,2048]{1,0:T(8,128)(2,1)}, bf16[768,2048]{1,0:T(8,128)(2,1)}, u32[]{:S(2)}, u32[]{:S(2)}) collective-permute-start(bf16[768,2048]{1,0:T(8,128)(2,1)} %bitcast.22), channel_id=1, source_target_pairs={{0,1},{1,0},{2,3},{3,2},{4,5},{5,4},{6,7},{7,6},{8,9},{9,8},{10,11... | collective-permute-start | bytes 9437192 | tf_op jit(solution)/shard_map/ppermute | solution.py:376
  3.6 16.2 %collective-permute-start = (bf16[128,2176]{1,0:T(8,128)(2,1)}, bf16[128,2176]{1,0:T(8,128)(2,1)}, u32[]{:S(2)}, u32[]{:S(2)}) collective-permute-start(bf16[128,2176]{1,0:T(8,128)(2,1)} %shard_map.104.refs_0_), channel_id=1, source_target_pairs={{0,4},{4,0},{8,12},{12,8},{1,5},{5,1},{9,13},{13,9},{2,6},{6,2},{1... | collective-permute-start | bytes 1671176 | tf_op jit(solution)/shard_map/ppermute | solution.py:341
  6.6 13.2 %collective-permute-start.1 = (bf16[128,2176]{1,0:T(8,128)(2,1)}, bf16[128,2176]{1,0:T(8,128)(2,1)}, u32[]{:S(2)}, u32[]{:S(2)}) collective-permute-start(bf16[128,2176]{1,0:T(8,128)(2,1)} %shard_map.104.refs_0_), channel_id=1, source_target_pairs={{4,8},{8,4},{5,9},{9,5},{6,10},{10,6},{7,11},{11,7},{20,24},{24,20... | collective-permute-start | bytes 1671176 | tf_op jit(solution)/shard_map/ppermute | solution.py:341
  8.1 15.4 %collective-permute-start.6 = (bf16[128,2176]{1,0:T(8,128)(2,1)}, bf16[128,2176]{1,0:T(8,128)(2,1)}, u32[]{:S(2)}, u32[]{:S(2)}) collective-permute-start(bf16[128,2176]{1,0:T(8,128)(2,1)} %shard_map.104.refs_0_), channel_id=1, source_target_pairs={{0,2},{1,3},{2,0},{3,1},{4,6},{5,7},{6,4},{7,5},{8,10},{9,11},{10,... | collective-permute-start | bytes 1671176 | tf_op jit(solution)/shard_map/ppermute | solution.py:345
  19.8 18.3 %collective-permute-start.4 = (bf16[128,2176]{1,0:T(8,128)(2,1)}, bf16[128,2176]{1,0:T(8,128)(2,1)S(1)}, u32[]{:S(2)}, u32[]{:S(2)}) collective-permute-start(bf16[128,2176]{1,0:T(8,128)(2,1)} %collective-permute-done.1), channel_id=1, source_target_pairs={{4,0},{8,12},{5,1},{9,13},{6,2},{10,14},{7,3},{11,15},{20,16},{24,... | collective-permute-start | bytes 1671176 | tf_op jit(solution)/shard_map/ppermute | solution.py:341
  21.1 17.0 %collective-permute-start.5 = (bf16[128,2176]{1,0:T(8,128)(2,1)}, bf16[128,2176]{1,0:T(8,128)(2,1)S(1)}, u32[]{:S(2)}, u32[]{:S(2)}) collective-permute-start(bf16[128,2176]{1,0:T(8,128)(2,1)} %collective-permute-done.refs_2_), channel_id=1, source_target_pairs={{4,8},{8,4},{5,9},{9,5},{6,10},{10,6},{7,11},{11,7},{20,24},{24,20... | collective-permute-start | bytes 1671176 | tf_op jit(solution)/shard_map/ppermute | solution.py:341
  21.8 19.2 %collective-permute-start.9 = (bf16[128,2176]{1,0:T(8,128)(2,1)}, bf16[128,2176]{1,0:T(8,128)(2,1)S(1)}, u32[]{:S(2)}, u32[]{:S(2)}) collective-permute-start(bf16[128,2176]{1,0:T(8,128)(2,1)} %collective-permute-done.refs_2_), channel_id=1, source_target_pairs={{0,2},{1,3},{2,0},{3,1},{4,6},{5,7},{6,4},{7,5},{8,10},{9,11},{10,... | collective-permute-start | bytes 1671176 | tf_op jit(solution)/shard_map/ppermute | solution.py:345
  38.1 16.0 %collective-permute-start.8 = (bf16[128,2176]{1,0:T(8,128)(2,1)S(1)}, bf16[128,2176]{1,0:T(8,128)(2,1)S(1)}, u32[]{:S(2)}, u32[]{:S(2)}) collective-permute-start(bf16[128,2176]{1,0:T(8,128)(2,1)S(1)} %collective-permute-done.5), channel_id=1, source_target_pairs={{4,0},{8,12},{5,1},{9,13},{6,2},{10,14},{7,3},{11,15},{20,16},{24,... | collective-permute-start | bytes 1671176 | tf_op jit(solution)/shard_map/ppermute | solution.py:341
  39.4 18.3 %collective-permute-start.7 = (bf16[128,2176]{1,0:T(8,128)(2,1)S(1)}, bf16[128,2176]{1,0:T(8,128)(2,1)S(1)}, u32[]{:S(2)}, u32[]{:S(2)}) collective-permute-start(bf16[128,2176]{1,0:T(8,128)(2,1)S(1)} %broadcast_select_fusion.1.refs_1_), channel_id=1, source_target_pairs={{0,2},{1,3},{2,0},{3,1},{4,6},{5,7},{6,4},{7,5},{8,10},{9,11},{10,... | collective-permute-start | bytes 1671176 | tf_op jit(solution)/shard_map/ppermute | solution.py:345
  54.2 12.3 %collective-permute-start.12 = (bf16[128,2176]{1,0:T(8,128)(2,1)S(1)}, bf16[128,2176]{1,0:T(8,128)(2,1)S(1)}, u32[]{:S(2)}, u32[]{:S(2)}) collective-permute-start(bf16[128,2176]{1,0:T(8,128)(2,1)S(1)} %broadcast_select_fusion.refs_1_), channel_id=1, source_target_pairs={{0,2},{1,3},{2,0},{3,1},{4,6},{5,7},{6,4},{7,5},{8,10},{9,11},{10,... | collective-permute-start | bytes 1671176 | tf_op jit(solution)/shard_map/ppermute | solution.py:345
  55.7 10.1 %collective-permute-start.13 = (bf16[128,512]{1,0:T(8,128)(2,1)S(1)}, bf16[128,512]{1,0:T(8,128)(2,1)S(1)}, u32[]{:S(2)}, u32[]{:S(2)}) collective-permute-start(bf16[128,512]{1,0:T(8,128)(2,1)S(1)} %bitcast_dynamic-update-slice_fusion.own_ref), channel_id=1, source_target_pairs={{0,4},{1,9},{2,6},{3,11},{4,0},{5,13},{6,2},{7,15},{8,12},{9,1},{1... | collective-permute-start | bytes 393224 | tf_op jit(solution)/shard_map/ppermute | solution.py:413
  55.7 10.1 %collective-permute-start.14 = (bf16[64,512]{1,0:T(8,128)(2,1)S(1)}, bf16[64,512]{1,0:T(8,128)(2,1)S(1)}, u32[]{:S(2)}, u32[]{:S(2)}) collective-permute-start(bf16[64,512]{1,0:T(8,128)(2,1)S(1)} %slice_select_fusion), channel_id=1, source_target_pairs={{0,12},{4,8},{8,4},{12,0},{1,13},{5,9},{9,5},{13,1},{2,14},{6,10},... | collective-permute-start | bytes 196616 | tf_op jit(solution)/shard_map/ppermute | solution.py:341
  61.9 15.2 %collective-permute-start.10 = (bf16[128,2048]{1,0:T(8,128)(2,1)S(1)}, bf16[128,2048]{1,0:T(8,128)(2,1)S(1)}, u32[]{:S(2)}, u32[]{:S(2)}) collective-permute-start(bf16[128,2048]{1,0:T(8,128)(2,1)S(1)} %get-tuple-element.83), channel_id=1, source_target_pairs={{0,4},{12,8},{1,5},{13,9},{2,6},{14,10},{3,7},{15,11},{16,20},{28,... | collective-permute-start | bytes 1572872 | tf_op jit(solution)/shard_map/ppermute | solution.py:341
  64.9 12.2 %collective-permute-start.11 = (bf16[128,2048]{1,0:T(8,128)(2,1)S(1)}, bf16[128,2048]{1,0:T(8,128)(2,1)S(1)}, u32[]{:S(2)}, u32[]{:S(2)}) collective-permute-start(bf16[128,2048]{1,0:T(8,128)(2,1)S(1)} %get-tuple-element.79), channel_id=1, source_target_pairs={{4,8},{8,4},{5,9},{9,5},{6,10},{10,6},{7,11},{11,7},{20,24},{24,20... | collective-permute-start | bytes 1572872 | tf_op jit(solution)/shard_map/ppermute | solution.py:341
  69.0 15.7 %collective-permute-start.15 = (bf16[128,2048]{1,0:T(8,128)(2,1)S(1)}, bf16[128,2048]{1,0:T(8,128)(2,1)S(1)}, u32[]{:S(2)}, u32[]{:S(2)}) collective-permute-start(bf16[128,2048]{1,0:T(8,128)(2,1)S(1)} %shard_map.109), channel_id=1, source_target_pairs={{0,8},{12,4},{1,9},{13,5},{2,10},{14,6},{3,11},{15,7},{16,24},{28,... | collective-permute-start | bytes 1572872 | tf_op jit(solution)/shard_map/ppermute | solution.py:341
  73.0 11.7 %collective-permute-start.16 = (bf16[128,2048]{1,0:T(8,128)(2,1)S(1)}, bf16[128,2048]{1,0:T(8,128)(2,1)S(1)}, u32[]{:S(2)}, u32[]{:S(2)}) collective-permute-start(bf16[128,2048]{1,0:T(8,128)(2,1)S(1)} %shard_map.109), channel_id=1, source_target_pairs={{4,6},{5,7},{6,4},{7,5},{8,10},{9,11},{10,8},{11,9},{20,22},{21,23... | collective-permute-start | bytes 1572872 | tf_op jit(solution)/shard_map/ppermute | solution.py:350
  73.7 15.1 %collective-permute-start.19 = (bf16[128,2048]{1,0:T(8,128)(2,1)S(1)}, bf16[128,2048]{1,0:T(8,128)(2,1)S(1)}, u32[]{:S(2)}, u32[]{:S(2)}) collective-permute-start(bf16[128,2048]{1,0:T(8,128)(2,1)S(1)} %get-tuple-element.79), channel_id=1, source_target_pairs={{0,2},{1,3},{2,0},{3,1},{12,14},{13,15},{14,12},{15,13},{16,18},{1... | collective-permute-start | bytes 1572872 | tf_op jit(solution)/shard_map/ppermute | solution.py:350
  77.1 30.3 %collective-permute-start.17 = (bf16[192,512]{1,0:T(8,128)(2,1)S(1)}, bf16[192,512]{1,0:T(8,128)(2,1)S(1)}, u32[]{:S(2)}, u32[]{:S(2)}) collective-permute-start(bf16[192,512]{1,0:T(8,128)(2,1)S(1)} %constant_dynamic-update-slice_fusion.mine_ref), channel_id=1, source_target_pairs={{0,1},{1,0},{2,3},{3,2},{4,5},{5,4},{6,7},{7,6},{8,9},{9,8},{10,11... | collective-permute-start | bytes 589832 | tf_op jit(solution)/shard_map/ppermute | solution.py:428
  84.8 16.4 %collective-permute-start.22 = (bf16[128,2048]{1,0:T(8,128)(2,1)S(1)}, bf16[128,2048]{1,0:T(8,128)(2,1)S(1)}, u32[]{:S(2)}, u32[]{:S(2)}) collective-permute-start(bf16[128,2048]{1,0:T(8,128)(2,1)S(1)} %add_convert_fusion.2), channel_id=1, source_target_pairs={{0,2},{1,3},{2,0},{3,1},{4,6},{5,7},{6,4},{7,5},{8,10},{9,11},{10,... | collective-permute-start | bytes 1572872 | tf_op jit(solution)/shard_map/ppermute | solution.py:345
  88.9 10.7 %collective-permute-start.20 = (bf16[128,2048]{1,0:T(8,128)(2,1)S(1)}, bf16[128,2048]{1,0:T(8,128)(2,1)S(1)}, u32[]{:S(2)}, u32[]{:S(2)}) collective-permute-start(bf16[128,2048]{1,0:T(8,128)(2,1)S(1)} %add_convert_fusion.4), channel_id=1, source_target_pairs={{0,4},{12,8},{1,5},{13,9},{2,6},{14,10},{3,7},{15,11},{16,20},{28,... | collective-permute-start | bytes 1572872 | tf_op jit(solution)/shard_map/ppermute | solution.py:341
  91.5 9.8 %collective-permute-start.23 = (bf16[128,2048]{1,0:T(8,128)(2,1)S(1)}, bf16[128,2048]{1,0:T(8,128)(2,1)S(1)}, u32[]{:S(2)}, u32[]{:S(2)}) collective-permute-start(bf16[128,2048]{1,0:T(8,128)(2,1)S(1)} %add_convert_fusion.1), channel_id=1, source_target_pairs={{4,8},{8,4},{5,9},{9,5},{6,10},{10,6},{7,11},{11,7},{20,24},{24,20... | collective-permute-start | bytes 1572872 | tf_op jit(solution)/shard_map/ppermute | solution.py:341
  92.3 17.4 %collective-permute-start.18 = (bf16[128,2048]{1,0:T(8,128)(2,1)S(1)}, bf16[128,2048]{1,0:T(8,128)(2,1)S(1)}, u32[]{:S(2)}, u32[]{:S(2)}) collective-permute-start(bf16[128,2048]{1,0:T(8,128)(2,1)S(1)} %add_convert_fusion.5), channel_id=1, source_target_pairs={{0,2},{1,3},{2,0},{3,1},{4,6},{5,7},{6,4},{7,5},{8,10},{9,11},{10,... | collective-permute-start | bytes 1572872 | tf_op jit(solution)/shard_map/ppermute | solution.py:345
  102.3 13.9 %collective-permute-start.24 = (bf16[128,2048]{1,0:T(8,128)(2,1)}, bf16[128,2048]{1,0:T(8,128)(2,1)S(1)}, u32[]{:S(2)}, u32[]{:S(2)}) collective-permute-start(bf16[128,2048]{1,0:T(8,128)(2,1)} %add_convert_fusion), channel_id=1, source_target_pairs={{0,4},{4,0},{8,12},{12,8},{1,5},{5,1},{9,13},{13,9},{2,6},{6,2},{1... | collective-permute-start | bytes 1572872 | tf_op jit(solution)/shard_map/ppermute | solution.py:341
  (4 other events, 19.6 us)

commit v7 on v6

--- a/solution.py
+++ b/solution.py
@@ -379,8 +379,8 @@
         return experts(ids, blocks, gates, downs, expert_total, weight)
 
     own = prepare(tokens, routes, gate_share, expert_total)
+    mid_one = along_z(own, MIDDLE)
     near = along_z(own, NEAR)
-    mid_one = along_z(own, MIDDLE)
     own_x = across(own)
     keys = jnp.concatenate([key_rows.reshape(span, -1), values.reshape(span, -1)], axis=1)
     flat = queries.reshape(query_rows, -1)
@@ -389,15 +389,15 @@
         gate_a, keys, part, flat, positions, ids, middle
     )
     gates, downs = hold(gate_a, gate_b, down_a, down_b)
-    near, mid_one, gates, downs = together(near, mid_one, gates, downs)
+    mid_one, near, gates, downs = together(mid_one, near, gates, downs)
 
     mid_two = along_z(near, MIDDLE)
     end_one = along_z(mid_one, OUTWARD)
     near_x = across(near)
     part_own, part_own_x, part_near = run(own, own_x, near)
     second = jnp.where(middle, mid_one, end_one)
-    second, mid_two, part_own, part_own_x, part_near = together(
-        second, mid_two, part_own, part_own_x, part_near
+    mid_two, second, part_own, part_own_x, part_near = together(
+        mid_two, second, part_own, part_own_x, part_near
     )
 
     second_x = across(second)

time: 118 us -> 117 us (level)
  waiting for transfers between devices: 40.8 us -> 39 us
  starting transfers between devices: 39.6 us -> 40.9 us
    ppermute x13, waiting for transfers between devices: 36.8 us -> 34.6 us  [along_z(): return lax.ppermute(array, 'ctx', pairs)]
    ppermute x13, starting transfers between devices: 26.4 us -> 27.8 us  [along_z(): return lax.ppermute(array, 'ctx', pairs)]
  transfers between devices with their start and end apart: 25 -> 25, of which waited for: 8 -> 9; matrix products, arithmetic and copies ran while one was open for 6% -> 6% of each run, Pallas kernels for 20% -> 20%
where the time goes in v7:
time: 117 us
  starting transfers between devices  40.9 us (35%)
  waiting for transfers between devices  39 us (33%)
  Pallas kernels  24.7 us (21%)
  local copies, waits for them, and re-layouts  7.29 us (6%)
  other arithmetic  3.03 us (3%)
  between operations  1.62 us (1%)
    ppermute x13, waiting for transfers between devices, along_z(): return lax.ppermute(array, 'ctx', pairs)  34.6 us
    ppermute x13, starting transfers between devices, along_z(): return lax.ppermute(array, 'ctx', pairs)  27.8 us
    pallas_call x4, Pallas kernels, experts(): pl.pallas_call(functools.partial(experts_kernel, count=count, expert_tota...  17.3 us
    ppermute x6, starting transfers between devices, across(): return lax.ppermute(array, 'ep', ACROSS)  8.32 us
    unnamed x8, local copies, waits for them, and re-layouts  4.64 us
    ppermute x2, starting transfers between devices, across_at(): return lax.ppermute(array, ('ctx', 'ep'), pairs)  4.1 us
    ppermute x2, waiting for transfers between devices, across_at(): return lax.ppermute(array, ('ctx', 'ep'), pairs)  3.66 us
    convert_element_type x6, other arithmetic, added(): sum((term.astype(jnp.float32) for term in terms)).astype(jnp.bfloat16)  2.59 us
  transfers between devices with their start and end apart: 25, of which 9 were waited for; matrix products, arithmetic and copies ran while one was open for 6% of the time, Pallas kernels for 20%

profile of v7, /device:TPU:0, one launch (start us, length us, event | category | flops | bytes accessed | tf_op | source)
XLA Modules:
  0.0 116.5 jit_solution(11657390584554750317)
XLA Ops:
  1.2 2.4 %shard_map.104.refs_0_ = bf16[128,2176]{1,0:T(8,128)(2,1)} custom-call(bf16[128,2048]{1,0:T(8,128)(2,1)} %tokens_ref.1, s32[8,128]{1,0:T(8,128)} %bitcast.26, f32[8,128]{1,0:T(8,128)} %bitcast.27), custom_call_target="tpu_custom_call" | custom-call | tf_op jit(solution)/shard_map/pallas_call | solution.py:158
  5.1 5.1 %collective-permute-start.1 = (bf16[128,2176]{1,0:T(8,128)(2,1)}, bf16[128,2176]{1,0:T(8,128)(2,1)}, u32[]{:S(2)}, u32[]{:S(2)}) collective-permute-start(bf16[128,2176]{1,0:T(8,128)(2,1)} %shard_map.104.refs_0_), channel_id=1, source_target_pairs={{0,4},{4,0},{8,12},{12,8},{1,5},{5,1},{9,13},{13,9},{2,6},{6,2},{1... | collective-permute-start | bytes 1671176 | tf_op jit(solution)/shard_map/ppermute | solution.py:341
  15.2 1.9 %copy-done = bf16[1,2048,768]{2,1,0:T(8,128)(2,1)S(1)} copy-done((bf16[1,2048,768]{2,1,0:T(8,128)(2,1)S(1)}, bf16[1,2048,768]{2,1,0:T(8,128)(2,1)}, u32[]{:S(2)}) %copy-start) | copy-done | bytes 3145752
  17.1 1.9 %copy-done.1 = bf16[1,768,2048]{2,1,0:T(8,128)(2,1)S(1)} copy-done((bf16[1,768,2048]{2,1,0:T(8,128)(2,1)S(1)}, bf16[1,768,2048]{2,1,0:T(8,128)(2,1)}, u32[]{:S(2)}) %copy-start.1) | copy-done | bytes 3145752
  19.0 2.6 %shard_map.105 = (bf16[2,2048,768]{2,1,0:T(8,128)(2,1)S(1)}, bf16[2,768,2048]{2,1,0:T(8,128)(2,1)S(1)}) custom-call(bf16[2048,768]{1,0:T(8,128)(2,1)S(1)} %bitcast.21, bf16[2048,768]{1,0:T(8,128)(2,1)S(1)} %collective-permute-done.2.refs_1_, bf16[768,2048]{1,0:T(8,128)(2,1)S(1)} %bitcast.23, bf16[768,2048]{1,0:T(8,128)(2,1)} %collective-permute-done.3.refs_3_), custom_call_target="tpu_custom_call" | custom-call | tf_op jit(solution)/shard_map/pallas_call | solution.py:236
  26.6 6.5 %shard_map.106 = (bf16[128,2048]{1,0:T(8,128)(2,1)S(1)}, bf16[128,2048]{1,0:T(8,128)(2,1)S(1)}, bf16[128,2048]{1,0:T(8,128)(2,1)S(1)}) custom-call(s32[2]{0:T(128)S(1)} %pad_add_fusion.ids_ref, bf16[128,2176]{1,0:T(8,128)(2,1)S(1)} %copy-done.2, bf16[128,2176]{1,0:T(8,128)(2,1)} %collective-permute-done.6.refs_1_, ...), custom_call_target="tpu_custom_call" | custom-call | flops 4831838208 | bytes 12582912 | tf_op jit(solution)/shard_map/pallas_call | solution.py:205
  33.1 5.8 %collective-permute-done.5 = bf16[128,2176]{1,0:T(8,128)(2,1)S(1)} collective-permute-done((bf16[128,2176]{1,0:T(8,128)(2,1)}, bf16[128,2176]{1,0:T(8,128)(2,1)S(1)}, u32[]{:S(2)}, u32[]{:S(2)}) %collective-permute-start.5) | collective-permute-done | bytes 557088 | tf_op jit(solution)/shard_map/ppermute | solution.py:341
  40.3 1.6 %collective-permute-start.7 = (bf16[128,2176]{1,0:T(8,128)(2,1)S(1)}, bf16[128,2176]{1,0:T(8,128)(2,1)S(1)}, u32[]{:S(2)}, u32[]{:S(2)}) collective-permute-start(bf16[128,2176]{1,0:T(8,128)(2,1)S(1)} %broadcast_select_fusion.1.refs_1_), channel_id=1, source_target_pairs={{0,2},{1,3},{2,0},{3,1},{4,6},{5,7},{6,4},{7,5},{8,10},{9,11},{10,... | collective-permute-start | bytes 1671176 | tf_op jit(solution)/shard_map/ppermute | solution.py:345
  41.9 4.1 %shard_map.107 = (bf16[128,2048]{1,0:T(8,128)(2,1)S(1)}, bf16[128,2048]{1,0:T(8,128)(2,1)S(1)}) custom-call(s32[2]{0:T(128)S(1)} %pad_add_fusion.ids_ref, bf16[128,2176]{1,0:T(8,128)(2,1)S(1)} %collective-permute-done.9.refs_0_, bf16[128,2176]{1,0:T(8,128)(2,1)S(1)} %broadcast_select_fusion.1.refs_1_, ...), custom_call_target="tpu_custom_call" | custom-call | flops 3221225472 | bytes 12582912 | tf_op jit(solution)/shard_map/pallas_call | solution.py:205
  46.0 8.7 %collective-permute-done.8 = bf16[128,2176]{1,0:T(8,128)(2,1)S(1)} collective-permute-done((bf16[128,2176]{1,0:T(8,128)(2,1)S(1)}, bf16[128,2176]{1,0:T(8,128)(2,1)S(1)}, u32[]{:S(2)}, u32[]{:S(2)}) %collective-permute-start.8) | collective-permute-done | bytes 557088 | tf_op jit(solution)/shard_map/ppermute | solution.py:341
  56.3 2.0 %collective-permute-start.14 = (bf16[64,512]{1,0:T(8,128)(2,1)S(1)}, bf16[64,512]{1,0:T(8,128)(2,1)S(1)}, u32[]{:S(2)}, u32[]{:S(2)}) collective-permute-start(bf16[64,512]{1,0:T(8,128)(2,1)S(1)} %slice_select_fusion), channel_id=1, source_target_pairs={{0,12},{4,8},{8,4},{12,0},{1,13},{5,9},{9,5},{13,1},{2,14},{6,10},... | collective-permute-start | bytes 196616 | tf_op jit(solution)/shard_map/ppermute | solution.py:341
  58.3 4.1 %shard_map.108 = (bf16[128,2048]{1,0:T(8,128)(2,1)S(1)}, bf16[128,2048]{1,0:T(8,128)(2,1)S(1)}) custom-call(s32[2]{0:T(128)S(1)} %pad_add_fusion.ids_ref, bf16[128,2176]{1,0:T(8,128)(2,1)S(1)} %collective-permute-done.7.refs_0_, bf16[128,2176]{1,0:T(8,128)(2,1)S(1)} %broadcast_select_fusion.refs_1_, ...), custom_call_target="tpu_custom_call" | custom-call | flops 3221225472 | bytes 12582912 | tf_op jit(solution)/shard_map/pallas_call | solution.py:205
  62.4 3.1 %collective-permute-start.10 = (bf16[128,2048]{1,0:T(8,128)(2,1)S(1)}, bf16[128,2048]{1,0:T(8,128)(2,1)S(1)}, u32[]{:S(2)}, u32[]{:S(2)}) collective-permute-start(bf16[128,2048]{1,0:T(8,128)(2,1)S(1)} %get-tuple-element.83), channel_id=1, source_target_pairs={{0,4},{12,8},{1,5},{13,9},{2,6},{14,10},{3,7},{15,11},{16,20},{28,... | collective-permute-start | bytes 1572872 | tf_op jit(solution)/shard_map/ppermute | solution.py:341
  66.7 2.5 %shard_map.109 = bf16[128,2048]{1,0:T(8,128)(2,1)S(1)} custom-call(s32[2]{0:T(128)S(1)} %pad_add_fusion.ids_ref, bf16[128,2176]{1,0:T(8,128)(2,1)S(1)} %collective-permute-done.12.refs_0_, bf16[2,2048,768]{2,1,0:T(8,128)(2,1)S(1)} %get-tuple-element.52.refs_3_.refs_2_.refs_1_, bf16[2,768,2048]{2,1,0:T(8,128)(2,1)S(1)} %get-tuple-element.53.refs_4_.refs_3_.refs_2_), custom_call_target="tpu_custom_call" | custom-call | flops 16106127360 | bytes 12582912 | tf_op jit(solution)/shard_map/pallas_call | solution.py:205
  69.3 4.2 %collective-permute-start.15 = (bf16[128,2048]{1,0:T(8,128)(2,1)S(1)}, bf16[128,2048]{1,0:T(8,128)(2,1)S(1)}, u32[]{:S(2)}, u32[]{:S(2)}) collective-permute-start(bf16[128,2048]{1,0:T(8,128)(2,1)S(1)} %shard_map.109), channel_id=1, source_target_pairs={{0,8},{12,4},{1,9},{13,5},{2,10},{14,6},{3,11},{15,7},{16,24},{28,... | collective-permute-start | bytes 1572872 | tf_op jit(solution)/shard_map/ppermute | solution.py:341
  74.2 3.4 %collective-permute-start.19 = (bf16[128,2048]{1,0:T(8,128)(2,1)S(1)}, bf16[128,2048]{1,0:T(8,128)(2,1)S(1)}, u32[]{:S(2)}, u32[]{:S(2)}) collective-permute-start(bf16[128,2048]{1,0:T(8,128)(2,1)S(1)} %get-tuple-element.79), channel_id=1, source_target_pairs={{0,2},{1,3},{2,0},{3,1},{12,14},{13,15},{14,12},{15,13},{16,18},{1... | collective-permute-start | bytes 1572872 | tf_op jit(solution)/shard_map/ppermute | solution.py:350
  77.8 7.2 %collective-permute-done.15 = bf16[128,2048]{1,0:T(8,128)(2,1)S(1)} collective-permute-done((bf16[128,2048]{1,0:T(8,128)(2,1)S(1)}, bf16[128,2048]{1,0:T(8,128)(2,1)S(1)}, u32[]{:S(2)}, u32[]{:S(2)}) %collective-permute-start.15) | collective-permute-done | bytes 524320 | tf_op jit(solution)/shard_map/ppermute | solution.py:341
  85.7 3.7 %collective-permute-done.19 = bf16[128,2048]{1,0:T(8,128)(2,1)S(1)} collective-permute-done((bf16[128,2048]{1,0:T(8,128)(2,1)S(1)}, bf16[128,2048]{1,0:T(8,128)(2,1)S(1)}, u32[]{:S(2)}, u32[]{:S(2)}) %collective-permute-start.19) | collective-permute-done | bytes 524320 | tf_op jit(solution)/shard_map/ppermute | solution.py:350
  89.5 2.0 %collective-permute-start.20 = (bf16[128,2048]{1,0:T(8,128)(2,1)S(1)}, bf16[128,2048]{1,0:T(8,128)(2,1)S(1)}, u32[]{:S(2)}, u32[]{:S(2)}) collective-permute-start(bf16[128,2048]{1,0:T(8,128)(2,1)S(1)} %add_convert_fusion.4), channel_id=1, source_target_pairs={{0,4},{12,8},{1,5},{13,9},{2,6},{14,10},{3,7},{15,11},{16,20},{28,... | collective-permute-start | bytes 1572872 | tf_op jit(solution)/shard_map/ppermute | solution.py:341
  92.7 1.6 %collective-permute-start.18 = (bf16[128,2048]{1,0:T(8,128)(2,1)S(1)}, bf16[128,2048]{1,0:T(8,128)(2,1)S(1)}, u32[]{:S(2)}, u32[]{:S(2)}) collective-permute-start(bf16[128,2048]{1,0:T(8,128)(2,1)S(1)} %add_convert_fusion.5), channel_id=1, source_target_pairs={{0,2},{1,3},{2,0},{3,1},{4,6},{5,7},{6,4},{7,5},{8,10},{9,11},{10,... | collective-permute-start | bytes 1572872 | tf_op jit(solution)/shard_map/ppermute | solution.py:345
  94.2 6.0 %collective-permute-done.20 = bf16[128,2048]{1,0:T(8,128)(2,1)S(1)} collective-permute-done((bf16[128,2048]{1,0:T(8,128)(2,1)S(1)}, bf16[128,2048]{1,0:T(8,128)(2,1)S(1)}, u32[]{:S(2)}, u32[]{:S(2)}) %collective-permute-start.20) | collective-permute-done | bytes 524320 | tf_op jit(solution)/shard_map/ppermute | solution.py:341
  102.9 4.5 %collective-permute-start.24 = (bf16[128,2048]{1,0:T(8,128)(2,1)}, bf16[128,2048]{1,0:T(8,128)(2,1)S(1)}, u32[]{:S(2)}, u32[]{:S(2)}) collective-permute-start(bf16[128,2048]{1,0:T(8,128)(2,1)} %add_convert_fusion), channel_id=1, source_target_pairs={{0,4},{4,0},{8,12},{12,8},{1,5},{5,1},{9,13},{13,9},{2,6},{6,2},{1... | collective-permute-start | bytes 1572872 | tf_op jit(solution)/shard_map/ppermute | solution.py:341
  107.4 1.6 %shard_map.110 = bf16[64,1024]{1,0:T(8,128)(2,1)S(1)} custom-call(s32[6]{0:T(128)S(1)} %stack.36.where_ref, bf16[64,1024]{1,0:T(8,128)(2,1)S(1)} %reshape.18.queries_ref, bf16[128,512]{1,0:T(8,128)(2,1)S(1)} %bitcast_dynamic-update-slice_fusion.own_ref, bf16[192,512]{1,0:T(8,128)(2,1)S(1)} %constant_dynamic-update-slice_fusion.mine_ref, ...), custom_call_target="tpu_custom_call" | custom-call | flops 1000000000 | bytes 4000000 | tf_op jit(solution)/shard_map/pallas_call | solution.py:300
  110.3 5.3 %collective-permute-done.24.refs_1_ = bf16[128,2048]{1,0:T(8,128)(2,1)S(1)} collective-permute-done((bf16[128,2048]{1,0:T(8,128)(2,1)}, bf16[128,2048]{1,0:T(8,128)(2,1)S(1)}, u32[]{:S(2)}, u32[]{:S(2)}) %collective-permute-start.24) | collective-permute-done | bytes 524320 | tf_op jit(solution)/shard_map/ppermute | solution.py:341
  (58 shorter events, 23.2 us)
Async XLA Ops:
  0.6 14.5 %collective-permute-start.2 = (bf16[2048,768]{1,0:T(8,128)(2,1)}, bf16[2048,768]{1,0:T(8,128)(2,1)S(1)}, u32[]{:S(2)}, u32[]{:S(2)}) collective-permute-start(bf16[2048,768]{1,0:T(8,128)(2,1)} %bitcast.20), channel_id=1, source_target_pairs={{0,1},{1,0},{2,3},{3,2},{4,5},{5,4},{6,7},{7,6},{8,9},{9,8},{10,11... | collective-permute-start | bytes 9437192 | tf_op jit(solution)/shard_map/ppermute | solution.py:375
  1.1 14.0 %collective-permute-start.3 = (bf16[768,2048]{1,0:T(8,128)(2,1)}, bf16[768,2048]{1,0:T(8,128)(2,1)}, u32[]{:S(2)}, u32[]{:S(2)}) collective-permute-start(bf16[768,2048]{1,0:T(8,128)(2,1)} %bitcast.22), channel_id=1, source_target_pairs={{0,1},{1,0},{2,3},{3,2},{4,5},{5,4},{6,7},{7,6},{8,9},{9,8},{10,11... | collective-permute-start | bytes 9437192 | tf_op jit(solution)/shard_map/ppermute | solution.py:376
  3.6 17.9 %collective-permute-start = (bf16[128,2176]{1,0:T(8,128)(2,1)}, bf16[128,2176]{1,0:T(8,128)(2,1)}, u32[]{:S(2)}, u32[]{:S(2)}) collective-permute-start(bf16[128,2176]{1,0:T(8,128)(2,1)} %shard_map.104.refs_0_), channel_id=1, source_target_pairs={{4,8},{8,4},{5,9},{9,5},{6,10},{10,6},{7,11},{11,7},{20,24},{24,20... | collective-permute-start | bytes 1671176 | tf_op jit(solution)/shard_map/ppermute | solution.py:341
  5.1 18.0 %collective-permute-start.1 = (bf16[128,2176]{1,0:T(8,128)(2,1)}, bf16[128,2176]{1,0:T(8,128)(2,1)}, u32[]{:S(2)}, u32[]{:S(2)}) collective-permute-start(bf16[128,2176]{1,0:T(8,128)(2,1)} %shard_map.104.refs_0_), channel_id=1, source_target_pairs={{0,4},{4,0},{8,12},{12,8},{1,5},{5,1},{9,13},{13,9},{2,6},{6,2},{1... | collective-permute-start | bytes 1671176 | tf_op jit(solution)/shard_map/ppermute | solution.py:341
  10.1 16.5 %collective-permute-start.6 = (bf16[128,2176]{1,0:T(8,128)(2,1)}, bf16[128,2176]{1,0:T(8,128)(2,1)}, u32[]{:S(2)}, u32[]{:S(2)}) collective-permute-start(bf16[128,2176]{1,0:T(8,128)(2,1)} %shard_map.104.refs_0_), channel_id=1, source_target_pairs={{0,2},{1,3},{2,0},{3,1},{4,6},{5,7},{6,4},{7,5},{8,10},{9,11},{10,... | collective-permute-start | bytes 1671176 | tf_op jit(solution)/shard_map/ppermute | solution.py:345
  23.0 15.9 %collective-permute-start.5 = (bf16[128,2176]{1,0:T(8,128)(2,1)}, bf16[128,2176]{1,0:T(8,128)(2,1)S(1)}, u32[]{:S(2)}, u32[]{:S(2)}) collective-permute-start(bf16[128,2176]{1,0:T(8,128)(2,1)} %collective-permute-done), channel_id=1, source_target_pairs={{4,0},{8,12},{5,1},{9,13},{6,2},{10,14},{7,3},{11,15},{20,16},{24,... | collective-permute-start | bytes 1671176 | tf_op jit(solution)/shard_map/ppermute | solution.py:341
  24.3 14.6 %collective-permute-start.4 = (bf16[128,2176]{1,0:T(8,128)(2,1)}, bf16[128,2176]{1,0:T(8,128)(2,1)S(1)}, u32[]{:S(2)}, u32[]{:S(2)}) collective-permute-start(bf16[128,2176]{1,0:T(8,128)(2,1)} %collective-permute-done.1.refs_2_), channel_id=1, source_target_pairs={{4,8},{8,4},{5,9},{9,5},{6,10},{10,6},{7,11},{11,7},{20,24},{24,20... | collective-permute-start | bytes 1671176 | tf_op jit(solution)/shard_map/ppermute | solution.py:341
  25.0 16.8 %collective-permute-start.9 = (bf16[128,2176]{1,0:T(8,128)(2,1)}, bf16[128,2176]{1,0:T(8,128)(2,1)S(1)}, u32[]{:S(2)}, u32[]{:S(2)}) collective-permute-start(bf16[128,2176]{1,0:T(8,128)(2,1)} %collective-permute-done.1.refs_2_), channel_id=1, source_target_pairs={{0,2},{1,3},{2,0},{3,1},{4,6},{5,7},{6,4},{7,5},{8,10},{9,11},{10,... | collective-permute-start | bytes 1671176 | tf_op jit(solution)/shard_map/ppermute | solution.py:345
  39.0 15.7 %collective-permute-start.8 = (bf16[128,2176]{1,0:T(8,128)(2,1)S(1)}, bf16[128,2176]{1,0:T(8,128)(2,1)S(1)}, u32[]{:S(2)}, u32[]{:S(2)}) collective-permute-start(bf16[128,2176]{1,0:T(8,128)(2,1)S(1)} %collective-permute-done.4), channel_id=1, source_target_pairs={{4,0},{8,12},{5,1},{9,13},{6,2},{10,14},{7,3},{11,15},{20,16},{24,... | collective-permute-start | bytes 1671176 | tf_op jit(solution)/shard_map/ppermute | solution.py:341
  40.3 18.0 %collective-permute-start.7 = (bf16[128,2176]{1,0:T(8,128)(2,1)S(1)}, bf16[128,2176]{1,0:T(8,128)(2,1)S(1)}, u32[]{:S(2)}, u32[]{:S(2)}) collective-permute-start(bf16[128,2176]{1,0:T(8,128)(2,1)S(1)} %broadcast_select_fusion.1.refs_1_), channel_id=1, source_target_pairs={{0,2},{1,3},{2,0},{3,1},{4,6},{5,7},{6,4},{7,5},{8,10},{9,11},{10,... | collective-permute-start | bytes 1671176 | tf_op jit(solution)/shard_map/ppermute | solution.py:345
  54.8 12.0 %collective-permute-start.12 = (bf16[128,2176]{1,0:T(8,128)(2,1)S(1)}, bf16[128,2176]{1,0:T(8,128)(2,1)S(1)}, u32[]{:S(2)}, u32[]{:S(2)}) collective-permute-start(bf16[128,2176]{1,0:T(8,128)(2,1)S(1)} %broadcast_select_fusion.refs_1_), channel_id=1, source_target_pairs={{0,2},{1,3},{2,0},{3,1},{4,6},{5,7},{6,4},{7,5},{8,10},{9,11},{10,... | collective-permute-start | bytes 1671176 | tf_op jit(solution)/shard_map/ppermute | solution.py:345
  56.3 10.1 %collective-permute-start.13 = (bf16[128,512]{1,0:T(8,128)(2,1)S(1)}, bf16[128,512]{1,0:T(8,128)(2,1)S(1)}, u32[]{:S(2)}, u32[]{:S(2)}) collective-permute-start(bf16[128,512]{1,0:T(8,128)(2,1)S(1)} %bitcast_dynamic-update-slice_fusion.own_ref), channel_id=1, source_target_pairs={{0,4},{1,9},{2,6},{3,11},{4,0},{5,13},{6,2},{7,15},{8,12},{9,1},{1... | collective-permute-start | bytes 393224 | tf_op jit(solution)/shard_map/ppermute | solution.py:413
  56.3 10.1 %collective-permute-start.14 = (bf16[64,512]{1,0:T(8,128)(2,1)S(1)}, bf16[64,512]{1,0:T(8,128)(2,1)S(1)}, u32[]{:S(2)}, u32[]{:S(2)}) collective-permute-start(bf16[64,512]{1,0:T(8,128)(2,1)S(1)} %slice_select_fusion), channel_id=1, source_target_pairs={{0,12},{4,8},{8,4},{12,0},{1,13},{5,9},{9,5},{13,1},{2,14},{6,10},... | collective-permute-start | bytes 196616 | tf_op jit(solution)/shard_map/ppermute | solution.py:341
  62.4 15.2 %collective-permute-start.10 = (bf16[128,2048]{1,0:T(8,128)(2,1)S(1)}, bf16[128,2048]{1,0:T(8,128)(2,1)S(1)}, u32[]{:S(2)}, u32[]{:S(2)}) collective-permute-start(bf16[128,2048]{1,0:T(8,128)(2,1)S(1)} %get-tuple-element.83), channel_id=1, source_target_pairs={{0,4},{12,8},{1,5},{13,9},{2,6},{14,10},{3,7},{15,11},{16,20},{28,... | collective-permute-start | bytes 1572872 | tf_op jit(solution)/shard_map/ppermute | solution.py:341
  65.5 12.3 %collective-permute-start.11 = (bf16[128,2048]{1,0:T(8,128)(2,1)S(1)}, bf16[128,2048]{1,0:T(8,128)(2,1)S(1)}, u32[]{:S(2)}, u32[]{:S(2)}) collective-permute-start(bf16[128,2048]{1,0:T(8,128)(2,1)S(1)} %get-tuple-element.79), channel_id=1, source_target_pairs={{4,8},{8,4},{5,9},{9,5},{6,10},{10,6},{7,11},{11,7},{20,24},{24,20... | collective-permute-start | bytes 1572872 | tf_op jit(solution)/shard_map/ppermute | solution.py:341
  69.3 15.7 %collective-permute-start.15 = (bf16[128,2048]{1,0:T(8,128)(2,1)S(1)}, bf16[128,2048]{1,0:T(8,128)(2,1)S(1)}, u32[]{:S(2)}, u32[]{:S(2)}) collective-permute-start(bf16[128,2048]{1,0:T(8,128)(2,1)S(1)} %shard_map.109), channel_id=1, source_target_pairs={{0,8},{12,4},{1,9},{13,5},{2,10},{14,6},{3,11},{15,7},{16,24},{28,... | collective-permute-start | bytes 1572872 | tf_op jit(solution)/shard_map/ppermute | solution.py:341
  73.5 11.5 %collective-permute-start.16 = (bf16[128,2048]{1,0:T(8,128)(2,1)S(1)}, bf16[128,2048]{1,0:T(8,128)(2,1)S(1)}, u32[]{:S(2)}, u32[]{:S(2)}) collective-permute-start(bf16[128,2048]{1,0:T(8,128)(2,1)S(1)} %shard_map.109), channel_id=1, source_target_pairs={{4,6},{5,7},{6,4},{7,5},{8,10},{9,11},{10,8},{11,9},{20,22},{21,23... | collective-permute-start | bytes 1572872 | tf_op jit(solution)/shard_map/ppermute | solution.py:350
  74.2 15.2 %collective-permute-start.19 = (bf16[128,2048]{1,0:T(8,128)(2,1)S(1)}, bf16[128,2048]{1,0:T(8,128)(2,1)S(1)}, u32[]{:S(2)}, u32[]{:S(2)}) collective-permute-start(bf16[128,2048]{1,0:T(8,128)(2,1)S(1)} %get-tuple-element.79), channel_id=1, source_target_pairs={{0,2},{1,3},{2,0},{3,1},{12,14},{13,15},{14,12},{15,13},{16,18},{1... | collective-permute-start | bytes 1572872 | tf_op jit(solution)/shard_map/ppermute | solution.py:350
  77.7 29.8 %collective-permute-start.17 = (bf16[192,512]{1,0:T(8,128)(2,1)S(1)}, bf16[192,512]{1,0:T(8,128)(2,1)S(1)}, u32[]{:S(2)}, u32[]{:S(2)}) collective-permute-start(bf16[192,512]{1,0:T(8,128)(2,1)S(1)} %constant_dynamic-update-slice_fusion.mine_ref), channel_id=1, source_target_pairs={{0,1},{1,0},{2,3},{3,2},{4,5},{5,4},{6,7},{7,6},{8,9},{9,8},{10,11... | collective-permute-start | bytes 589832 | tf_op jit(solution)/shard_map/ppermute | solution.py:428
  85.1 16.7 %collective-permute-start.22 = (bf16[128,2048]{1,0:T(8,128)(2,1)S(1)}, bf16[128,2048]{1,0:T(8,128)(2,1)S(1)}, u32[]{:S(2)}, u32[]{:S(2)}) collective-permute-start(bf16[128,2048]{1,0:T(8,128)(2,1)S(1)} %add_convert_fusion.2), channel_id=1, source_target_pairs={{0,2},{1,3},{2,0},{3,1},{4,6},{5,7},{6,4},{7,5},{8,10},{9,11},{10,... | collective-permute-start | bytes 1572872 | tf_op jit(solution)/shard_map/ppermute | solution.py:345
  89.5 10.7 %collective-permute-start.20 = (bf16[128,2048]{1,0:T(8,128)(2,1)S(1)}, bf16[128,2048]{1,0:T(8,128)(2,1)S(1)}, u32[]{:S(2)}, u32[]{:S(2)}) collective-permute-start(bf16[128,2048]{1,0:T(8,128)(2,1)S(1)} %add_convert_fusion.4), channel_id=1, source_target_pairs={{0,4},{12,8},{1,5},{13,9},{2,6},{14,10},{3,7},{15,11},{16,20},{28,... | collective-permute-start | bytes 1572872 | tf_op jit(solution)/shard_map/ppermute | solution.py:341
  91.8 10.0 %collective-permute-start.23 = (bf16[128,2048]{1,0:T(8,128)(2,1)S(1)}, bf16[128,2048]{1,0:T(8,128)(2,1)S(1)}, u32[]{:S(2)}, u32[]{:S(2)}) collective-permute-start(bf16[128,2048]{1,0:T(8,128)(2,1)S(1)} %add_convert_fusion.1), channel_id=1, source_target_pairs={{4,8},{8,4},{5,9},{9,5},{6,10},{10,6},{7,11},{11,7},{20,24},{24,20... | collective-permute-start | bytes 1572872 | tf_op jit(solution)/shard_map/ppermute | solution.py:341
  92.7 17.5 %collective-permute-start.18 = (bf16[128,2048]{1,0:T(8,128)(2,1)S(1)}, bf16[128,2048]{1,0:T(8,128)(2,1)S(1)}, u32[]{:S(2)}, u32[]{:S(2)}) collective-permute-start(bf16[128,2048]{1,0:T(8,128)(2,1)S(1)} %add_convert_fusion.5), channel_id=1, source_target_pairs={{0,2},{1,3},{2,0},{3,1},{4,6},{5,7},{6,4},{7,5},{8,10},{9,11},{10,... | collective-permute-start | bytes 1572872 | tf_op jit(solution)/shard_map/ppermute | solution.py:345
  102.9 12.7 %collective-permute-start.24 = (bf16[128,2048]{1,0:T(8,128)(2,1)}, bf16[128,2048]{1,0:T(8,128)(2,1)S(1)}, u32[]{:S(2)}, u32[]{:S(2)}) collective-permute-start(bf16[128,2048]{1,0:T(8,128)(2,1)} %add_convert_fusion), channel_id=1, source_target_pairs={{0,4},{4,0},{8,12},{12,8},{1,5},{5,1},{9,13},{13,9},{2,6},{6,2},{1... | collective-permute-start | bytes 1572872 | tf_op jit(solution)/shard_map/ppermute | solution.py:341
  (4 other events, 20.4 us)
